TPU v7x, 512 devices: a whole 4x8x8 slice. The times are simulated.
512 devices in a mesh: band: 8 (over z), tile: 64 (over x, y, core).
Axes of the slice: x: 4, y: 8, z: 8, core: 2. Of those that a mesh axis runs over, the one named last changes fastest.
Arguments:
- frames: bfloat16 [512, 256, 512], P('tile', 'band'), may hold values from -6 to 6
- disk_mask: int32 [256, 512], P('band'), may hold values from 0 to 1, as said below
- offsets: int32 [8, 8, 2], replicated, may hold values from -4 to 4, as said below
- filter_gain: float32 [128], replicated, may hold values from 0.5 to 2
- filter_mix: float32 [128], replicated, may hold values from -1 to 1
Outputs:
- cross_spectra: float32 [64, 128, 8, 2, 128], P('band', 'tile')
Inputs may be any that keep to these rules, and one draw needn't show every extreme that they name: `disk_mask`: 1 on the pixels of one disk whose centre lies within the image rows, 0 elsewhere; the first column is off the disk. In every distance's list the row offsets and the column offsets each reach -4 and 4.
All inputs are finite; a program needn't handle non-finite values.
Results may differ from a plain program's by a relative error of at most 0.006.
Values may be sent and summed in bfloat16 or wider, within the bound.
No kernel may reach another device: no remote copies, remote signals or barrier semaphores. Data moves between devices by JAX's collectives and lax.ppermute only.
A program may use at most 128 MiB of HBM per device.

v0:
```python
import math

import jax
import jax.numpy as jnp
from jax import lax
from jax.sharding import PartitionSpec as P

FRAMES = 512
FREQ = 128
OFFS = 8
FLO = 48
RAD = 4
MARGIN = 5


def padded(x, sides, width):
    for axis, dim in sides:
        devices, length = (lax.axis_size(axis), x.shape[dim])
        up = [(i, (i + 1) % devices) for i in range(devices - 1)]
        down = [(j, i) for i, j in up]
        last = lax.slice_in_dim(x, length - width, length, axis=dim)
        first = lax.slice_in_dim(x, 0, width, axis=dim)
        before = lax.ppermute(last, axis, up)
        after = lax.ppermute(first, axis, down)
        x = jnp.concatenate([before, x, after], axis=dim)
    return x


def dft_table():
    times = jnp.arange(FRAMES, dtype=jnp.int32)
    freqs = FLO + jnp.arange(FREQ, dtype=jnp.int32)
    phases = times[:, None] * freqs[None, :] % FRAMES
    angles = phases.astype(jnp.float32) * (2.0 * math.pi / FRAMES)
    factor = 1.0 / math.sqrt(FRAMES)
    return jnp.concatenate([jnp.cos(angles) * factor, -jnp.sin(angles) * factor], axis=1).astype(
        jnp.bfloat16
    )


def transform(series, table):
    result = lax.dot_general(
        series, table, (((0,), (0,)), ((), ())), preferred_element_type=jnp.float32
    )
    return result.astype(jnp.bfloat16)


def cross_all(centre, annulus, weight, denom):
    real_c = centre[None, ..., :FREQ]
    imag_c = centre[None, ..., FREQ:]
    real_a = annulus[..., :FREQ]
    imag_a = annulus[..., FREQ:]
    masks = weight[None, :, :, None]
    first_part = (real_c * real_a + imag_c * imag_a) * masks
    second_part = (real_c * imag_a - imag_c * real_a) * masks
    dists = annulus.shape[0]
    row_count = weight.shape[0]
    col_count = weight.shape[1]
    first_sum = first_part.reshape(dists, row_count // 4, 4, col_count // 4, 4, FREQ).sum(
        axis=(2, 4)
    )
    second_sum = second_part.reshape(dists, row_count // 4, 4, col_count // 4, 4, FREQ).sum(
        axis=(2, 4)
    )
    summed = jnp.stack([first_sum, second_sum], axis=3)
    result = summed / denom[None, :, :, None, None]
    return jnp.transpose(result, (1, 2, 0, 3, 4))


def on_device(frames, disk_mask, offsets, filter_gain, filter_mix):
    row_count = frames.shape[1]
    all_cols = frames.shape[2]
    tiles = lax.axis_size("tile")
    col_count = all_cols // tiles
    margin = MARGIN
    reach = RAD
    table = dft_table()
    masked = frames * disk_mask[None].astype(jnp.bfloat16)
    received = lax.all_to_all(masked, "tile", split_axis=2, concat_axis=0, tiled=True)
    series = received.reshape(FRAMES, row_count * col_count)
    spectrum = transform(series, table).reshape(row_count, col_count, 2 * FREQ)
    extended = padded(spectrum, (("band", 0), ("tile", 1)), margin)
    gain_both = jnp.concatenate([filter_gain, filter_gain])
    mix_both = jnp.concatenate([filter_mix, filter_mix])
    ext_float = extended.astype(jnp.float32)
    inner = ext_float[1:-1, 1:-1]
    beside_all = 0.25 * (
        ext_float[2:, 1:-1] + ext_float[:-2, 1:-1] + ext_float[1:-1, 2:] + ext_float[1:-1, :-2]
    )
    filtered = gain_both * inner + mix_both * (beside_all - inner)
    centre = filtered[reach : reach + row_count, reach : reach + col_count]
    tile_start = lax.axis_index("tile") * col_count
    weight = lax.dynamic_slice_in_dim(disk_mask, tile_start, col_count, 1).astype(jnp.float32)
    counts = weight.reshape(row_count // 4, 4, col_count // 4, 4).sum(axis=(1, 3))
    denom = jnp.maximum(counts, 1.0)

    def window_at(start_row, start_col):
        return lax.dynamic_slice(
            filtered, (start_row, start_col, jnp.int32(0)), (row_count, col_count, 2 * FREQ)
        )

    annulus = jnp.zeros((offsets.shape[0], row_count, col_count, 2 * FREQ), jnp.float32)
    for member in range(OFFS):
        start_rows = reach + offsets[:, member, 0]
        start_cols = reach + offsets[:, member, 1]
        annulus = annulus + jax.vmap(window_at)(start_rows, start_cols)
    return cross_all(centre, annulus, weight, denom)


def solution(mesh):
    return jax.shard_map(
        on_device,
        mesh=mesh,
        in_specs=(P("tile", "band", None), P("band", None), P(), P(), P()),
        out_specs=P("band", "tile", None, None, None),
        check_vma=False,
    )
```

profile of v0, /device:TPU:251, one launch (start us, length us, event | category | flops | bytes accessed | tf_op | source)
XLA Modules:
  0.0 244.1 jit_solution(12349484819845566556)
XLA Ops:
  4.6 10.3 %all-to-all-start = ((bf16[64,2,1024]{2,1,0:T(2,128)(2,1)}), bf16[64,2,1024]{2,1,0:T(2,128)(2,1)S(1)}, u32[]{:S(2)}, u32[]{:S(2)}) async-start(bf16[64,2,1024]{2,1,0:T(2,128)(2,1)} %reshape.717), calls=%async_computation | async-start | bytes 524288 | tf_op jit(solution)/shard_map/all_to_all | solution.py:78
  14.8 2.9 %add_reduce_fusion.27 = (s32[8]{0:T(128)S(1)}, s32[8]{0:T(128)S(1)}, s32[8]{0:T(128)S(1)}, s32[8]{0:T(128)S(1)}, s32[8]{0:T(128)S(1)}, /*index=5*/s32[8]{0:T(128...) fusion(s32[8,8,2]{1,2,0:T(2,128)S(1)} %copy-done), kind=kLoop, calls=%fused_computation.84 | loop fusion | flops 152 | bytes 1120 | tf_op jit(solution)/shard_map/add | solution.py:103
  17.8 2.1 add_reduce_fusion.25
  22.2 2.4 all-to-all-done
  25.0 3.2 %copy.12 = bf16[64,8,32,8]{3,2,1,0:T(8,128)(2,1)} copy(bf16[64,8,32,8]{2,1,3,0:T(8,128)(2,1)S(1)} %bitcast.166) | data formatting | bytes 524288 | tf_op jit(solution)/shard_map/all_to_all | solution.py:78
  28.3 6.9 %reshape.496 = bf16[512,256]{1,0:T(8,128)(2,1)S(1)} reshape(bf16[64,8,32,8]{3,2,1,0:T(8,128)(2,1)} %copy.12) | data formatting | bytes 524288 | tf_op jit(solution)/shard_map/reshape | solution.py:79
  35.5 5.2 %collective-permute-start = (bf16[5,8,256]{2,1,0:T(8,128)(2,1)S(1)}, bf16[5,8,256]{2,1,0:T(8,128)(2,1)S(1)}, u32[]{:S(2)}, u32[]{:S(2)}) collective-permute-start(bf16[5,8,256]{2,1,0:T(8,128)(2,1)S(1)} %get-tuple-element.187), channel_id=1, source_target_pairs={{0,64},{64,128},{128,192},{192,256},{256,320},{320,384},{384,448},... | collective-permute-start | bytes 61448 | tf_op jit(solution)/shard_map/ppermute | solution.py:23
  42.8 3.7 %collective-permute-done.1 = bf16[5,8,256]{2,1,0:T(8,128)(2,1)S(1)} collective-permute-done((bf16[5,8,256]{2,1,0:T(8,128)(2,1)S(1)}, bf16[5,8,256]{2,1,0:T(8,128)(2,1)S(1)}, u32[]{:S(2)}, u32[]{:S(2)}) %collective-permute-start.1) | collective-permute-done | bytes 20512 | tf_op jit(solution)/shard_map/ppermute | solution.py:24
  46.5 6.6 %collective-permute-start.2 = (bf16[42,5,256]{2,1,0:T(8,128)(2,1)S(1)}, bf16[42,5,256]{2,1,0:T(8,128)(2,1)S(1)}, u32[]{:S(2)}, u32[]{:S(2)}) collective-permute-start(bf16[42,5,256]{2,1,0:T(8,128)(2,1)S(1)} %get-tuple-element.185), channel_id=1, source_target_pairs={{0,1},{1,2},{2,3},{3,4},{4,5},{5,6},{6,7},{7,8},{8,9},{9,10},{10,1... | collective-permute-start | bytes 322568 | tf_op jit(solution)/shard_map/ppermute | solution.py:23
  53.2 2.1 collective-permute-start.3
  55.5 6.5 %collective-permute-done.3 = bf16[42,5,256]{2,1,0:T(8,128)(2,1)S(1)} collective-permute-done((bf16[42,5,256]{2,1,0:T(8,128)(2,1)S(1)}, bf16[42,5,256]{2,1,0:T(8,128)(2,1)S(1)}, u32[]{:S(2)}, u32[]{:S(2)}) %collective-permute-start.3) | collective-permute-done | bytes 107552 | tf_op jit(solution)/shard_map/ppermute | solution.py:24
  62.7 14.7 %while.9 = (s32[]{:T(128)}, f32[40,16,256]{2,1,0:T(8,128)S(1)}, s32[8,3]{0,1:T(4,128)S(1)}, f32[8,32,8,256]{3,2,1,0:T(8,128)S(1)}, s32[]{:T(128)}) while((s32[]{:T(128)}, f32[40,16,256]{2,1,0:T(8,128)S(1)}, s32[8,3]{0,1:T(4,128)S(1)}, f32[8,32,8,256]{3,2,1,0:T(8,128)S(1)}, s32[]{:T(128)}) %tuple.188), condition=%wide.while_cond.1, body=%wide.while_body.1.sunk | while | flops 2 | bytes 524405 | solution.py:97
  79.0 20.2 %while.11 = (s32[]{:T(128)}, f32[40,16,256]{2,1,0:T(8,128)S(1)}, s32[8,3]{0,1:T(4,128)S(1)}, f32[8,32,8,256]{3,2,1,0:T(8,128)}, s32[]{:T(128)}) while((s32[]{:T(128)}, f32[40,16,256]{2,1,0:T(8,128)S(1)}, s32[8,3]{0,1:T(4,128)S(1)}, f32[8,32,8,256]{3,2,1,0:T(8,128)}, s32[]{:T(128)}) %tuple.191), condition=%wide.while_cond.3, body=%wide.while_body.3.sunk | while | flops 2 | bytes 525929 | solution.py:97
  100.6 20.5 %while.12 = (s32[]{:T(128)}, f32[40,16,256]{2,1,0:T(8,128)S(1)}, s32[8,3]{0,1:T(4,128)S(1)}, f32[8,32,8,256]{3,2,1,0:T(8,128)}, s32[]{:T(128)}) while((s32[]{:T(128)}, f32[40,16,256]{2,1,0:T(8,128)S(1)}, s32[8,3]{0,1:T(4,128)S(1)}, f32[8,32,8,256]{3,2,1,0:T(8,128)}, s32[]{:T(128)}) %tuple.192), condition=%wide.while_cond.4, body=%wide.while_body.4.sunk | while | flops 2 | bytes 525929 | solution.py:97
  101.2 2.0 bitcast_dynamic-update-slice_fusion.20
  108.9 2.0 bitcast_dynamic-update-slice_fusion.20
  111.5 2.0 bitcast_dynamic-update-slice_fusion.20
  114.0 1.9 bitcast_dynamic-update-slice_fusion.20
  122.6 20.9 %while.13 = (s32[]{:T(128)}, f32[40,16,256]{2,1,0:T(8,128)S(1)}, s32[8,3]{0,1:T(4,128)S(1)}, f32[8,32,8,256]{3,2,1,0:T(8,128)}, s32[]{:T(128)}) while((s32[]{:T(128)}, f32[40,16,256]{2,1,0:T(8,128)S(1)}, s32[8,3]{0,1:T(4,128)S(1)}, f32[8,32,8,256]{3,2,1,0:T(8,128)}, s32[]{:T(128)}) %tuple.193), condition=%wide.while_cond.5, body=%wide.while_body.5.sunk | while | flops 2 | bytes 525929 | solution.py:97
  123.2 2.0 bitcast_dynamic-update-slice_fusion.21
  125.8 2.0 bitcast_dynamic-update-slice_fusion.21
  128.4 2.0 bitcast_dynamic-update-slice_fusion.21
  131.0 2.0 bitcast_dynamic-update-slice_fusion.21
  133.7 2.0 bitcast_dynamic-update-slice_fusion.21
  136.3 2.0 bitcast_dynamic-update-slice_fusion.21
  138.9 2.0 bitcast_dynamic-update-slice_fusion.21
  141.5 2.0 bitcast_dynamic-update-slice_fusion.21
  145.1 21.4 %while.14 = (s32[]{:T(128)}, f32[40,16,256]{2,1,0:T(8,128)S(1)}, s32[8,3]{0,1:T(4,128)S(1)}, f32[8,32,8,256]{3,2,1,0:T(8,128)}, s32[]{:T(128)}) while((s32[]{:T(128)}, f32[40,16,256]{2,1,0:T(8,128)S(1)}, s32[8,3]{0,1:T(4,128)S(1)}, f32[8,32,8,256]{3,2,1,0:T(8,128)}, s32[]{:T(128)}) %tuple.194), condition=%wide.while_cond.6, body=%wide.while_body.6.sunk | while | flops 2 | bytes 525929 | solution.py:97
  145.7 2.0 bitcast_dynamic-update-slice_fusion.22
  148.4 2.0 bitcast_dynamic-update-slice_fusion.22
  151.1 2.0 bitcast_dynamic-update-slice_fusion.22
  153.8 2.0 bitcast_dynamic-update-slice_fusion.22
  156.5 2.0 bitcast_dynamic-update-slice_fusion.22
  159.1 2.0 bitcast_dynamic-update-slice_fusion.22
  161.8 2.0 bitcast_dynamic-update-slice_fusion.22
  164.5 2.0 bitcast_dynamic-update-slice_fusion.22
  168.1 21.0 %while.8 = (s32[]{:T(128)}, f32[40,16,256]{2,1,0:T(8,128)S(1)}, s32[8,3]{0,1:T(4,128)S(1)}, f32[8,32,8,256]{3,2,1,0:T(8,128)}, s32[]{:T(128)}) while((s32[]{:T(128)}, f32[40,16,256]{2,1,0:T(8,128)S(1)}, s32[8,3]{0,1:T(4,128)S(1)}, f32[8,32,8,256]{3,2,1,0:T(8,128)}, s32[]{:T(128)}) %tuple.195), condition=%wide.while_cond, body=%wide.while_body.sunk | while | flops 2 | bytes 525929 | solution.py:97
  168.7 2.0 bitcast_dynamic-update-slice_fusion.16
  171.3 2.0 bitcast_dynamic-update-slice_fusion.16
  174.0 2.0 bitcast_dynamic-update-slice_fusion.16
  176.6 2.0 bitcast_dynamic-update-slice_fusion.16
  179.2 2.0 bitcast_dynamic-update-slice_fusion.16
  181.8 2.0 bitcast_dynamic-update-slice_fusion.16
  184.5 2.0 bitcast_dynamic-update-slice_fusion.16
  187.1 2.0 bitcast_dynamic-update-slice_fusion.16
  190.5 21.6 %while.10 = (s32[]{:T(128)}, f32[40,16,256]{2,1,0:T(8,128)S(1)}, s32[8,3]{0,1:T(4,128)S(1)}, f32[8,32,8,256]{3,2,1,0:T(8,128)}, s32[]{:T(128)}) while((s32[]{:T(128)}, f32[40,16,256]{2,1,0:T(8,128)S(1)}, s32[8,3]{0,1:T(4,128)S(1)}, f32[8,32,8,256]{3,2,1,0:T(8,128)}, s32[]{:T(128)}) %tuple.196), condition=%wide.while_cond.2, body=%wide.while_body.2.sunk | while | flops 2 | bytes 525929 | solution.py:97
  191.2 2.1 bitcast_dynamic-update-slice_fusion.18
  193.9 2.1 bitcast_dynamic-update-slice_fusion.18
  196.6 2.1 bitcast_dynamic-update-slice_fusion.18
  199.3 2.0 bitcast_dynamic-update-slice_fusion.18
  202.0 2.0 bitcast_dynamic-update-slice_fusion.18
  204.7 2.0 bitcast_dynamic-update-slice_fusion.18
  207.4 2.0 bitcast_dynamic-update-slice_fusion.18
  210.1 2.1 bitcast_dynamic-update-slice_fusion.18
  213.7 21.9 %while.15 = (s32[]{:T(128)}, f32[40,16,256]{2,1,0:T(8,128)S(1)}, s32[8,3]{0,1:T(4,128)S(1)}, f32[8,32,8,256]{3,2,1,0:T(8,128)}, s32[]{:T(128)}) while((s32[]{:T(128)}, f32[40,16,256]{2,1,0:T(8,128)S(1)}, s32[8,3]{0,1:T(4,128)S(1)}, f32[8,32,8,256]{3,2,1,0:T(8,128)}, s32[]{:T(128)}) %tuple.197), condition=%wide.while_cond.7, body=%wide.while_body.7.sunk | while | flops 2 | bytes 525929 | solution.py:97
  214.4 2.1 bitcast_dynamic-update-slice_fusion.23
  217.1 2.1 bitcast_dynamic-update-slice_fusion.23
  219.9 2.1 bitcast_dynamic-update-slice_fusion.23
  222.6 2.1 bitcast_dynamic-update-slice_fusion.23
  225.4 2.1 bitcast_dynamic-update-slice_fusion.23
  228.1 2.1 bitcast_dynamic-update-slice_fusion.23
  230.8 2.1 bitcast_dynamic-update-slice_fusion.23
  233.5 2.1 bitcast_dynamic-update-slice_fusion.23
  235.6 6.3 %add_add_fusion = f32[8,32,8,256]{3,2,1,0:T(8,128)S(1)} fusion(f32[8,32,8,256]{3,2,1,0:T(8,128)} %get-tuple-element.68, f32[8,32,8,256]{3,2,1,0:T(8,128)} %get-tuple-element.60, f32[8,32,8,256]{3,2,1,0:T(8,128)} %get-tuple-element.52, f32[8,32,8,256]{3,2,1,0:T(8,128)} %get-tuple-element.44, f32[8,32,8,256]{3,2,1,0:T(8,128)} %get-tuple-element.36, ...), kind=kLoop, calls=%fused_computation.16 | loop fusion | flops 3670016 | bytes 18874368 | tf_op jit(solution)/shard_map/add | solution.py:105
  (203 shorter events, 96.6 us)
Async XLA Ops:
  2.6 12.3 %copy-start = (s32[8,8,2]{1,2,0:T(2,128)S(1)}, s32[8,8,2]{1,2,0:T(2,128)}, u32[]{:S(2)}) copy-start(s32[8,8,2]{1,2,0:T(2,128)} %param.7) | copy-start | bytes 1540
  4.6 20.0 %all-to-all-start = ((bf16[64,2,1024]{2,1,0:T(2,128)(2,1)}), bf16[64,2,1024]{2,1,0:T(2,128)(2,1)S(1)}, u32[]{:S(2)}, u32[]{:S(2)}) async-start(bf16[64,2,1024]{2,1,0:T(2,128)(2,1)} %reshape.717), calls=%async_computation | async-start | bytes 524288 | tf_op jit(solution)/shard_map/all_to_all | solution.py:78
  28.3 27.0 %copy-start.1 = (f32[128]{0:T(128)S(1)}, f32[128]{0:T(128)}, u32[]{:S(2)}) copy-start(f32[128]{0:T(128)} %param.8) | copy-start | bytes 1540
  28.3 27.0 %copy-start.2 = (f32[128]{0:T(128)S(1)}, f32[128]{0:T(128)}, u32[]{:S(2)}) copy-start(f32[128]{0:T(128)} %param.9) | copy-start | bytes 1540
  35.5 7.2 %collective-permute-start = (bf16[5,8,256]{2,1,0:T(8,128)(2,1)S(1)}, bf16[5,8,256]{2,1,0:T(8,128)(2,1)S(1)}, u32[]{:S(2)}, u32[]{:S(2)}) collective-permute-start(bf16[5,8,256]{2,1,0:T(8,128)(2,1)S(1)} %get-tuple-element.187), channel_id=1, source_target_pairs={{0,64},{64,128},{128,192},{192,256},{256,320},{320,384},{384,448},... | collective-permute-start | bytes 61448 | tf_op jit(solution)/shard_map/ppermute | solution.py:23
  40.7 5.7 %collective-permute-start.1 = (bf16[5,8,256]{2,1,0:T(8,128)(2,1)S(1)}, bf16[5,8,256]{2,1,0:T(8,128)(2,1)S(1)}, u32[]{:S(2)}, u32[]{:S(2)}) collective-permute-start(bf16[5,8,256]{2,1,0:T(8,128)(2,1)S(1)} %get-tuple-element.188), channel_id=1, source_target_pairs={{64,0},{128,64},{192,128},{256,192},{320,256},{384,320},{448,384},... | collective-permute-start | bytes 61448 | tf_op jit(solution)/shard_map/ppermute | solution.py:24
  46.5 9.0 %collective-permute-start.2 = (bf16[42,5,256]{2,1,0:T(8,128)(2,1)S(1)}, bf16[42,5,256]{2,1,0:T(8,128)(2,1)S(1)}, u32[]{:S(2)}, u32[]{:S(2)}) collective-permute-start(bf16[42,5,256]{2,1,0:T(8,128)(2,1)S(1)} %get-tuple-element.185), channel_id=1, source_target_pairs={{0,1},{1,2},{2,3},{3,4},{4,5},{5,6},{6,7},{7,8},{8,9},{9,10},{10,1... | collective-permute-start | bytes 322568 | tf_op jit(solution)/shard_map/ppermute | solution.py:23
  53.2 8.8 %collective-permute-start.3 = (bf16[42,5,256]{2,1,0:T(8,128)(2,1)S(1)}, bf16[42,5,256]{2,1,0:T(8,128)(2,1)S(1)}, u32[]{:S(2)}, u32[]{:S(2)}) collective-permute-start(bf16[42,5,256]{2,1,0:T(8,128)(2,1)S(1)} %get-tuple-element.186), channel_id=1, source_target_pairs={{1,0},{2,1},{3,2},{4,3},{5,4},{6,5},{7,6},{8,7},{9,8},{10,9},{11,1... | collective-permute-start | bytes 322568 | tf_op jit(solution)/shard_map/ppermute | solution.py:24
where the time goes:
time: 246 us; the launch traced here: 244 us
  local copies, waits for them, and re-layouts  188 us (76%)
  starting transfers between devices  26.1 us (11%)
  other arithmetic  16.3 us (7%)
  waiting for transfers between devices  12.8 us (5%)
    gather x192, local copies, waits for them, and re-layouts  162 us
    unnamed x17, local copies, waits for them, and re-layouts  14.7 us
    ppermute x2, starting transfers between devices, padded(): before = lax.ppermute(last, axis, up)  11.8 us
    all_to_all x1, starting transfers between devices, on_device(): lax.all_to_all(masked, 'tile', split_axis=2, concat_axis=0, tiled=True)  10.3 us
    ppermute x2, waiting for transfers between devices, padded(): after = lax.ppermute(first, axis, down)  10.2 us
    reshape x1, local copies, waits for them, and re-layouts, on_device(): series = received.reshape(FRAMES, row_count * col_count)  6.91 us
    add x1, other arithmetic, on_device(): annulus = annulus + jax.vmap(window_at)(start_rows, start_cols)  6.35 us
  transfers between devices with their start and end apart: 5, of which 4 were waited for; matrix products, arithmetic and copies ran while one was open for 3% of the time, Pallas kernels for 0%

commit v1 on v0

v1 whole, which is shorter than its diff:
```python
import math

import jax
import jax.numpy as jnp
import numpy as np
from jax import lax
from jax.experimental import pallas as pl
from jax.experimental.pallas import tpu as pltpu
from jax.sharding import PartitionSpec as P

FRAMES = 512
FREQ = 128
DIST = 8
OFFS = 8
FLO = 48
TILES = 64
LOCAL = 8
ROWS = 32
COLS = 8
WIDE = 20
LEAD = 6
BLOCKS = 72
TALL = 48
REACH = 40
SIDE = 16

F32 = jnp.float32
BF16 = jnp.bfloat16


def dft_table():
    times = np.arange(FRAMES, dtype=np.int32)
    freqs = FLO + np.arange(FREQ, dtype=np.int32)
    phases = times[:, None] * freqs[None, :] % FRAMES
    angles = phases.astype(np.float32) * np.float32(2.0 * math.pi / FRAMES)
    factor = np.float32(1.0 / math.sqrt(FRAMES))
    both = np.concatenate([np.cos(angles) * factor, -np.sin(angles) * factor], axis=1)
    return jnp.asarray(both.astype(np.float32)).astype(BF16)


def pack_kernel(frames_ref, mask_ref, out_ref, low_ref, high_ref):
    mask = mask_ref[...].astype(F32)
    masked = (frames_ref[...].astype(F32) * mask[None]).astype(BF16)
    flat = masked.reshape(LOCAL * ROWS, mask.shape[1])
    cols = lax.broadcasted_iota(jnp.int32, (BLOCKS, mask.shape[1]), 1)
    block = lax.broadcasted_iota(jnp.int32, (BLOCKS, mask.shape[1]), 0)
    place = cols - 8 * block + LEAD
    rolled = []
    for c in range(COLS):
        pick = jnp.where(place == c, 1.0, 0.0).astype(BF16)
        turned = lax.dot_general(
            pick, flat, (((1,), (1,)), ((), ())), preferred_element_type=F32
        )
        halves = [turned[:, :128], turned[:, 128:]]
        rolled.append(
            [[h if s == 0 else pltpu.roll(h, 32 * s, 1) for s in range(4)] for h in halves]
        )
    lane_group = lax.broadcasted_iota(jnp.int32, (BLOCKS, 128), 1) // 32
    for f in range(LOCAL):
        for part in range(2):
            value = None
            for g in range(4):
                piece = rolled[part * 4 + g][f // 4][(g - f % 4) % 4]
                value = piece if value is None else jnp.where(lane_group == g, piece, value)
            (low_ref, high_ref)[part][pl.ds(f, BLOCKS, stride=LOCAL), :] = value
    count = TILES * LOCAL
    for at, source, start in (
        (0, low_ref, 0),
        (128, high_ref, 0),
        (256, low_ref, 8),
        (384, high_ref, 8),
        (512, low_ref, 16),
    ):
        out_ref[:, at : at + 128] = source[start : start + count, :].astype(BF16)


def pack(frames, mask):
    return pl.pallas_call(
        pack_kernel,
        out_shape=jax.ShapeDtypeStruct((TILES * LOCAL, WIDE * ROWS), BF16),
        scratch_shapes=[pltpu.VMEM((BLOCKS * LOCAL, 128), F32)] * 2,
        compiler_params=pltpu.CompilerParams(vmem_limit_bytes=32 * 1024 * 1024),
    )(frames, mask)


def spectra_kernel(series_ref, table_ref, own_ref, last_ref, first_ref):
    spectrum = lax.dot_general(
        series_ref[...],
        table_ref[...],
        (((0,), (0,)), ((), ())),
        preferred_element_type=F32,
    )
    own_ref[...] = spectrum.astype(BF16)
    by_column = spectrum.reshape(WIDE, ROWS, 2 * FREQ)
    last_ref[...] = by_column[:, ROWS - 8 :].reshape(WIDE * 8, 2 * FREQ).astype(BF16)
    first_ref[...] = by_column[:, :8].reshape(WIDE * 8, 2 * FREQ).astype(BF16)


def spectra(series, table):
    edge = jax.ShapeDtypeStruct((WIDE * 8, 2 * FREQ), BF16)
    return pl.pallas_call(
        spectra_kernel,
        out_shape=(jax.ShapeDtypeStruct((WIDE * ROWS, 2 * FREQ), BF16), edge, edge),
        compiler_params=pltpu.CompilerParams(vmem_limit_bytes=32 * 1024 * 1024),
    )(series, table)


def cross_kernel(
    offsets_ref,
    own_ref,
    before_ref,
    after_ref,
    mask_ref,
    gain_ref,
    mix_ref,
    out_ref,
    tall_re,
    tall_im,
    filt_re,
    filt_im,
    centre_re,
    centre_im,
    sums,
    seen,
):
    own = own_ref[...].astype(F32).reshape(WIDE, ROWS, 2 * FREQ)
    before = before_ref[...].astype(F32).reshape(WIDE, 8, 2 * FREQ)
    after = after_ref[...].astype(F32).reshape(WIDE, 8, 2 * FREQ)
    for q in range(WIDE):
        for tall, low in ((tall_re, 0), (tall_im, FREQ)):
            lanes = slice(low, low + FREQ)
            tall[q * TALL : q * TALL + 8, :] = before[q, :, lanes]
            tall[q * TALL + 8 : q * TALL + 40, :] = own[q, :, lanes]
            tall[q * TALL + 40 : q * TALL + 48, :] = after[q, :, lanes]

    gain = gain_ref[...]
    mix = mix_ref[...]
    for tall, filt in ((tall_re, filt_re), (tall_im, filt_im)):
        for q in range(SIDE):
            at = (q + 2) * TALL + 4
            inner = tall[at : at + REACH, :]
            beside = 0.25 * (
                tall[at + 1 : at + 1 + REACH, :]
                + tall[at - 1 : at - 1 + REACH, :]
                + tall[at + TALL : at + TALL + REACH, :]
                + tall[at - TALL : at - TALL + REACH, :]
            )
            filt[q * REACH : (q + 1) * REACH, :] = gain * inner + mix * (beside - inner)

    tile = lax.axis_index("tile")
    wide = pl.multiple_of((tile // 16) * 128, 128)
    near = mask_ref[:, pl.ds(wide, 128)].astype(F32)
    near = pltpu.roll(near, (128 - 8 * (tile % 16)) % 128, 1)
    for part in range(2):
        total = jnp.zeros((ROWS, 128), F32)
        for c in range(part * 4, part * 4 + 4):
            weight = jnp.broadcast_to(near[:, c : c + 1], (ROWS, 128))
            total = total + weight
            at = (c + 4) * REACH + 4
            centre_re[c * ROWS : (c + 1) * ROWS, :] = filt_re[at : at + ROWS, :] * weight
            centre_im[c * ROWS : (c + 1) * ROWS, :] = filt_im[at : at + ROWS, :] * weight
        seen[part * ROWS : (part + 1) * ROWS, :] = total

    def distance(d, carry):
        starts = [offsets_ref[d * OFFS + k] for k in range(OFFS)]
        for part in range(2):
            first = jnp.zeros((ROWS, 128), F32)
            second = jnp.zeros((ROWS, 128), F32)
            for c in range(part * 4, part * 4 + 4):
                real_a = filt_re[pl.ds(starts[0] + c * REACH, ROWS), :]
                imag_a = filt_im[pl.ds(starts[0] + c * REACH, ROWS), :]
                for k in range(1, OFFS):
                    real_a = real_a + filt_re[pl.ds(starts[k] + c * REACH, ROWS), :]
                    imag_a = imag_a + filt_im[pl.ds(starts[k] + c * REACH, ROWS), :]
                real_c = centre_re[c * ROWS : (c + 1) * ROWS, :]
                imag_c = centre_im[c * ROWS : (c + 1) * ROWS, :]
                first = first + (real_c * real_a + imag_c * imag_a)
                second = second + (real_c * imag_a - imag_c * real_a)
            for group in range(4):
                at = pl.multiple_of(((group * 2 + part) * 16 + 2 * d) * 8, 8)
                sums[pl.ds(at, 8), :] = first[group * 8 : group * 8 + 8]
                sums[pl.ds(at + 8, 8), :] = second[group * 8 : group * 8 + 8]
        return carry

    lax.fori_loop(0, DIST, distance, 0)

    for group in range(4):
        for half in range(2):
            for part in range(2):
                at = part * ROWS + group * 8 + half * 4
                count = seen[at : at + 1, :]
                for k in range(1, 4):
                    count = count + seen[at + k : at + k + 1, :]
                denom = jnp.broadcast_to(jnp.maximum(count, 1.0), (8, 128))
                for piece in range(2):
                    base = ((group * 2 + part) * 16 + piece * 8) * 8 + half * 4
                    total = sums[pl.ds(base, 8, stride=8), :]
                    for k in range(1, 4):
                        total = total + sums[pl.ds(base + k, 8, stride=8), :]
                    row = ((group * 2 + half) * 2 + part) * 16 + piece * 8
                    out_ref[row : row + 8, :] = total / denom


def cross_spectra(starts, own, before, after, mask, gain, mix):
    vmem = pl.BlockSpec(memory_space=pltpu.VMEM)
    return pl.pallas_call(
        cross_kernel,
        out_shape=jax.ShapeDtypeStruct((8 * 2 * DIST * 2, FREQ), F32),
        in_specs=[pl.BlockSpec(memory_space=pltpu.SMEM)] + [vmem] * 6,
        scratch_shapes=[
            pltpu.VMEM((WIDE * TALL, FREQ), F32),
            pltpu.VMEM((WIDE * TALL, FREQ), F32),
            pltpu.VMEM((SIDE * REACH, FREQ), F32),
            pltpu.VMEM((SIDE * REACH, FREQ), F32),
            pltpu.VMEM((COLS * ROWS, FREQ), F32),
            pltpu.VMEM((COLS * ROWS, FREQ), F32),
            pltpu.VMEM((8 * 16 * 8, FREQ), F32),
            pltpu.VMEM((2 * ROWS, FREQ), F32),
        ],
        compiler_params=pltpu.CompilerParams(vmem_limit_bytes=32 * 1024 * 1024),
    )(starts, own, before, after, mask, gain, mix)


def on_device(frames, disk_mask, offsets, filter_gain, filter_mix):
    packed = pack(frames, disk_mask).reshape(TILES, LOCAL, WIDE * ROWS)
    received = lax.all_to_all(packed, "tile", split_axis=0, concat_axis=0, tiled=True)
    series = received.reshape(FRAMES, WIDE * ROWS)
    own, last, first = spectra(series, dft_table())
    bands = lax.axis_size("band")
    up = [(i, i + 1) for i in range(bands - 1)]
    down = [(j, i) for i, j in up]
    before = lax.ppermute(last, "band", up)
    after = lax.ppermute(first, "band", down)
    starts = ((offsets[..., 1] + 4) * REACH + offsets[..., 0] + 4).reshape(DIST * OFFS)
    out = cross_spectra(
        starts,
        own,
        before,
        after,
        disk_mask,
        filter_gain.reshape(1, FREQ),
        filter_mix.reshape(1, FREQ),
    )
    return out.reshape(8, 2, DIST, 2, FREQ)


def solution(mesh):
    return jax.shard_map(
        on_device,
        mesh=mesh,
        in_specs=(P("tile", "band", None), P("band", None), P(), P(), P()),
        out_specs=P("band", "tile", None, None, None),
        check_vma=False,
    )
```

time: 246 us -> 50.9 us (0.21)
  the two profiles are of different devices: /device:TPU:251 before, /device:TPU:198 now
where the time goes in v1:
time: 50.9 us; the launch traced here: 50.7 us
  blocking collectives  30 us (59%)
  starting transfers between devices  7.41 us (15%)
  waiting for transfers between devices  5.99 us (12%)
  Pallas kernels  4.64 us (9%)
  local copies, waits for them, and re-layouts  2.55 us (5%)
    all_to_all x1, blocking collectives, on_device(): lax.all_to_all(packed, 'tile', split_axis=0, concat_axis=0, tiled=True)  30 us
    ppermute x1, starting transfers between devices, on_device(): before = lax.ppermute(last, 'band', up)  5.49 us
    ppermute x1, waiting for transfers between devices, on_device(): after = lax.ppermute(first, 'band', down)  5.33 us
    pallas_call x1, Pallas kernels, cross_spectra(): pl.pallas_call(cross_kernel, out_shape=jax.ShapeDtypeStruct((8 * 2 * DIST...  3.27 us
    unnamed x14, local copies, waits for them, and re-layouts  2.47 us
    ppermute x1, starting transfers between devices, on_device(): after = lax.ppermute(first, 'band', down)  1.92 us
  transfers between devices with their start and end apart: 2, of which 2 were waited for; matrix products, arithmetic and copies ran while one was open for 0% of the time, Pallas kernels for 0%

profile of v1, /device:TPU:198, one launch (start us, length us, event | category | flops | bytes accessed | tf_op | source)
XLA Modules:
  0.0 50.7 jit_solution(15854034478533441386)
XLA Ops:
  0.0 0.0 copy-start.1
  0.0 0.9 %copy-done.1 = bf16[8,32,512]{2,1,0:T(8,128)(2,1)S(1)} copy-done((bf16[8,32,512]{2,1,0:T(8,128)(2,1)S(1)}, bf16[8,32,512]{2,1,0:T(8,128)(2,1)}, u32[]{:S(2)}) %copy-start.1) | copy-done | bytes 262168
  1.0 0.0 copy-start.2
  1.0 0.8 %copy-done.2 = s32[32,512]{1,0:T(8,128)S(1)} copy-done((s32[32,512]{1,0:T(8,128)S(1)}, s32[32,512]{1,0:T(8,128)}, u32[]{:S(2)}) %copy-start.2) | copy-done | bytes 65560
  1.8 1.0 %shard_map.64 = bf16[512,640]{1,0:T(8,128)(2,1)S(1)} custom-call(bf16[8,32,512]{2,1,0:T(8,128)(2,1)S(1)} %copy-done.1, s32[32,512]{1,0:T(8,128)S(1)} %copy-done.2), custom_call_target="tpu_custom_call" | custom-call | tf_op jit(solution)/shard_map/pallas_call | solution.py:78
  2.8 0.0 copy-start
  2.8 30.0 %all_to_all.5 = bf16[64,8,640]{2,1,0:T(8,128)(2,1)S(1)} all-to-all(bf16[64,8,640]{2,1,0:T(8,128)(2,1)S(1)} %bitcast.6), channel_id=1, replica_groups=mesh['band'=8,'tile'=64] {'tile'}, dimensions={0} | all-to-all | bytes 1310720 | tf_op jit(solution)/shard_map/all_to_all | solution.py:226
  32.8 0.0 copy-done
  32.8 0.0 copy-start.6
  32.8 0.0 copy-start.3
  32.8 0.4 shard_map.65
  33.2 5.5 %collective-permute-start = (bf16[160,256]{1,0:T(8,128)(2,1)S(1)}, bf16[160,256]{1,0:T(8,128)(2,1)S(1)}, u32[]{:S(2)}, u32[]{:S(2)}) collective-permute-start(bf16[160,256]{1,0:T(8,128)(2,1)S(1)} %get-tuple-element.9), channel_id=1, source_target_pairs={{0,64},{64,128},{128,192},{192,256},{256,320},{320,384},{384,448},... | collective-permute-start | bytes 245768 | tf_op jit(solution)/shard_map/ppermute | solution.py:232
  38.7 1.9 %collective-permute-start.1 = (bf16[160,256]{1,0:T(8,128)(2,1)S(1)}, bf16[160,256]{1,0:T(8,128)(2,1)S(1)}, u32[]{:S(2)}, u32[]{:S(2)}) collective-permute-start(bf16[160,256]{1,0:T(8,128)(2,1)S(1)} %get-tuple-element.10), channel_id=1, source_target_pairs={{64,0},{128,64},{192,128},{256,192},{320,256},{384,320},{448,384},... | collective-permute-start | bytes 245768 | tf_op jit(solution)/shard_map/ppermute | solution.py:233
  40.6 0.0 copy-done.6
  40.7 0.1 add.20.offsets_ref
  40.7 0.7 %collective-permute-done.before_ref = bf16[160,256]{1,0:T(8,128)(2,1)S(1)} collective-permute-done((bf16[160,256]{1,0:T(8,128)(2,1)S(1)}, bf16[160,256]{1,0:T(8,128)(2,1)S(1)}, u32[]{:S(2)}, u32[]{:S(2)}) %collective-permute-start) | collective-permute-done | bytes 81952 | tf_op jit(solution)/shard_map/ppermute | solution.py:232
  41.4 5.3 %collective-permute-done.1.after_ref = bf16[160,256]{1,0:T(8,128)(2,1)S(1)} collective-permute-done((bf16[160,256]{1,0:T(8,128)(2,1)S(1)}, bf16[160,256]{1,0:T(8,128)(2,1)S(1)}, u32[]{:S(2)}, u32[]{:S(2)}) %collective-permute-start.1) | collective-permute-done | bytes 81952 | tf_op jit(solution)/shard_map/ppermute | solution.py:233
  46.7 0.0 copy-start.4
  46.7 0.0 copy-start.5
  46.7 0.0 copy-done.3
  46.7 0.6 %copy-done.4 = f32[128]{0:T(128)S(1)} copy-done((f32[128]{0:T(128)S(1)}, f32[128]{0:T(128)}, u32[]{:S(2)}) %copy-start.4) | copy-done | bytes 536
  47.4 0.0 copy-done.5
  47.4 3.3 %shard_map.66 = f32[256,128]{1,0:T(8,128)} custom-call(s32[64]{0:T(128)S(1)} %add.20.offsets_ref, bf16[640,256]{1,0:T(8,128)(2,1)S(1)} %get-tuple-element.8.own_ref, bf16[160,256]{1,0:T(8,128)(2,1)S(1)} %collective-permute-done.before_ref, bf16[160,256]{1,0:T(8,128)(2,1)S(1)} %collective-permute-done.1.after_ref, s32[32,512]{1,0:T(8,128)S(1)} %copy-done.3, ...), custom_call_target="tpu_custom_call" | custom-call | tf_op jit(solution)/shard_map/pallas_call | solution.py:206
  (1 shorter events, 0.0 us)
Async XLA Ops:
  0.0 0.9 %copy-start.1 = (bf16[8,32,512]{2,1,0:T(8,128)(2,1)S(1)}, bf16[8,32,512]{2,1,0:T(8,128)(2,1)}, u32[]{:S(2)}) copy-start(bf16[8,32,512]{2,1,0:T(8,128)(2,1)} %frames_ref.1) | copy-start | bytes 786436
  1.0 0.8 %copy-start.2 = (s32[32,512]{1,0:T(8,128)S(1)}, s32[32,512]{1,0:T(8,128)}, u32[]{:S(2)}) copy-start(s32[32,512]{1,0:T(8,128)} %mask_ref.3) | copy-start | bytes 196612
  2.8 30.0 %copy-start = (bf16[512,256]{1,0:T(8,128)(2,1)S(1)}, bf16[512,256]{1,0:T(8,128)(2,1)}, u32[]{:S(2)}) copy-start(bf16[512,256]{1,0:T(8,128)(2,1)} %constant.8.table_ref) | copy-start | bytes 786436
  32.8 7.8 %copy-start.6 = (s32[8,8,2]{1,2,0:T(2,128)S(1)}, s32[8,8,2]{1,2,0:T(2,128)}, u32[]{:S(2)}) copy-start(s32[8,8,2]{1,2,0:T(2,128)} %param.8) | copy-start | bytes 1540
  32.8 13.9 %copy-start.3 = (s32[32,512]{1,0:T(8,128)S(1)}, s32[32,512]{1,0:T(8,128)}, u32[]{:S(2)}) copy-start(s32[32,512]{1,0:T(8,128)} %mask_ref.3) | copy-start | bytes 196612
  33.2 8.2 %collective-permute-start = (bf16[160,256]{1,0:T(8,128)(2,1)S(1)}, bf16[160,256]{1,0:T(8,128)(2,1)S(1)}, u32[]{:S(2)}, u32[]{:S(2)}) collective-permute-start(bf16[160,256]{1,0:T(8,128)(2,1)S(1)} %get-tuple-element.9), channel_id=1, source_target_pairs={{0,64},{64,128},{128,192},{192,256},{256,320},{320,384},{384,448},... | collective-permute-start | bytes 245768 | tf_op jit(solution)/shard_map/ppermute | solution.py:232
  38.7 8.0 %collective-permute-start.1 = (bf16[160,256]{1,0:T(8,128)(2,1)S(1)}, bf16[160,256]{1,0:T(8,128)(2,1)S(1)}, u32[]{:S(2)}, u32[]{:S(2)}) collective-permute-start(bf16[160,256]{1,0:T(8,128)(2,1)S(1)} %get-tuple-element.10), channel_id=1, source_target_pairs={{64,0},{128,64},{192,128},{256,192},{320,256},{384,320},{448,384},... | collective-permute-start | bytes 245768 | tf_op jit(solution)/shard_map/ppermute | solution.py:233
  46.7 0.7 %copy-start.4 = (f32[128]{0:T(128)S(1)}, f32[128]{0:T(128)}, u32[]{:S(2)}) copy-start(f32[128]{0:T(128)} %param.9) | copy-start | bytes 1540
  46.7 0.7 %copy-start.5 = (f32[128]{0:T(128)S(1)}, f32[128]{0:T(128)}, u32[]{:S(2)}) copy-start(f32[128]{0:T(128)} %param.10) | copy-start | bytes 1540

commit v2 on v1

v2 whole, which is shorter than its diff:
```python
import math

import jax
import jax.numpy as jnp
import numpy as np
from jax import lax
from jax.experimental import pallas as pl
from jax.experimental.pallas import tpu as pltpu
from jax.sharding import PartitionSpec as P

FRAMES = 512
FREQ = 128
DIST = 8
OFFS = 8
FLO = 48
TILES = 64
LOCAL = 8
ROWS = 32
COLS = 8
WIDE = 20
LEAD = 6
BLOCKS = 72
TALL = 48
REACH = 40
SIDE = 16

F32 = jnp.float32
BF16 = jnp.bfloat16


def dft_table():
    times = np.arange(FRAMES, dtype=np.int32)
    freqs = FLO + np.arange(FREQ, dtype=np.int32)
    phases = times[:, None] * freqs[None, :] % FRAMES
    angles = phases.astype(np.float32) * np.float32(2.0 * math.pi / FRAMES)
    factor = np.float32(1.0 / math.sqrt(FRAMES))
    both = np.concatenate([np.cos(angles) * factor, -np.sin(angles) * factor], axis=1)
    return jnp.asarray(both.astype(np.float32)).astype(BF16)


def pack_kernel(frames_ref, mask_ref, out_ref, frames_vmem, mask_vmem, pick_ref, low_ref, high_ref, sems):
    copies = [
        pltpu.make_async_copy(mask_ref, mask_vmem, sems.at[0]),
        pltpu.make_async_copy(frames_ref, frames_vmem, sems.at[1]),
    ]
    for copy in copies:
        copy.start()
    width = mask_vmem.shape[1]
    cols = lax.broadcasted_iota(jnp.int32, (BLOCKS, width), 1)
    block = lax.broadcasted_iota(jnp.int32, (BLOCKS, width), 0)
    place = cols - 8 * block + LEAD
    for c in range(COLS):
        pick_ref[c] = jnp.where(place == c, 1.0, 0.0)
    for copy in copies:
        copy.wait()
    mask = mask_vmem[...].astype(F32)
    masked = (frames_vmem[...].astype(F32) * mask[None]).astype(BF16)
    flat = masked.reshape(LOCAL * ROWS, width)
    rolled = []
    for c in range(COLS):
        turned = lax.dot_general(
            pick_ref[c].astype(BF16), flat, (((1,), (1,)), ((), ())), preferred_element_type=F32
        )
        halves = [turned[:, :128], turned[:, 128:]]
        rolled.append(
            [[h if s == 0 else pltpu.roll(h, 32 * s, 1) for s in range(4)] for h in halves]
        )
    lane_group = lax.broadcasted_iota(jnp.int32, (BLOCKS, 128), 1) // 32
    for f in range(LOCAL):
        for part in range(2):
            value = None
            for g in range(4):
                piece = rolled[part * 4 + g][f // 4][(g - f % 4) % 4]
                value = piece if value is None else jnp.where(lane_group == g, piece, value)
            (low_ref, high_ref)[part][pl.ds(f, BLOCKS, stride=LOCAL), :] = value
    count = TILES * LOCAL
    for at, source, start in (
        (0, low_ref, 0),
        (128, high_ref, 0),
        (256, low_ref, 8),
        (384, high_ref, 8),
        (512, low_ref, 16),
    ):
        out_ref[:, at : at + 128] = source[start : start + count, :].astype(BF16)


def pack(frames, mask):
    return pl.pallas_call(
        pack_kernel,
        out_shape=pltpu.VMEM((TILES * LOCAL, WIDE * ROWS), BF16),
        in_specs=[pl.BlockSpec(memory_space=pltpu.HBM)] * 2,
        scratch_shapes=[
            pltpu.VMEM(frames.shape, BF16),
            pltpu.VMEM(mask.shape, jnp.int32),
            pltpu.VMEM((COLS, BLOCKS, mask.shape[1]), F32),
            pltpu.VMEM((BLOCKS * LOCAL, 128), F32),
            pltpu.VMEM((BLOCKS * LOCAL, 128), F32),
            pltpu.SemaphoreType.DMA((2,)),
        ],
        compiler_params=pltpu.CompilerParams(vmem_limit_bytes=60000000),
    )(frames, mask)


def spectra_kernel(series_ref, table_ref, own_ref, last_ref, first_ref):
    spectrum = lax.dot_general(
        series_ref[...],
        table_ref[...],
        (((0,), (0,)), ((), ())),
        preferred_element_type=F32,
    )
    own_ref[...] = spectrum.astype(BF16)
    by_column = spectrum.reshape(WIDE, ROWS, 2 * FREQ)
    last_ref[...] = by_column[:, ROWS - 8 :].reshape(WIDE * 8, 2 * FREQ).astype(BF16)
    first_ref[...] = by_column[:, :8].reshape(WIDE * 8, 2 * FREQ).astype(BF16)


def spectra(series, table):
    edge = jax.ShapeDtypeStruct((WIDE * 8, 2 * FREQ), BF16)
    return pl.pallas_call(
        spectra_kernel,
        out_shape=(jax.ShapeDtypeStruct((WIDE * ROWS, 2 * FREQ), BF16), edge, edge),
        compiler_params=pltpu.CompilerParams(vmem_limit_bytes=32 * 1024 * 1024),
    )(series, table)


def filtered(tall, at, rows, gain, mix):
    rim = tall[1]
    tall = tall[0]
    inner = tall[at : at + rows, :]
    beside = 0.25 * (
        tall[at + 1 : at + 1 + rows, :]
        + tall[at - 1 : at - 1 + rows, :]
        + tall[at + rim : at + rim + rows, :]
        + tall[at - rim : at - rim + rows, :]
    )
    return gain * inner + mix * (beside - inner)


def block_rows(groups, offsets_ref, filt_re, filt_im, centre_re, centre_im, sums):
    at_group = {group: n for n, group in enumerate(groups)}

    def distance(d, carry):
        starts = [offsets_ref[d * OFFS + k] for k in range(OFFS)]
        for part in range(2):
            for group in groups:
                first = jnp.zeros((8, 128), F32)
                second = jnp.zeros((8, 128), F32)
                for c in range(part * 4, part * 4 + 4):
                    shift = c * REACH + group * 8
                    real_a = filt_re[pl.ds(starts[0] + shift, 8), :]
                    imag_a = filt_im[pl.ds(starts[0] + shift, 8), :]
                    for k in range(1, OFFS):
                        real_a = real_a + filt_re[pl.ds(starts[k] + shift, 8), :]
                        imag_a = imag_a + filt_im[pl.ds(starts[k] + shift, 8), :]
                    at = c * ROWS + group * 8
                    real_c = centre_re[at : at + 8, :]
                    imag_c = centre_im[at : at + 8, :]
                    first = first + (real_c * real_a + imag_c * imag_a)
                    second = second + (real_c * imag_a - imag_c * real_a)
                at = pl.multiple_of(((at_group[group] * 2 + part) * 16 + 2 * d) * 8, 8)
                sums[pl.ds(at, 8), :] = first
                sums[pl.ds(at + 8, 8), :] = second
        return carry

    lax.fori_loop(0, DIST, distance, 0)


def block_means(groups, sums, seen, out_ref, first_row):
    for n, group in enumerate(groups):
        for half in range(2):
            for part in range(2):
                at = part * ROWS + group * 8 + half * 4
                count = seen[at : at + 1, :]
                for k in range(1, 4):
                    count = count + seen[at + k : at + k + 1, :]
                denom = jnp.broadcast_to(jnp.maximum(count, 1.0), (8, 128))
                for piece in range(2):
                    base = ((n * 2 + part) * 16 + piece * 8) * 8 + half * 4
                    total = sums[pl.ds(base, 8, stride=8), :]
                    for k in range(1, 4):
                        total = total + sums[pl.ds(base + k, 8, stride=8), :]
                    row = ((group * 2 + half) * 2 + part) * 16 + piece * 8 - first_row
                    out_ref[row : row + 8, :] = total / denom


def middle_kernel(
    offsets_ref,
    own_ref,
    mask_ref,
    gain_ref,
    mix_ref,
    out_ref,
    filt_re,
    filt_im,
    seen,
    pair_ref,
    own_re,
    own_im,
    centre_re,
    centre_im,
    sums,
):
    own_re[...] = own_ref[:, :FREQ].astype(F32)
    own_im[...] = own_ref[:, FREQ:].astype(F32)
    gain = gain_ref[...]
    mix = mix_ref[...]
    pair_ref[0:1, :] = gain
    pair_ref[1:2, :] = mix
    for source, filt in ((own_re, filt_re), (own_im, filt_im)):
        for q in range(SIDE):
            at = (q + 2) * ROWS + 1
            value = filtered((source, ROWS), at, ROWS - 2, gain, mix)
            filt[q * REACH + 5 : q * REACH + 5 + ROWS - 2, :] = value

    tile = lax.axis_index("tile")
    wide = pl.multiple_of((tile // 16) * 128, 128)
    near = mask_ref[:, pl.ds(wide, 128)].astype(F32)
    near = pltpu.roll(near, (128 - 8 * (tile % 16)) % 128, 1)
    for part in range(2):
        total = jnp.zeros((ROWS, 128), F32)
        for c in range(part * 4, part * 4 + 4):
            weight = jnp.broadcast_to(near[:, c : c + 1], (ROWS, 128))
            total = total + weight
            at = (c + 4) * REACH + 12
            to = c * ROWS + 8
            centre_re[to : to + 16, :] = filt_re[at : at + 16, :] * weight[8:24]
            centre_im[to : to + 16, :] = filt_im[at : at + 16, :] * weight[8:24]
            pair_ref[8 + c * 8 : 16 + c * 8, :] = weight[0:8]
            pair_ref[72 + c * 8 : 80 + c * 8, :] = weight[24:32]
        seen[part * ROWS : (part + 1) * ROWS, :] = total

    groups = (1, 2)
    block_rows(groups, offsets_ref, filt_re, filt_im, centre_re, centre_im, sums)
    block_means(groups, sums, seen, out_ref, 64)


def outer_kernel(
    offsets_ref,
    before_ref,
    first_ref,
    last_ref,
    after_ref,
    mid_ref,
    own_filt_re,
    own_filt_im,
    seen,
    pair_ref,
    out_ref,
    top_re,
    top_im,
    low_re,
    low_im,
    filt_re,
    filt_im,
    centre_re,
    centre_im,
    sums,
):
    for upper, lower, real, imag in (
        (before_ref, first_ref, top_re, top_im),
        (last_ref, after_ref, low_re, low_im),
    ):
        for at, ref in ((0, upper), (8, lower)):
            value = ref[...].astype(F32).reshape(WIDE, 8, 2 * FREQ)
            for q in range(WIDE):
                real[q * 16 + at : q * 16 + at + 8, :] = value[q, :, :FREQ]
                imag[q * 16 + at : q * 16 + at + 8, :] = value[q, :, FREQ:]
    gain = pair_ref[0:1, :]
    mix = pair_ref[1:2, :]
    for top, low, inside, filt in (
        (top_re, low_re, own_filt_re, filt_re),
        (top_im, low_im, own_filt_im, filt_im),
    ):
        for q in range(SIDE):
            at = q * REACH
            filt[at : at + 8, :] = filtered((top, 16), (q + 2) * 16 + 4, 8, gain, mix)
            filt[at + 8 : at + 32, :] = inside[at + 8 : at + 32, :]
            filt[at + 32 : at + 40, :] = filtered((low, 16), (q + 2) * 16 + 4, 8, gain, mix)
    for c in range(COLS):
        at = (c + 4) * REACH + 4
        for weight_at, row in ((8, 0), (72, 24)):
            weight = pair_ref[weight_at + c * 8 : weight_at + c * 8 + 8, :]
            to = c * ROWS + row
            centre_re[to : to + 8, :] = filt_re[at + row : at + row + 8, :] * weight
            centre_im[to : to + 8, :] = filt_im[at + row : at + row + 8, :] * weight

    groups = (0, 3)
    block_rows(groups, offsets_ref, filt_re, filt_im, centre_re, centre_im, sums)
    out_ref[64:192, :] = mid_ref[...]
    block_means(groups, sums, seen, out_ref, 0)


def float_shape(rows):
    return jax.ShapeDtypeStruct((rows, FREQ), F32)


def middle(starts, own, mask, gain, mix):
    vmem = pl.BlockSpec(memory_space=pltpu.VMEM)
    rows = (128, SIDE * REACH, SIDE * REACH, 2 * ROWS, 136)
    return pl.pallas_call(
        middle_kernel,
        out_shape=tuple(float_shape(n) for n in rows),
        in_specs=[pl.BlockSpec(memory_space=pltpu.SMEM)] + [vmem] * 4,
        scratch_shapes=[
            pltpu.VMEM((WIDE * ROWS, FREQ), F32),
            pltpu.VMEM((WIDE * ROWS, FREQ), F32),
            pltpu.VMEM((COLS * ROWS, FREQ), F32),
            pltpu.VMEM((COLS * ROWS, FREQ), F32),
            pltpu.VMEM((4 * 16 * 8, FREQ), F32),
        ],
        compiler_params=pltpu.CompilerParams(vmem_limit_bytes=32 * 1024 * 1024),
        cost_estimate=pl.CostEstimate(flops=6_000_000, bytes_accessed=4_000_000, transcendentals=0),
    )(starts, own, mask, gain, mix)


def outer(starts, before, first, last, after, kept):
    vmem = pl.BlockSpec(memory_space=pltpu.VMEM)
    rows = [WIDE * 16] * 4 + [SIDE * REACH] * 2 + [COLS * ROWS] * 2 + [4 * 16 * 8]
    return pl.pallas_call(
        outer_kernel,
        out_shape=float_shape(8 * 2 * DIST * 2),
        in_specs=[pl.BlockSpec(memory_space=pltpu.SMEM)] + [vmem] * (4 + len(kept)),
        scratch_shapes=[pltpu.VMEM((n, FREQ), F32) for n in rows],
        compiler_params=pltpu.CompilerParams(vmem_limit_bytes=32 * 1024 * 1024),
    )(starts, before, first, last, after, *kept)


def on_device(frames, disk_mask, offsets, filter_gain, filter_mix):
    packed = pack(frames, disk_mask).reshape(TILES, LOCAL, WIDE * ROWS)
    received = lax.all_to_all(packed, "tile", split_axis=0, concat_axis=0, tiled=True)
    series = received.reshape(FRAMES, WIDE * ROWS)
    own, last, first = spectra(series, dft_table())
    bands = lax.axis_size("band")
    up = [(i, i + 1) for i in range(bands - 1)]
    down = [(j, i) for i, j in up]
    before = lax.ppermute(last, "band", up)
    after = lax.ppermute(first, "band", down)
    starts = ((offsets[..., 1] + 4) * REACH + offsets[..., 0] + 4).reshape(DIST * OFFS)
    gain = filter_gain.reshape(1, FREQ)
    mix = filter_mix.reshape(1, FREQ)
    kept = middle(starts, own, disk_mask, gain, mix)
    out = outer(starts, before, first, last, after, kept)
    return out.reshape(8, 2, DIST, 2, FREQ)


def solution(mesh):
    return jax.shard_map(
        on_device,
        mesh=mesh,
        in_specs=(P("tile", "band", None), P("band", None), P(), P(), P()),
        out_specs=P("band", "tile", None, None, None),
        check_vma=False,
    )
```

time: 50.9 us -> 48.3 us (0.949)
  waiting for transfers between devices: 5.99 us -> 3.64 us
  local copies, waits for them, and re-layouts: 2.55 us -> 0.75 us
  Pallas kernels: 4.64 us -> 6.21 us
    unnamed x14 -> x10, local copies, waits for them, and re-layouts: 2.47 us -> 0.67 us
    ppermute x1, waiting for transfers between devices: 5.33 us -> 3.64 us  [on_device(): after = lax.ppermute(first, 'band', down)]
    pallas_call x2 -> x3, Pallas kernels: 4.26 us -> 5.82 us  [the longest x1 2.17 us: outer(): pl.pallas_call(outer_kernel, out_shape=float_shape(8 * 2 * DIST * 2), in_...]
    ppermute x1, waiting for transfers between devices: 0.66 us -> 0.01 us  [on_device(): before = lax.ppermute(last, 'band', up)]
  transfers between devices with their start and end apart: 2 -> 2, of which waited for: 2 -> 1; matrix products, arithmetic and copies ran while one was open for 0% -> 0% of each run, Pallas kernels for 0% -> 3%
where the time goes in v2:
time: 48.3 us; the launch traced here: 48.1 us
  blocking collectives  30 us (62%)
  starting transfers between devices  7.41 us (15%)
  Pallas kernels  6.21 us (13%)
  waiting for transfers between devices  3.64 us (8%)
  local copies, waits for them, and re-layouts  0.75 us (2%)
    all_to_all x1, blocking collectives, on_device(): lax.all_to_all(packed, 'tile', split_axis=0, concat_axis=0, tiled=True)  30 us
    ppermute x1, starting transfers between devices, on_device(): before = lax.ppermute(last, 'band', up)  5.49 us
    ppermute x1, waiting for transfers between devices, on_device(): after = lax.ppermute(first, 'band', down)  3.64 us
    pallas_call x1, Pallas kernels, outer(): pl.pallas_call(outer_kernel, out_shape=float_shape(8 * 2 * DIST * 2), in_...  2.17 us
    pallas_call x1, Pallas kernels, pack(): pl.pallas_call(pack_kernel, out_shape=pltpu.VMEM((TILES * LOCAL, WIDE * R...  1.99 us
    ppermute x1, starting transfers between devices, on_device(): after = lax.ppermute(first, 'band', down)  1.92 us
    pallas_call x1, Pallas kernels, middle(): pl.pallas_call(middle_kernel, out_shape=tuple((float_shape(n) for n in ro...  1.66 us
  transfers between devices with their start and end apart: 2, of which 1 were waited for; matrix products, arithmetic and copies ran while one was open for 0% of the time, Pallas kernels for 3%

profile of v2, /device:TPU:198, one launch (start us, length us, event | category | flops | bytes accessed | tf_op | source)
XLA Modules:
  0.0 48.1 jit_solution(8465693232066770935)
XLA Ops:
  0.0 2.0 %shard_map.64 = bf16[512,640]{1,0:T(8,128)(2,1)S(1)} custom-call(bf16[8,32,512]{2,1,0:T(8,128)(2,1)} %frames_ref.1, s32[32,512]{1,0:T(8,128)} %mask_ref.3), custom_call_target="tpu_custom_call" | custom-call | tf_op jit(solution)/shard_map/pallas_call | solution.py:88
  2.0 0.0 copy-start
  2.0 30.0 %all_to_all.5 = bf16[64,8,640]{2,1,0:T(8,128)(2,1)S(1)} all-to-all(bf16[64,8,640]{2,1,0:T(8,128)(2,1)S(1)} %bitcast.6), channel_id=1, replica_groups=mesh['band'=8,'tile'=64] {'tile'}, dimensions={0} | all-to-all | bytes 1310720 | tf_op jit(solution)/shard_map/all_to_all | solution.py:330
  32.0 0.0 copy-done
  32.0 0.0 copy-start.4
  32.0 0.0 copy-start.1
  32.0 0.4 shard_map.65
  32.4 5.5 %collective-permute-start = (bf16[160,256]{1,0:T(8,128)(2,1)S(1)}, bf16[160,256]{1,0:T(8,128)(2,1)S(1)}, u32[]{:S(2)}, u32[]{:S(2)}) collective-permute-start(bf16[160,256]{1,0:T(8,128)(2,1)S(1)} %get-tuple-element.13.last_ref), channel_id=1, source_target_pairs={{0,64},{64,128},{128,192},{192,256},{256,320},{320,384},{384,448},... | collective-permute-start | bytes 245768 | tf_op jit(solution)/shard_map/ppermute | solution.py:336
  37.9 1.9 %collective-permute-start.1 = (bf16[160,256]{1,0:T(8,128)(2,1)S(1)}, bf16[160,256]{1,0:T(8,128)(2,1)S(1)}, u32[]{:S(2)}, u32[]{:S(2)}) collective-permute-start(bf16[160,256]{1,0:T(8,128)(2,1)S(1)} %get-tuple-element.14.first_ref), channel_id=1, source_target_pairs={{64,0},{128,64},{192,128},{256,192},{320,256},{384,320},{448,384},... | collective-permute-start | bytes 245768 | tf_op jit(solution)/shard_map/ppermute | solution.py:337
  39.8 0.0 copy-done.4
  39.9 0.1 add.20.offsets_ref
  40.0 0.0 copy-start.2
  40.0 0.0 copy-start.3
  40.0 0.0 copy-done.1
  40.0 0.6 %copy-done.2 = f32[128]{0:T(128)S(1)} copy-done((f32[128]{0:T(128)S(1)}, f32[128]{0:T(128)}, u32[]{:S(2)}) %copy-start.2) | copy-done | bytes 536
  40.6 0.0 copy-done.3
  40.6 1.7 %shard_map.66 = (f32[128,128]{1,0:T(8,128)S(1)}, f32[640,128]{1,0:T(8,128)S(1)}, f32[640,128]{1,0:T(8,128)S(1)}, f32[64,128]{1,0:T(8,128)S(1)}, f32[136,128]{1,0:T(8,128)S(1)}) custom-call(s32[64]{0:T(128)S(1)} %add.20.offsets_ref, bf16[640,256]{1,0:T(8,128)(2,1)S(1)} %get-tuple-element.15.own_ref, s32[32,512]{1,0:T(8,128)S(1)} %copy-done.1, ...), custom_call_target="tpu_custom_call" | custom-call | flops 6000000 | bytes 4000000 | tf_op jit(solution)/shard_map/pallas_call | solution.py:300
  42.3 0.0 collective-permute-done.before_ref
  42.3 3.6 %collective-permute-done.1.after_ref = bf16[160,256]{1,0:T(8,128)(2,1)S(1)} collective-permute-done((bf16[160,256]{1,0:T(8,128)(2,1)S(1)}, bf16[160,256]{1,0:T(8,128)(2,1)S(1)}, u32[]{:S(2)}, u32[]{:S(2)}) %collective-permute-start.1) | collective-permute-done | bytes 81952 | tf_op jit(solution)/shard_map/ppermute | solution.py:337
  45.9 2.2 %shard_map.67 = f32[256,128]{1,0:T(8,128)} custom-call(s32[64]{0:T(128)S(1)} %add.20.offsets_ref, bf16[160,256]{1,0:T(8,128)(2,1)S(1)} %collective-permute-done.before_ref, bf16[160,256]{1,0:T(8,128)(2,1)S(1)} %get-tuple-element.14.first_ref, bf16[160,256]{1,0:T(8,128)(2,1)S(1)} %get-tuple-element.13.last_ref, ...), custom_call_target="tpu_custom_call" | custom-call | tf_op jit(solution)/shard_map/pallas_call | solution.py:319
  (1 shorter events, 0.0 us)
Async XLA Ops:
  2.0 30.0 %copy-start = (bf16[512,256]{1,0:T(8,128)(2,1)S(1)}, bf16[512,256]{1,0:T(8,128)(2,1)}, u32[]{:S(2)}) copy-start(bf16[512,256]{1,0:T(8,128)(2,1)} %constant.8.table_ref) | copy-start | bytes 786436
  32.0 7.8 %copy-start.4 = (s32[8,8,2]{1,2,0:T(2,128)S(1)}, s32[8,8,2]{1,2,0:T(2,128)}, u32[]{:S(2)}) copy-start(s32[8,8,2]{1,2,0:T(2,128)} %param.8) | copy-start | bytes 1540
  32.0 7.9 %copy-start.1 = (s32[32,512]{1,0:T(8,128)S(1)}, s32[32,512]{1,0:T(8,128)}, u32[]{:S(2)}) copy-start(s32[32,512]{1,0:T(8,128)} %mask_ref.3) | copy-start | bytes 196612
  32.4 9.9 %collective-permute-start = (bf16[160,256]{1,0:T(8,128)(2,1)S(1)}, bf16[160,256]{1,0:T(8,128)(2,1)S(1)}, u32[]{:S(2)}, u32[]{:S(2)}) collective-permute-start(bf16[160,256]{1,0:T(8,128)(2,1)S(1)} %get-tuple-element.13.last_ref), channel_id=1, source_target_pairs={{0,64},{64,128},{128,192},{192,256},{256,320},{320,384},{384,448},... | collective-permute-start | bytes 245768 | tf_op jit(solution)/shard_map/ppermute | solution.py:336
  37.9 8.0 %collective-permute-start.1 = (bf16[160,256]{1,0:T(8,128)(2,1)S(1)}, bf16[160,256]{1,0:T(8,128)(2,1)S(1)}, u32[]{:S(2)}, u32[]{:S(2)}) collective-permute-start(bf16[160,256]{1,0:T(8,128)(2,1)S(1)} %get-tuple-element.14.first_ref), channel_id=1, source_target_pairs={{64,0},{128,64},{192,128},{256,192},{320,256},{384,320},{448,384},... | collective-permute-start | bytes 245768 | tf_op jit(solution)/shard_map/ppermute | solution.py:337
  40.0 0.7 %copy-start.2 = (f32[128]{0:T(128)S(1)}, f32[128]{0:T(128)}, u32[]{:S(2)}) copy-start(f32[128]{0:T(128)} %param.9) | copy-start | bytes 1540
  40.0 0.7 %copy-start.3 = (f32[128]{0:T(128)S(1)}, f32[128]{0:T(128)}, u32[]{:S(2)}) copy-start(f32[128]{0:T(128)} %param.10) | copy-start | bytes 1540

commit v3 on v2

v3 whole, which is shorter than its diff:
```python
import math

import jax
import jax.numpy as jnp
import numpy as np
from jax import lax
from jax.experimental import pallas as pl
from jax.experimental.pallas import tpu as pltpu
from jax.sharding import PartitionSpec as P

FRAMES = 512
FREQ = 128
DIST = 8
OFFS = 8
FLO = 48
TILES = 64
LOCAL = 8
ROWS = 32
COLS = 8
WIDE = 20
LEAD = 6
BLOCKS = 72
TALL = 48
REACH = 40
SIDE = 16

F32 = jnp.float32
BF16 = jnp.bfloat16


def dft_table():
    times = np.arange(FRAMES, dtype=np.int32)
    freqs = FLO + np.arange(FREQ, dtype=np.int32)
    phases = times[:, None] * freqs[None, :] % FRAMES
    angles = phases.astype(np.float32) * np.float32(2.0 * math.pi / FRAMES)
    factor = np.float32(1.0 / math.sqrt(FRAMES))
    both = np.concatenate([np.cos(angles) * factor, -np.sin(angles) * factor], axis=1)
    return jnp.asarray(both.astype(np.float32)).astype(BF16)


def pack_kernel(frames_ref, mask_ref, out_ref, frames_vmem, mask_vmem, pick_ref, low_ref, high_ref, sems):
    near = LOCAL // 2
    copies = [
        pltpu.make_async_copy(mask_ref, mask_vmem, sems.at[0]),
        pltpu.make_async_copy(frames_ref.at[:near], frames_vmem.at[:near], sems.at[1]),
        pltpu.make_async_copy(frames_ref.at[near:], frames_vmem.at[near:], sems.at[2]),
    ]
    for copy in copies:
        copy.start()
    width = mask_vmem.shape[1]
    cols = lax.broadcasted_iota(jnp.int32, (BLOCKS, width), 1)
    block = lax.broadcasted_iota(jnp.int32, (BLOCKS, width), 0)
    place = cols - 8 * block + LEAD
    for c in range(COLS):
        pick_ref[c] = jnp.where(place == c, 1.0, 0.0)
    copies[0].wait()
    mask = mask_vmem[...].astype(F32)
    lane_group = lax.broadcasted_iota(jnp.int32, (BLOCKS, 128), 1) // 32
    for half in range(2):
        copies[1 + half].wait()
        chosen = frames_vmem[half * near : (half + 1) * near].astype(F32)
        flat = (chosen * mask[None]).astype(BF16).reshape(near * ROWS, width)
        rolled = []
        for c in range(COLS):
            turned = lax.dot_general(
                pick_ref[c].astype(BF16),
                flat,
                (((1,), (1,)), ((), ())),
                preferred_element_type=F32,
            )
            rolled.append([turned if n == 0 else pltpu.roll(turned, 32 * n, 1) for n in range(4)])
        for f in range(near):
            for part in range(2):
                value = None
                for g in range(4):
                    piece = rolled[part * 4 + g][(g - f) % 4]
                    value = piece if value is None else jnp.where(lane_group == g, piece, value)
                at = half * near + f
                (low_ref, high_ref)[part][pl.ds(at, BLOCKS, stride=LOCAL), :] = value
    count = TILES * LOCAL
    for at, source, start in (
        (0, low_ref, 0),
        (128, high_ref, 0),
        (256, low_ref, 8),
        (384, high_ref, 8),
        (512, low_ref, 16),
    ):
        out_ref[:, at : at + 128] = source[start : start + count, :].astype(BF16)


def pack(frames, mask):
    return pl.pallas_call(
        pack_kernel,
        out_shape=pltpu.VMEM((TILES * LOCAL, WIDE * ROWS), BF16),
        in_specs=[pl.BlockSpec(memory_space=pltpu.HBM)] * 2,
        scratch_shapes=[
            pltpu.VMEM(frames.shape, BF16),
            pltpu.VMEM(mask.shape, jnp.int32),
            pltpu.VMEM((COLS, BLOCKS, mask.shape[1]), F32),
            pltpu.VMEM((BLOCKS * LOCAL, 128), F32),
            pltpu.VMEM((BLOCKS * LOCAL, 128), F32),
            pltpu.SemaphoreType.DMA((3,)),
        ],
        compiler_params=pltpu.CompilerParams(vmem_limit_bytes=60000000),
    )(frames, mask)


def spectra_kernel(series_ref, table_ref, own_ref, even_ref, odd_ref):
    spectrum = lax.dot_general(
        series_ref[...],
        table_ref[...],
        (((0,), (0,)), ((), ())),
        preferred_element_type=F32,
    )
    own_ref[...] = spectrum.astype(BF16)
    by_column = spectrum.reshape(WIDE, ROWS, 2 * FREQ)
    last = by_column[:, ROWS - 8 :].reshape(WIDE * 8, 2 * FREQ).astype(BF16)
    first = by_column[:, :8].reshape(WIDE * 8, 2 * FREQ).astype(BF16)
    odd_band = lax.axis_index("band") % 2

    @pl.when(odd_band == 0)
    def _():
        even_ref[...] = last
        odd_ref[...] = first

    @pl.when(odd_band == 1)
    def _():
        even_ref[...] = first
        odd_ref[...] = last


def spectra(series, table):
    edge = jax.ShapeDtypeStruct((WIDE * 8, 2 * FREQ), BF16)
    return pl.pallas_call(
        spectra_kernel,
        out_shape=(jax.ShapeDtypeStruct((WIDE * ROWS, 2 * FREQ), BF16), edge, edge),
        compiler_params=pltpu.CompilerParams(vmem_limit_bytes=32 * 1024 * 1024),
    )(series, table)


def filtered(tall, at, rows, gain, mix):
    rim = tall[1]
    tall = tall[0]
    inner = tall[at : at + rows, :]
    beside = 0.25 * (
        tall[at + 1 : at + 1 + rows, :]
        + tall[at - 1 : at - 1 + rows, :]
        + tall[at + rim : at + rim + rows, :]
        + tall[at - rim : at - rim + rows, :]
    )
    return gain * inner + mix * (beside - inner)


def block_rows(rows, offsets_ref, filt_re, filt_im, centre_re, centre_im, sums):
    def distance(d, carry):
        starts = [offsets_ref[d * OFFS + k] for k in range(OFFS)]
        for n, row in enumerate(rows):
            for part in range(2):
                first = jnp.zeros((8, 128), F32)
                second = jnp.zeros((8, 128), F32)
                for c in range(part * 4, part * 4 + 4):
                    shift = c * REACH + row
                    real_a = filt_re[pl.ds(starts[0] + shift, 8), :]
                    imag_a = filt_im[pl.ds(starts[0] + shift, 8), :]
                    for k in range(1, OFFS):
                        real_a = real_a + filt_re[pl.ds(starts[k] + shift, 8), :]
                        imag_a = imag_a + filt_im[pl.ds(starts[k] + shift, 8), :]
                    at = (n * COLS + c) * 8
                    real_c = centre_re[at : at + 8, :]
                    imag_c = centre_im[at : at + 8, :]
                    first = first + (real_c * real_a + imag_c * imag_a)
                    second = second + (real_c * imag_a - imag_c * real_a)
                at = pl.multiple_of(((n * 2 + part) * 16 + 2 * d) * 8, 8)
                sums[pl.ds(at, 8), :] = first
                sums[pl.ds(at + 8, 8), :] = second
        return carry

    lax.fori_loop(0, DIST, distance, 0)


def block_means(rows, sums, seen, out_ref):
    for n, row in enumerate(rows):
        for half in range(2):
            for part in range(2):
                at = row + part * ROWS + half * 4
                count = seen[pl.ds(at, 1), :]
                for k in range(1, 4):
                    count = count + seen[pl.ds(at + k, 1), :]
                denom = jnp.broadcast_to(jnp.maximum(count, 1.0), (8, 128))
                for piece in range(2):
                    base = ((n * 2 + part) * 16 + piece * 8) * 8 + half * 4
                    total = sums[pl.ds(base, 8, stride=8), :]
                    for k in range(1, 4):
                        total = total + sums[pl.ds(base + k, 8, stride=8), :]
                    to = ((n * 2 + half) * 2 + part) * 16 + piece * 8
                    out_ref[to : to + 8, :] = total / denom


def middle_kernel(
    offsets_ref,
    own_ref,
    mask_ref,
    gain_ref,
    mix_ref,
    out_ref,
    filt_re,
    filt_im,
    seen,
    pair_ref,
    own_re,
    own_im,
    centre_re,
    centre_im,
    sums,
):
    own_re[...] = own_ref[:, :FREQ].astype(F32)
    own_im[...] = own_ref[:, FREQ:].astype(F32)
    gain = gain_ref[...]
    mix = mix_ref[...]
    pair_ref[0:1, :] = gain
    pair_ref[1:2, :] = mix
    for source, filt in ((own_re, filt_re), (own_im, filt_im)):
        for q in range(SIDE):
            at = (q + 2) * ROWS + 1
            value = filtered((source, ROWS), at, ROWS - 2, gain, mix)
            filt[q * REACH + 5 : q * REACH + 5 + ROWS - 2, :] = value

    tile = lax.axis_index("tile")
    wide = pl.multiple_of((tile // 16) * 128, 128)
    near = mask_ref[:, pl.ds(wide, 128)].astype(F32)
    near = pltpu.roll(near, (128 - 8 * (tile % 16)) % 128, 1)
    for part in range(2):
        total = jnp.zeros((ROWS, 128), F32)
        for c in range(part * 4, part * 4 + 4):
            weight = jnp.broadcast_to(near[:, c : c + 1], (ROWS, 128))
            total = total + weight
            for n, row in enumerate((8, 16)):
                at = (c + 4) * REACH + 4 + row
                to = (n * COLS + c) * 8
                centre_re[to : to + 8, :] = filt_re[at : at + 8, :] * weight[row : row + 8]
                centre_im[to : to + 8, :] = filt_im[at : at + 8, :] * weight[row : row + 8]
            pair_ref[8 + c * 8 : 16 + c * 8, :] = weight[0:8]
            pair_ref[72 + c * 8 : 80 + c * 8, :] = weight[24:32]
        seen[part * ROWS : (part + 1) * ROWS, :] = total

    rows = (8, 16)
    block_rows(rows, offsets_ref, filt_re, filt_im, centre_re, centre_im, sums)
    block_means(rows, sums, seen, out_ref)


def edge_rows(
    top,
    offsets_ref,
    came_ref,
    went_ref,
    own_filt_re,
    own_filt_im,
    seen,
    pair_ref,
    result,
    tall_re,
    tall_im,
    filt_re,
    filt_im,
    centre_re,
    centre_im,
    sums,
):
    for at, ref in ((8 - 8 * top, came_ref), (8 * top, went_ref)):
        value = ref[...].astype(F32).reshape(WIDE, 8, 2 * FREQ)
        at = pl.multiple_of(at, 8)
        for q in range(WIDE):
            tall_re[pl.ds(at + q * 16, 8), :] = value[q, :, :FREQ]
            tall_im[pl.ds(at + q * 16, 8), :] = value[q, :, FREQ:]
    gain = pair_ref[0:1, :]
    mix = pair_ref[1:2, :]
    edge = pl.multiple_of(32 - 32 * top, 8)
    kept = pl.multiple_of(24 - 16 * top, 8)
    row = pl.multiple_of(24 - 24 * top, 8)
    for tall, inside, filt in ((tall_re, own_filt_re, filt_re), (tall_im, own_filt_im, filt_im)):
        for q in range(SIDE):
            at = q * REACH
            filt[pl.ds(edge + at, 8), :] = filtered((tall, 16), (q + 2) * 16 + 4, 8, gain, mix)
            filt[pl.ds(kept + at, 8), :] = inside[pl.ds(kept + at, 8), :]
    for c in range(COLS):
        weight = pair_ref[pl.ds(pl.multiple_of(72 - 64 * top, 8) + c * 8, 8), :]
        at = (c + 4) * REACH + 4
        centre_re[c * 8 : c * 8 + 8, :] = filt_re[pl.ds(row + at, 8), :] * weight
        centre_im[c * 8 : c * 8 + 8, :] = filt_im[pl.ds(row + at, 8), :] * weight
    block_rows((row,), offsets_ref, filt_re, filt_im, centre_re, centre_im, sums)
    block_means((row,), sums, seen, result)


def edge_kernel(*refs):
    edge_rows(lax.axis_index("band") % 2, *refs)


def last_kernel(offsets_ref, came_ref, went_ref, filt_re, filt_im, seen, pair_ref, mid_ref, edge_ref, out_ref, result, *rest):
    sems = rest[-1]
    top = 1 - lax.axis_index("band") % 2
    there = pl.multiple_of(192 * top, 64)
    here = pl.multiple_of(192 - 192 * top, 64)
    copies = [
        pltpu.make_async_copy(mid_ref, out_ref.at[pl.ds(64, 128)], sems.at[0]),
        pltpu.make_async_copy(edge_ref, out_ref.at[pl.ds(there, 64)], sems.at[1]),
        pltpu.make_async_copy(result, out_ref.at[pl.ds(here, 64)], sems.at[2]),
    ]
    copies[0].start()
    copies[1].start()
    edge_rows(
        top, offsets_ref, came_ref, went_ref, filt_re, filt_im, seen, pair_ref, result, *rest[:-1]
    )
    copies[2].start()
    for copy in copies:
        copy.wait()


def float_shape(rows):
    return jax.ShapeDtypeStruct((rows, FREQ), F32)


def middle(starts, own, mask, gain, mix):
    vmem = pl.BlockSpec(memory_space=pltpu.VMEM)
    rows = (128, SIDE * REACH, SIDE * REACH, 2 * ROWS, 136)
    return pl.pallas_call(
        middle_kernel,
        out_shape=tuple(float_shape(n) for n in rows),
        in_specs=[pl.BlockSpec(memory_space=pltpu.SMEM)] + [vmem] * 4,
        scratch_shapes=[
            pltpu.VMEM((WIDE * ROWS, FREQ), F32),
            pltpu.VMEM((WIDE * ROWS, FREQ), F32),
            pltpu.VMEM((2 * COLS * 8, FREQ), F32),
            pltpu.VMEM((2 * COLS * 8, FREQ), F32),
            pltpu.VMEM((4 * 16 * 8, FREQ), F32),
        ],
        compiler_params=pltpu.CompilerParams(vmem_limit_bytes=32 * 1024 * 1024),
        cost_estimate=pl.CostEstimate(flops=6_000_000, bytes_accessed=4_000_000, transcendentals=0),
    )(starts, own, mask, gain, mix)


def edges(starts, even, odd, kept):
    vmem = pl.BlockSpec(memory_space=pltpu.VMEM)
    smem = pl.BlockSpec(memory_space=pltpu.SMEM)
    bands = lax.axis_size("band")
    pairs = [(i, i ^ 1) for i in range(bands)]
    between = [(i, ((i + 1) ^ 1) - 1) for i in range(1, bands - 1)]
    came_even = lax.ppermute(even, "band", pairs)
    came_odd = lax.ppermute(odd, "band", between)
    mid, *shared = kept
    rows = [WIDE * 16] * 2 + [SIDE * REACH] * 2 + [COLS * 8] * 2 + [2 * 16 * 8]
    scratch = [pltpu.VMEM((n, FREQ), F32) for n in rows]
    params = pltpu.CompilerParams(vmem_limit_bytes=32 * 1024 * 1024)
    cost = pl.CostEstimate(flops=3_000_000, bytes_accessed=3_000_000, transcendentals=0)
    edge = pl.pallas_call(
        edge_kernel,
        out_shape=float_shape(64),
        in_specs=[smem] + [vmem] * (2 + len(shared)),
        scratch_shapes=scratch,
        compiler_params=params,
        cost_estimate=cost,
    )(starts, came_even, even, *shared)
    return pl.pallas_call(
        last_kernel,
        out_shape=float_shape(8 * 2 * DIST * 2),
        in_specs=[smem] + [vmem] * (4 + len(shared)),
        out_specs=pl.BlockSpec(memory_space=pltpu.HBM),
        scratch_shapes=[pltpu.VMEM((64, FREQ), F32)] + scratch + [pltpu.SemaphoreType.DMA((3,))],
        compiler_params=params,
        cost_estimate=cost,
    )(starts, came_odd, odd, *shared, mid, edge)


def on_device(frames, disk_mask, offsets, filter_gain, filter_mix):
    packed = pack(frames, disk_mask).reshape(TILES, LOCAL, WIDE * ROWS)
    received = lax.all_to_all(packed, "tile", split_axis=0, concat_axis=0, tiled=True)
    series = received.reshape(FRAMES, WIDE * ROWS)
    own, even, odd = spectra(series, dft_table())
    starts = ((offsets[..., 1] + 4) * REACH + offsets[..., 0] + 4).reshape(DIST * OFFS)
    gain = filter_gain.reshape(1, FREQ)
    mix = filter_mix.reshape(1, FREQ)
    out = edges(starts, even, odd, middle(starts, own, disk_mask, gain, mix))
    return out.reshape(8, 2, DIST, 2, FREQ)


def solution(mesh):
    return jax.shard_map(
        on_device,
        mesh=mesh,
        in_specs=(P("tile", "band", None), P("band", None), P(), P(), P()),
        out_specs=P("band", "tile", None, None, None),
        check_vma=False,
    )
```

time: 48.3 us -> 47.5 us (0.983)
  the two profiles are of different devices: /device:TPU:198 before, /device:TPU:192 now
where the time goes in v3:
time: 47.5 us; the launch traced here: 47.3 us
  blocking collectives  30.5 us (64%)
  starting transfers between devices  8.87 us (19%)
  Pallas kernels  7.06 us (15%)
  local copies, waits for them, and re-layouts  0.75 us (2%)
    all_to_all x1, blocking collectives, on_device(): lax.all_to_all(packed, 'tile', split_axis=0, concat_axis=0, tiled=True)  30.5 us
    ppermute x1, starting transfers between devices, edges(): came_odd = lax.ppermute(odd, 'band', between)  6.95 us
    pallas_call x1, Pallas kernels, pack(): pl.pallas_call(pack_kernel, out_shape=pltpu.VMEM((TILES * LOCAL, WIDE * R...  2.22 us
    ppermute x1, starting transfers between devices, edges(): came_even = lax.ppermute(even, 'band', pairs)  1.92 us
    pallas_call x1, Pallas kernels, edges(): pl.pallas_call(last_kernel, out_shape=float_shape(8 * 2 * DIST * 2), in_s...  1.72 us
    pallas_call x1, Pallas kernels, middle(): pl.pallas_call(middle_kernel, out_shape=tuple((float_shape(n) for n in ro...  1.65 us
    pallas_call x1, Pallas kernels, edges(): pl.pallas_call(edge_kernel, out_shape=float_shape(64), in_specs=[smem] +...  1.07 us
  transfers between devices with their start and end apart: 2, of which 0 were waited for; matrix products, arithmetic and copies ran while one was open for 0% of the time, Pallas kernels for 6%

profile of v3, /device:TPU:192, one launch (start us, length us, event | category | flops | bytes accessed | tf_op | source)
XLA Modules:
  0.0 47.3 jit_solution(2469024604123261948)
XLA Ops:
  0.0 2.2 %shard_map.64 = bf16[512,640]{1,0:T(8,128)(2,1)S(1)} custom-call(bf16[8,32,512]{2,1,0:T(8,128)(2,1)} %frames_ref.1, s32[32,512]{1,0:T(8,128)} %mask_ref.3), custom_call_target="tpu_custom_call" | custom-call | tf_op jit(solution)/shard_map/pallas_call | solution.py:92
  2.2 0.0 copy-start
  2.2 30.5 %all_to_all.5 = bf16[64,8,640]{2,1,0:T(8,128)(2,1)S(1)} all-to-all(bf16[64,8,640]{2,1,0:T(8,128)(2,1)S(1)} %bitcast.6), channel_id=1, replica_groups=mesh['band'=8,'tile'=64] {'tile'}, dimensions={0} | all-to-all | bytes 1310720 | tf_op jit(solution)/shard_map/all_to_all | solution.py:375
  32.7 0.0 copy-done
  32.7 0.0 copy-start.4
  32.7 0.0 copy-start.1
  32.7 0.4 shard_map.65
  33.1 1.9 %collective-permute-start.1 = (bf16[160,256]{1,0:T(8,128)(2,1)S(1)}, bf16[160,256]{1,0:T(8,128)(2,1)S(1)}, u32[]{:S(2)}, u32[]{:S(2)}) collective-permute-start(bf16[160,256]{1,0:T(8,128)(2,1)S(1)} %get-tuple-element.20.refs_2_), channel_id=1, source_target_pairs={{0,64},{64,0},{128,192},{192,128},{256,320},{320,256},{384,448},{4... | collective-permute-start | bytes 245768 | tf_op jit(solution)/shard_map/ppermute | solution.py:347
  35.0 7.0 %collective-permute-start = (bf16[160,256]{1,0:T(8,128)(2,1)S(1)}, bf16[160,256]{1,0:T(8,128)(2,1)S(1)}, u32[]{:S(2)}, u32[]{:S(2)}) collective-permute-start(bf16[160,256]{1,0:T(8,128)(2,1)S(1)} %get-tuple-element.13.went_ref), channel_id=1, source_target_pairs={{64,128},{128,64},{192,256},{256,192},{320,384},{384,320},{65,129}... | collective-permute-start | bytes 245768 | tf_op jit(solution)/shard_map/ppermute | solution.py:348
  42.0 0.0 copy-done.4
  42.0 0.1 add.20.offsets_ref.refs_0_
  42.1 0.0 copy-start.2
  42.1 0.0 copy-start.3
  42.1 0.0 copy-done.1
  42.1 0.6 %copy-done.2 = f32[128]{0:T(128)S(1)} copy-done((f32[128]{0:T(128)S(1)}, f32[128]{0:T(128)}, u32[]{:S(2)}) %copy-start.2) | copy-done | bytes 536
  42.8 0.0 copy-done.3
  42.8 1.7 %shard_map.66 = (f32[128,128]{1,0:T(8,128)S(1)}, f32[640,128]{1,0:T(8,128)S(1)}, f32[640,128]{1,0:T(8,128)S(1)}, f32[64,128]{1,0:T(8,128)S(1)}, f32[136,128]{1,0:T(8,128)S(1)}) custom-call(s32[64]{0:T(128)S(1)} %add.20.offsets_ref.refs_0_, bf16[640,256]{1,0:T(8,128)(2,1)S(1)} %get-tuple-element.14.own_ref, s32[32,512]{1,0:T(8,128)S(1)} %copy-done.1, ...), custom_call_target="tpu_custom_call" | custom-call | flops 6000000 | bytes 4000000 | tf_op jit(solution)/shard_map/pallas_call | solution.py:325
  44.5 0.0 collective-permute-done.1.refs_1_
  44.5 1.1 %shard_map.67.edge_ref = f32[64,128]{1,0:T(8,128)S(1)} custom-call(s32[64]{0:T(128)S(1)} %add.20.offsets_ref.refs_0_, bf16[160,256]{1,0:T(8,128)(2,1)S(1)} %collective-permute-done.1.refs_1_, bf16[160,256]{1,0:T(8,128)(2,1)S(1)} %get-tuple-element.20.refs_2_, f32[640,128]{1,0:T(8,128)S(1)} %get-tuple-element.15.refs_3_.filt_re, ...), custom_call_target="tpu_custom_call" | custom-call | flops 3000000 | bytes 3000000 | tf_op jit(solution)/shard_map/pallas_call | solution.py:354
  45.5 0.0 collective-permute-done.came_ref
  45.6 1.7 %shard_map.68 = f32[256,128]{1,0:T(8,128)} custom-call(s32[64]{0:T(128)S(1)} %add.20.offsets_ref.refs_0_, bf16[160,256]{1,0:T(8,128)(2,1)S(1)} %collective-permute-done.came_ref, bf16[160,256]{1,0:T(8,128)(2,1)S(1)} %get-tuple-element.13.went_ref, f32[640,128]{1,0:T(8,128)S(1)} %get-tuple-element.15.refs_3_.filt_re, ...), custom_call_target="tpu_custom_call" | custom-call | flops 3000000 | bytes 3000000 | tf_op jit(solution)/shard_map/pallas_call | solution.py:362
  (1 shorter events, 0.0 us)
Async XLA Ops:
  2.2 30.5 %copy-start = (bf16[512,256]{1,0:T(8,128)(2,1)S(1)}, bf16[512,256]{1,0:T(8,128)(2,1)}, u32[]{:S(2)}) copy-start(bf16[512,256]{1,0:T(8,128)(2,1)} %constant.8.table_ref) | copy-start | bytes 786436
  32.7 9.3 %copy-start.4 = (s32[8,8,2]{1,2,0:T(2,128)S(1)}, s32[8,8,2]{1,2,0:T(2,128)}, u32[]{:S(2)}) copy-start(s32[8,8,2]{1,2,0:T(2,128)} %param.8) | copy-start | bytes 1540
  32.7 9.4 %copy-start.1 = (s32[32,512]{1,0:T(8,128)S(1)}, s32[32,512]{1,0:T(8,128)}, u32[]{:S(2)}) copy-start(s32[32,512]{1,0:T(8,128)} %mask_ref.3) | copy-start | bytes 196612
  33.1 11.3 %collective-permute-start.1 = (bf16[160,256]{1,0:T(8,128)(2,1)S(1)}, bf16[160,256]{1,0:T(8,128)(2,1)S(1)}, u32[]{:S(2)}, u32[]{:S(2)}) collective-permute-start(bf16[160,256]{1,0:T(8,128)(2,1)S(1)} %get-tuple-element.20.refs_2_), channel_id=1, source_target_pairs={{0,64},{64,0},{128,192},{192,128},{256,320},{320,256},{384,448},{4... | collective-permute-start | bytes 245768 | tf_op jit(solution)/shard_map/ppermute | solution.py:347
  35.0 10.5 %collective-permute-start = (bf16[160,256]{1,0:T(8,128)(2,1)S(1)}, bf16[160,256]{1,0:T(8,128)(2,1)S(1)}, u32[]{:S(2)}, u32[]{:S(2)}) collective-permute-start(bf16[160,256]{1,0:T(8,128)(2,1)S(1)} %get-tuple-element.13.went_ref), channel_id=1, source_target_pairs={{64,128},{128,64},{192,256},{256,192},{320,384},{384,320},{65,129}... | collective-permute-start | bytes 245768 | tf_op jit(solution)/shard_map/ppermute | solution.py:348
  42.1 0.7 %copy-start.2 = (f32[128]{0:T(128)S(1)}, f32[128]{0:T(128)}, u32[]{:S(2)}) copy-start(f32[128]{0:T(128)} %param.9) | copy-start | bytes 1540
  42.1 0.7 %copy-start.3 = (f32[128]{0:T(128)S(1)}, f32[128]{0:T(128)}, u32[]{:S(2)}) copy-start(f32[128]{0:T(128)} %param.10) | copy-start | bytes 1540

commit v4 on v3

v4 whole, which is shorter than its diff:
```python
import math

import jax
import jax.numpy as jnp
import numpy as np
from jax import lax
from jax.experimental import pallas as pl
from jax.experimental.pallas import tpu as pltpu
from jax.sharding import PartitionSpec as P

FRAMES = 512
FREQ = 128
DIST = 8
OFFS = 8
FLO = 48
TILES = 64
LOCAL = 8
ROWS = 32
COLS = 8
WIDE = 20
LEAD = 6
BLOCKS = 72
TALL = 48
REACH = 40
SIDE = 16

F32 = jnp.float32
BF16 = jnp.bfloat16


def dft_table():
    times = np.arange(FRAMES, dtype=np.int32)
    freqs = FLO + np.arange(FREQ, dtype=np.int32)
    phases = times[:, None] * freqs[None, :] % FRAMES
    angles = phases.astype(np.float32) * np.float32(2.0 * math.pi / FRAMES)
    factor = np.float32(1.0 / math.sqrt(FRAMES))
    both = np.concatenate([np.cos(angles) * factor, -np.sin(angles) * factor], axis=1)
    return jnp.asarray(both.astype(np.float32)).astype(BF16)


def pack_kernel(
    frames_ref, mask_ref, out_ref, frames_vmem, mask_vmem, pick_ref, low_ref, high_ref, laid_ref, sems
):
    copies = [
        pltpu.make_async_copy(mask_ref, mask_vmem, sems.at[0]),
        pltpu.make_async_copy(frames_ref, frames_vmem, sems.at[1]),
    ]
    for copy in copies:
        copy.start()
    width = mask_vmem.shape[1]
    cols = lax.broadcasted_iota(jnp.int32, (BLOCKS, width), 1)
    block = lax.broadcasted_iota(jnp.int32, (BLOCKS, width), 0)
    place = cols - 8 * block + LEAD
    for c in range(COLS):
        pick_ref[c * BLOCKS : (c + 1) * BLOCKS, :] = jnp.where(place == c, 1.0, 0.0)
    for copy in copies:
        copy.wait()
    mask = mask_vmem[...].astype(F32)
    masked = (frames_vmem[...].astype(F32) * mask[None]).astype(BF16)
    turned = lax.dot_general(
        pick_ref[...].astype(BF16),
        masked.reshape(LOCAL * ROWS, width),
        (((1,), (1,)), ((), ())),
        preferred_element_type=F32,
    )
    lane_group = lax.broadcasted_iota(jnp.int32, (BLOCKS, 128), 1) // 32
    for half in range(2):
        lanes = slice(half * 128, half * 128 + 128)
        rolled = []
        for c in range(COLS):
            piece = turned[c * BLOCKS : (c + 1) * BLOCKS, lanes]
            rolled.append([piece if n == 0 else pltpu.roll(piece, 32 * n, 1) for n in range(4)])
        for f in range(4):
            for part in range(2):
                value = None
                for g in range(4):
                    piece = rolled[part * 4 + g][(g - f) % 4]
                    value = piece if value is None else jnp.where(lane_group == g, piece, value)
                at = half * 4 + f
                (low_ref, high_ref)[part][pl.ds(at, BLOCKS, stride=LOCAL), :] = value
    rows = TILES * LOCAL // 4
    parts = []
    for n in range(4):
        here = slice(n * rows, (n + 1) * rows)
        for at, source, start in (
            (0, low_ref, 0),
            (128, high_ref, 0),
            (256, low_ref, 8),
            (384, high_ref, 8),
            (512, low_ref, 16),
        ):
            start = start + n * rows
            laid_ref[here, at : at + 128] = source[start : start + rows, :].astype(BF16)
        parts.append(pltpu.make_async_copy(laid_ref.at[here], out_ref.at[here], sems.at[2 + n]))
        parts[n].start()
    for part in parts:
        part.wait()


def pack(frames, mask):
    return pl.pallas_call(
        pack_kernel,
        out_shape=jax.ShapeDtypeStruct((TILES * LOCAL, WIDE * ROWS), BF16),
        in_specs=[pl.BlockSpec(memory_space=pltpu.HBM)] * 2,
        out_specs=pl.BlockSpec(memory_space=pltpu.HBM),
        scratch_shapes=[
            pltpu.VMEM(frames.shape, BF16),
            pltpu.VMEM(mask.shape, jnp.int32),
            pltpu.VMEM((COLS * BLOCKS, mask.shape[1]), F32),
            pltpu.VMEM((BLOCKS * LOCAL, 128), F32),
            pltpu.VMEM((BLOCKS * LOCAL, 128), F32),
            pltpu.VMEM((TILES * LOCAL, WIDE * ROWS), BF16),
            pltpu.SemaphoreType.DMA((6,)),
        ],
        compiler_params=pltpu.CompilerParams(vmem_limit_bytes=60000000),
    )(frames, mask)


def spectra_kernel(series_ref, table_ref, pair_ref, own_ref, even_ref, odd_ref):
    spectrum = lax.dot_general(
        series_ref[...],
        table_ref[...],
        (((0,), (0,)), ((), ())),
        preferred_element_type=F32,
    )
    own_ref[...] = spectrum.astype(BF16)
    by_column = spectrum.reshape(WIDE, ROWS, 2 * FREQ)
    last = by_column[:, ROWS - 8 :].reshape(WIDE * 8, 2 * FREQ).astype(BF16)
    first = by_column[:, :8].reshape(WIDE * 8, 2 * FREQ).astype(BF16)
    odd_band = lax.axis_index("band") % 2

    @pl.when(odd_band == 0)
    def _():
        even_ref[...] = last
        odd_ref[...] = first

    @pl.when(odd_band == 1)
    def _():
        even_ref[...] = first
        odd_ref[...] = last


def spectra(series, table, pair):
    edge = jax.ShapeDtypeStruct((WIDE * 8, 2 * FREQ), BF16)
    return pl.pallas_call(
        spectra_kernel,
        out_shape=(jax.ShapeDtypeStruct((WIDE * ROWS, 2 * FREQ), BF16), edge, edge),
        compiler_params=pltpu.CompilerParams(vmem_limit_bytes=32 * 1024 * 1024),
    )(series, table, pair)


def select_kernel(offsets_ref, mask_ref, gain_ref, mix_ref, pick_ref, weight_ref, share_ref, pair_ref):
    shape = (COLS * 8, SIDE * 16)
    pixel = lax.broadcasted_iota(jnp.int32, shape, 0)
    lane = lax.broadcasted_iota(jnp.int32, shape, 1)
    apart = lane - (pixel // 8) * 16 - pixel % 8

    def distance(d, carry):
        total = jnp.zeros(shape, F32)
        for k in range(OFFS):
            total = total + jnp.where(apart == offsets_ref[d * OFFS + k], 1.0, 0.0)
        picked = total.astype(BF16)
        at = pl.multiple_of(d * COLS * 8, COLS * 8)
        pick_ref[pl.ds(at, COLS * 8), 0 : SIDE * 16] = picked
        pick_ref[pl.ds(at, COLS * 8), SIDE * 16 : 2 * SIDE * 16] = picked
        return carry

    lax.fori_loop(0, DIST, distance, 0)
    tile = lax.axis_index("tile")
    wide = pl.multiple_of((tile // 16) * 128, 128)
    near = mask_ref[:, pl.ds(wide, 128)].astype(F32)
    near = pltpu.roll(near, (128 - 8 * (tile % 16)) % 128, 1)
    for part in range(2):
        total = jnp.zeros((ROWS, 128), F32)
        for c in range(part * 4, part * 4 + 4):
            weight = jnp.broadcast_to(near[:, c : c + 1], (ROWS, 128))
            total = total + weight
            for group in range(4):
                at = (group * COLS + c) * 8
                weight_ref[at : at + 8, :] = weight[group * 8 : group * 8 + 8]
        for block in range(8):
            count = total[block * 4 : block * 4 + 1]
            for k in range(1, 4):
                count = count + total[block * 4 + k : block * 4 + k + 1]
            share_ref[block * 2 + part : block * 2 + part + 1, :] = 1.0 / jnp.maximum(count, 1.0)
    pair_ref[0:1, :] = gain_ref[...]
    pair_ref[1:2, :] = mix_ref[...]


def filtered(tall, rim, at, rows, gain, mix):
    inner = tall[at : at + rows, :]
    beside = 0.25 * (
        tall[at + 1 : at + 1 + rows, :]
        + tall[at - 1 : at - 1 + rows, :]
        + tall[at + rim : at + rim + rows, :]
        + tall[at - rim : at - rim + rows, :]
    )
    return gain * inner + mix * (beside - inner)


def group_blocks(group, pick_ref, filt_re, filt_im, weight_ref, share_ref, out_ref, first, scratch):
    window, annulus, sums = scratch
    size = SIDE * 16
    for q in range(SIDE):
        at = q * REACH + group * 8
        for filt, lanes in ((filt_re, slice(0, FREQ)), (filt_im, slice(FREQ, 2 * FREQ))):
            value = filt[at : at + 16, :]
            high = value.astype(BF16)
            low = (value - high.astype(F32)).astype(BF16)
            window[q * 16 : q * 16 + 16, lanes] = high
            window[size + q * 16 : size + q * 16 + 16, lanes] = low
    annulus[...] = jnp.dot(pick_ref[...], window[...], preferred_element_type=F32)
    for part in range(2):
        centre = []
        for c in range(part * 4, part * 4 + 4):
            at = (c + 4) * REACH + 4 + group * 8
            weight = weight_ref[(group * COLS + c) * 8 : (group * COLS + c) * 8 + 8, :]
            centre.append((filt_re[at : at + 8, :] * weight, filt_im[at : at + 8, :] * weight))
        for d in range(DIST):
            first_sum = None
            for c in range(4):
                at = (d * COLS + part * 4 + c) * 8
                real_a = annulus[at : at + 8, :FREQ]
                imag_a = annulus[at : at + 8, FREQ:]
                real_c, imag_c = centre[c]
                one = real_c * real_a + imag_c * imag_a
                two = real_c * imag_a - imag_c * real_a
                first_sum = one if first_sum is None else first_sum + one
                second_sum = two if c == 0 else second_sum + two
            at = (part * 16 + 2 * d) * 8
            sums[at : at + 8, :] = first_sum
            sums[at + 8 : at + 16, :] = second_sum
    for half in range(2):
        for part in range(2):
            block = (group * 2 + half) * 2 + part
            share = jnp.broadcast_to(share_ref[block : block + 1, :], (8, 128))
            for piece in range(2):
                base = (part * 16 + piece * 8) * 8 + half * 4
                total = sums[pl.ds(base, 8, stride=8), :]
                for k in range(1, 4):
                    total = total + sums[pl.ds(base + k, 8, stride=8), :]
                to = first + (half * 2 + part) * 16 + piece * 8
                out_ref[to : to + 8, :] = total * share


def middle_kernel(
    own_ref, pick_ref, weight_ref, share_ref, pair_ref, out_ref, filt_re, filt_im, own_re, own_im, *scratch
):
    own_re[...] = own_ref[:, :FREQ].astype(F32)
    own_im[...] = own_ref[:, FREQ:].astype(F32)
    gain = pair_ref[0:1, :]
    mix = pair_ref[1:2, :]
    for source, filt in ((own_re, filt_re), (own_im, filt_im)):
        for q in range(SIDE):
            value = filtered(source, ROWS, (q + 2) * ROWS + 1, ROWS - 2, gain, mix)
            filt[q * REACH + 5 : q * REACH + 5 + ROWS - 2, :] = value
    for n in range(2):
        group_blocks(
            1 + n, pick_ref, filt_re, filt_im, weight_ref, share_ref, out_ref, n * 64, scratch
        )


def outer_kernel(
    came_even,
    came_odd,
    went_even,
    went_odd,
    pick_ref,
    weight_ref,
    share_ref,
    pair_ref,
    mid_ref,
    own_filt_re,
    own_filt_im,
    out_ref,
    tall_re,
    tall_im,
    filt_re,
    filt_im,
    result,
    sems,
    *scratch,
):
    copies = [
        pltpu.make_async_copy(mid_ref, out_ref.at[64:192], sems.at[0]),
        pltpu.make_async_copy(result.at[0:64], out_ref.at[0:64], sems.at[1]),
        pltpu.make_async_copy(result.at[64:128], out_ref.at[192:256], sems.at[2]),
    ]
    copies[0].start()
    odd = lax.axis_index("band") % 2
    half = WIDE * 16
    for ref, at in (
        (came_even, (1 - odd) * (half + 8)),
        (went_even, odd * 8 + (1 - odd) * half),
        (came_odd, odd * (half + 8)),
        (went_odd, odd * half + (1 - odd) * 8),
    ):
        value = ref[...].astype(F32).reshape(WIDE, 8, 2 * FREQ)
        at = pl.multiple_of(at, 8)
        for q in range(WIDE):
            tall_re[pl.ds(at + q * 16, 8), :] = value[q, :, :FREQ]
            tall_im[pl.ds(at + q * 16, 8), :] = value[q, :, FREQ:]
    gain = pair_ref[0:1, :]
    mix = pair_ref[1:2, :]
    for n, group in enumerate((0, 3)):
        edge, kept = ((0, 8), (32, 24))[n]
        for tall, inside, filt in (
            (tall_re, own_filt_re, filt_re),
            (tall_im, own_filt_im, filt_im),
        ):
            for q in range(SIDE):
                at = q * REACH
                value = filtered(tall, 16, n * half + (q + 2) * 16 + 4, 8, gain, mix)
                filt[at + edge : at + edge + 8, :] = value
                filt[at + kept : at + kept + 8, :] = inside[at + kept : at + kept + 8, :]
        group_blocks(
            group, pick_ref, filt_re, filt_im, weight_ref, share_ref, result, n * 64, scratch
        )
        copies[1 + n].start()
    for copy in copies:
        copy.wait()


def float_shape(rows):
    return jax.ShapeDtypeStruct((rows, FREQ), F32)


VMEM = pl.BlockSpec(memory_space=pltpu.VMEM)
SMEM = pl.BlockSpec(memory_space=pltpu.SMEM)
GROUP_SCRATCH = [
    pltpu.VMEM((2 * SIDE * 16, 2 * FREQ), BF16),
    pltpu.VMEM((DIST * COLS * 8, 2 * FREQ), F32),
    pltpu.VMEM((2 * 16 * 8, FREQ), F32),
]


def params():
    return pltpu.CompilerParams(vmem_limit_bytes=32 * 1024 * 1024)


def select(steps, mask, gain, mix):
    return pl.pallas_call(
        select_kernel,
        out_shape=(
            jax.ShapeDtypeStruct((DIST * COLS * 8, 2 * SIDE * 16), BF16),
            float_shape(COLS * ROWS),
            float_shape(16),
            float_shape(8),
        ),
        in_specs=[SMEM] + [VMEM] * 3,
        compiler_params=params(),
        cost_estimate=pl.CostEstimate(flops=4_000_000, bytes_accessed=4_000_000, transcendentals=0),
    )(steps, mask, gain, mix)


def middle(own, chosen):
    return pl.pallas_call(
        middle_kernel,
        out_shape=(float_shape(128), float_shape(SIDE * REACH), float_shape(SIDE * REACH)),
        in_specs=[VMEM] * 5,
        scratch_shapes=[pltpu.VMEM((WIDE * ROWS, FREQ), F32)] * 2 + GROUP_SCRATCH,
        compiler_params=params(),
        cost_estimate=pl.CostEstimate(flops=6_000_000, bytes_accessed=4_000_000, transcendentals=0),
    )(own, *chosen)


def outer(even, odd, chosen, kept):
    bands = lax.axis_size("band")
    pairs = [(i, i ^ 1) for i in range(bands)]
    between = [(i, ((i + 1) ^ 1) - 1) for i in range(1, bands - 1)]
    came_even = lax.ppermute(even, "band", pairs)
    came_odd = lax.ppermute(odd, "band", between)
    rows = [WIDE * 32] * 2 + [SIDE * REACH] * 2 + [128]
    return pl.pallas_call(
        outer_kernel,
        out_shape=float_shape(8 * 2 * DIST * 2),
        in_specs=[VMEM] * 11,
        out_specs=pl.BlockSpec(memory_space=pltpu.HBM),
        scratch_shapes=[pltpu.VMEM((n, FREQ), F32) for n in rows]
        + [pltpu.SemaphoreType.DMA((3,))]
        + GROUP_SCRATCH,
        compiler_params=params(),
    )(came_even, came_odd, even, odd, *chosen, *kept)


def on_device(frames, disk_mask, offsets, filter_gain, filter_mix):
    packed = pack(frames, disk_mask).reshape(TILES, LOCAL, WIDE * ROWS)
    received = lax.all_to_all(packed, "tile", split_axis=0, concat_axis=0, tiled=True)
    steps = ((offsets[..., 1] + 4) * 16 + offsets[..., 0] + 4).reshape(DIST * OFFS)
    gain = filter_gain.reshape(1, FREQ)
    mix = filter_mix.reshape(1, FREQ)
    chosen = select(steps, disk_mask, gain, mix)
    series = received.reshape(FRAMES, WIDE * ROWS)
    own, even, odd = spectra(series, dft_table(), chosen[-1])
    out = outer(even, odd, chosen, middle(own, chosen))
    return out.reshape(8, 2, DIST, 2, FREQ)


def solution(mesh):
    return jax.shard_map(
        on_device,
        mesh=mesh,
        in_specs=(P("tile", "band", None), P("band", None), P(), P(), P()),
        out_specs=P("band", "tile", None, None, None),
        check_vma=False,
    )
```

time: 47.5 us -> 47.1 us (level)
  the two profiles are of different devices: /device:TPU:192 before, /device:TPU:199 now
where the time goes in v4:
time: 47.1 us; the launch traced here: 46.8 us
  waiting for transfers between devices  20.1 us (43%)
  starting transfers between devices  19.6 us (42%)
  Pallas kernels  6.28 us (13%)
  local copies, waits for them, and re-layouts  0.76 us (2%)
    all_to_all x1, waiting for transfers between devices, on_device(): lax.all_to_all(packed, 'tile', split_axis=0, concat_axis=0, tiled=True)  18 us
    all_to_all x1, starting transfers between devices, on_device(): lax.all_to_all(packed, 'tile', split_axis=0, concat_axis=0, tiled=True)  11.3 us
    ppermute x1, starting transfers between devices, outer(): came_odd = lax.ppermute(odd, 'band', between)  6.4 us
    pallas_call x1, Pallas kernels, pack(): pl.pallas_call(pack_kernel, out_shape=jax.ShapeDtypeStruct((TILES * LOCAL...  2.61 us
    ppermute x1, waiting for transfers between devices, outer(): came_odd = lax.ppermute(odd, 'band', between)  2.13 us
    ppermute x1, starting transfers between devices, outer(): came_even = lax.ppermute(even, 'band', pairs)  1.92 us
    pallas_call x1, Pallas kernels, outer(): pl.pallas_call(outer_kernel, out_shape=float_shape(8 * 2 * DIST * 2), in_...  1.32 us
    pallas_call x1, Pallas kernels, select(): pl.pallas_call(select_kernel, out_shape=(jax.ShapeDtypeStruct((DIST * COL...  1.22 us
  transfers between devices with their start and end apart: 3, of which 2 were waited for; matrix products, arithmetic and copies ran while one was open for 0% of the time, Pallas kernels for 4%

profile of v4, /device:TPU:199, one launch (start us, length us, event | category | flops | bytes accessed | tf_op | source)
XLA Modules:
  0.0 46.8 jit_solution(7865905921490810135)
XLA Ops:
  0.0 2.6 %shard_map.64 = bf16[512,640]{1,0:T(8,128)(2,1)} custom-call(bf16[8,32,512]{2,1,0:T(8,128)(2,1)} %frames_ref.1, s32[32,512]{1,0:T(8,128)} %mask_ref.3), custom_call_target="tpu_custom_call" | custom-call | tf_op jit(solution)/shard_map/pallas_call | solution.py:101
  2.6 0.0 copy-start.4
  2.6 0.0 copy-start.1
  2.6 0.0 copy-start
  2.7 11.3 %all-to-all-start = ((bf16[64,8,640]{2,1,0:T(8,128)(2,1)}), bf16[64,8,640]{2,1,0:T(8,128)(2,1)S(1)}, u32[]{:S(2)}, u32[]{:S(2)}) async-start(bf16[64,8,640]{2,1,0:T(8,128)(2,1)} %bitcast.8), calls=%async_computation | async-start | bytes 1310720 | tf_op jit(solution)/shard_map/all_to_all | solution.py:388
  13.9 0.0 copy-done.4
  14.0 0.1 add.20.offsets_ref
  14.0 0.0 copy-start.2
  14.0 0.0 copy-start.3
  14.0 0.0 copy-done.1
  14.1 0.6 %copy-done.2 = f32[128]{0:T(128)S(1)} copy-done((f32[128]{0:T(128)S(1)}, f32[128]{0:T(128)}, u32[]{:S(2)}) %copy-start.2) | copy-done | bytes 536
  14.7 0.0 copy-done.3
  14.7 1.2 %shard_map.65 = (bf16[512,512]{1,0:T(8,128)(2,1)S(1)}, f32[256,128]{1,0:T(8,128)S(1)}, f32[16,128]{1,0:T(8,128)S(1)}, f32[8,128]{1,0:T(8,128)S(1)}) custom-call(s32[64]{0:T(128)S(1)} %add.20.offsets_ref, s32[32,512]{1,0:T(8,128)S(1)} %copy-done.1, f32[1,128]{1,0:T(1,128)S(1)} %bitcast.6, f32[1,128]{1,0:T(1,128)S(1)} %bitcast.7), custom_call_target="tpu_custom_call" | custom-call | flops 4000000 | bytes 4000000 | tf_op jit(solution)/shard_map/pallas_call | solution.py:342
  15.9 18.0 %all-to-all-done = bf16[64,8,640]{2,1,0:T(8,128)(2,1)S(1)} async-done(((bf16[64,8,640]{2,1,0:T(8,128)(2,1)}), bf16[64,8,640]{2,1,0:T(8,128)(2,1)S(1)}, u32[]{:S(2)}, u32[]{:S(2)}) %all-to-all-start) | async-done | bytes 655392 | tf_op jit(solution)/shard_map/all_to_all | solution.py:388
  33.9 0.0 copy-done
  33.9 0.4 shard_map.66
  34.3 1.9 %collective-permute-start = (bf16[160,256]{1,0:T(8,128)(2,1)S(1)}, bf16[160,256]{1,0:T(8,128)(2,1)S(1)}, u32[]{:S(2)}, u32[]{:S(2)}) collective-permute-start(bf16[160,256]{1,0:T(8,128)(2,1)S(1)} %get-tuple-element.16.went_even), channel_id=1, source_target_pairs={{0,64},{64,0},{128,192},{192,128},{256,320},{320,256},{384,448},{4... | collective-permute-start | bytes 245768 | tf_op jit(solution)/shard_map/ppermute | solution.py:371
  36.2 6.4 %collective-permute-start.1 = (bf16[160,256]{1,0:T(8,128)(2,1)S(1)}, bf16[160,256]{1,0:T(8,128)(2,1)S(1)}, u32[]{:S(2)}, u32[]{:S(2)}) collective-permute-start(bf16[160,256]{1,0:T(8,128)(2,1)S(1)} %get-tuple-element.17.went_odd), channel_id=1, source_target_pairs={{64,128},{128,64},{192,256},{256,192},{320,384},{384,320},{65,129}... | collective-permute-start | bytes 245768 | tf_op jit(solution)/shard_map/ppermute | solution.py:372
  42.6 0.7 %shard_map.67 = (f32[128,128]{1,0:T(8,128)S(1)}, f32[640,128]{1,0:T(8,128)S(1)}, f32[640,128]{1,0:T(8,128)S(1)}) custom-call(bf16[640,256]{1,0:T(8,128)(2,1)S(1)} %get-tuple-element.21.own_ref, bf16[512,512]{1,0:T(8,128)(2,1)S(1)} %get-tuple-element.18.pick_ref, f32[256,128]{1,0:T(8,128)S(1)} %get-tuple-element.19.weight_ref, ...), custom_call_target="tpu_custom_call" | custom-call | flops 6000000 | bytes 4000000 | tf_op jit(solution)/shard_map/pallas_call | solution.py:357
  43.4 0.0 collective-permute-done.came_even
  43.4 2.1 %collective-permute-done.1.came_odd = bf16[160,256]{1,0:T(8,128)(2,1)S(1)} collective-permute-done((bf16[160,256]{1,0:T(8,128)(2,1)S(1)}, bf16[160,256]{1,0:T(8,128)(2,1)S(1)}, u32[]{:S(2)}, u32[]{:S(2)}) %collective-permute-start.1) | collective-permute-done | bytes 81952 | tf_op jit(solution)/shard_map/ppermute | solution.py:372
  45.5 1.3 %shard_map.68 = f32[256,128]{1,0:T(8,128)} custom-call(bf16[160,256]{1,0:T(8,128)(2,1)S(1)} %collective-permute-done.came_even, bf16[160,256]{1,0:T(8,128)(2,1)S(1)} %collective-permute-done.1.came_odd, bf16[160,256]{1,0:T(8,128)(2,1)S(1)} %get-tuple-element.16.went_even, bf16[160,256]{1,0:T(8,128)(2,1)S(1)} %get-tuple-element.17.went_odd, ...), custom_call_target="tpu_custom_call" | custom-call | tf_op jit(solution)/shard_map/pallas_call | solution.py:374
  (1 shorter events, 0.0 us)
Async XLA Ops:
  2.6 11.3 %copy-start.4 = (s32[8,8,2]{1,2,0:T(2,128)S(1)}, s32[8,8,2]{1,2,0:T(2,128)}, u32[]{:S(2)}) copy-start(s32[8,8,2]{1,2,0:T(2,128)} %param.8) | copy-start | bytes 1540
  2.6 11.4 %copy-start.1 = (s32[32,512]{1,0:T(8,128)S(1)}, s32[32,512]{1,0:T(8,128)}, u32[]{:S(2)}) copy-start(s32[32,512]{1,0:T(8,128)} %mask_ref.3) | copy-start | bytes 196612
  2.6 31.3 %copy-start = (bf16[512,256]{1,0:T(8,128)(2,1)S(1)}, bf16[512,256]{1,0:T(8,128)(2,1)}, u32[]{:S(2)}) copy-start(bf16[512,256]{1,0:T(8,128)(2,1)} %constant.8.table_ref) | copy-start | bytes 786436
  2.7 31.2 %all-to-all-start = ((bf16[64,8,640]{2,1,0:T(8,128)(2,1)}), bf16[64,8,640]{2,1,0:T(8,128)(2,1)S(1)}, u32[]{:S(2)}, u32[]{:S(2)}) async-start(bf16[64,8,640]{2,1,0:T(8,128)(2,1)} %bitcast.8), calls=%async_computation | async-start | bytes 1310720 | tf_op jit(solution)/shard_map/all_to_all | solution.py:388
  14.0 0.7 %copy-start.2 = (f32[128]{0:T(128)S(1)}, f32[128]{0:T(128)}, u32[]{:S(2)}) copy-start(f32[128]{0:T(128)} %param.9) | copy-start | bytes 1540
  14.0 0.7 %copy-start.3 = (f32[128]{0:T(128)S(1)}, f32[128]{0:T(128)}, u32[]{:S(2)}) copy-start(f32[128]{0:T(128)} %param.10) | copy-start | bytes 1540
  34.3 9.1 %collective-permute-start = (bf16[160,256]{1,0:T(8,128)(2,1)S(1)}, bf16[160,256]{1,0:T(8,128)(2,1)S(1)}, u32[]{:S(2)}, u32[]{:S(2)}) collective-permute-start(bf16[160,256]{1,0:T(8,128)(2,1)S(1)} %get-tuple-element.16.went_even), channel_id=1, source_target_pairs={{0,64},{64,0},{128,192},{192,128},{256,320},{320,256},{384,448},{4... | collective-permute-start | bytes 245768 | tf_op jit(solution)/shard_map/ppermute | solution.py:371
  36.2 9.3 %collective-permute-start.1 = (bf16[160,256]{1,0:T(8,128)(2,1)S(1)}, bf16[160,256]{1,0:T(8,128)(2,1)S(1)}, u32[]{:S(2)}, u32[]{:S(2)}) collective-permute-start(bf16[160,256]{1,0:T(8,128)(2,1)S(1)} %get-tuple-element.17.went_odd), channel_id=1, source_target_pairs={{64,128},{128,64},{192,256},{256,192},{320,384},{384,320},{65,129}... | collective-permute-start | bytes 245768 | tf_op jit(solution)/shard_map/ppermute | solution.py:372

commit v5 on v4

--- a/solution.py
+++ b/solution.py
@@ -116,7 +116,7 @@
     )(frames, mask)
 
 
-def spectra_kernel(series_ref, table_ref, pair_ref, own_ref, even_ref, odd_ref):
+def spectra_kernel(series_ref, table_ref, pair_ref, own_ref, first_ref, last_ref):
     spectrum = lax.dot_general(
         series_ref[...],
         table_ref[...],
@@ -125,19 +125,8 @@
     )
     own_ref[...] = spectrum.astype(BF16)
     by_column = spectrum.reshape(WIDE, ROWS, 2 * FREQ)
-    last = by_column[:, ROWS - 8 :].reshape(WIDE * 8, 2 * FREQ).astype(BF16)
-    first = by_column[:, :8].reshape(WIDE * 8, 2 * FREQ).astype(BF16)
-    odd_band = lax.axis_index("band") % 2
-
-    @pl.when(odd_band == 0)
-    def _():
-        even_ref[...] = last
-        odd_ref[...] = first
-
-    @pl.when(odd_band == 1)
-    def _():
-        even_ref[...] = first
-        odd_ref[...] = last
+    first_ref[...] = by_column[:, :8].reshape(WIDE * 8, 2 * FREQ).astype(BF16)
+    last_ref[...] = by_column[:, ROWS - 8 :].reshape(WIDE * 8, 2 * FREQ).astype(BF16)
 
 
 def spectra(series, table, pair):
@@ -261,10 +250,10 @@
 
 
 def outer_kernel(
-    came_even,
-    came_odd,
-    went_even,
-    went_odd,
+    after_ref,
+    before_ref,
+    first_ref,
+    last_ref,
     pick_ref,
     weight_ref,
     share_ref,
@@ -287,19 +276,12 @@
         pltpu.make_async_copy(result.at[64:128], out_ref.at[192:256], sems.at[2]),
     ]
     copies[0].start()
-    odd = lax.axis_index("band") % 2
     half = WIDE * 16
-    for ref, at in (
-        (came_even, (1 - odd) * (half + 8)),
-        (went_even, odd * 8 + (1 - odd) * half),
-        (came_odd, odd * (half + 8)),
-        (went_odd, odd * half + (1 - odd) * 8),
-    ):
+    for ref, at in ((before_ref, 0), (first_ref, 8), (last_ref, half), (after_ref, half + 8)):
         value = ref[...].astype(F32).reshape(WIDE, 8, 2 * FREQ)
-        at = pl.multiple_of(at, 8)
         for q in range(WIDE):
-            tall_re[pl.ds(at + q * 16, 8), :] = value[q, :, :FREQ]
-            tall_im[pl.ds(at + q * 16, 8), :] = value[q, :, FREQ:]
+            tall_re[at + q * 16 : at + q * 16 + 8, :] = value[q, :, :FREQ]
+            tall_im[at + q * 16 : at + q * 16 + 8, :] = value[q, :, FREQ:]
     gain = pair_ref[0:1, :]
     mix = pair_ref[1:2, :]
     for n, group in enumerate((0, 3)):
@@ -364,12 +346,12 @@
     )(own, *chosen)
 
 
-def outer(even, odd, chosen, kept):
+def outer(first, last, chosen, kept):
     bands = lax.axis_size("band")
-    pairs = [(i, i ^ 1) for i in range(bands)]
-    between = [(i, ((i + 1) ^ 1) - 1) for i in range(1, bands - 1)]
-    came_even = lax.ppermute(even, "band", pairs)
-    came_odd = lax.ppermute(odd, "band", between)
+    up = [(i, i + 1) for i in range(bands - 1)]
+    down = [(j, i) for i, j in up]
+    after = lax.ppermute(first, "band", down)
+    before = lax.ppermute(last, "band", up)
     rows = [WIDE * 32] * 2 + [SIDE * REACH] * 2 + [128]
     return pl.pallas_call(
         outer_kernel,
@@ -380,7 +362,7 @@
         + [pltpu.SemaphoreType.DMA((3,))]
         + GROUP_SCRATCH,
         compiler_params=params(),
-    )(came_even, came_odd, even, odd, *chosen, *kept)
+    )(after, before, first, last, *chosen, *kept)
 
 
 def on_device(frames, disk_mask, offsets, filter_gain, filter_mix):
@@ -391,8 +373,8 @@
     mix = filter_mix.reshape(1, FREQ)
     chosen = select(steps, disk_mask, gain, mix)
     series = received.reshape(FRAMES, WIDE * ROWS)
-    own, even, odd = spectra(series, dft_table(), chosen[-1])
-    out = outer(even, odd, chosen, middle(own, chosen))
+    own, first, last = spectra(series, dft_table(), chosen[-1])
+    out = outer(first, last, chosen, middle(own, chosen))
     return out.reshape(8, 2, DIST, 2, FREQ)
 
 

time: 47.1 us -> 45.2 us (0.960)
  the two profiles are of different devices: /device:TPU:199 before, /device:TPU:263 now
where the time goes in v5:
time: 45.2 us; the launch traced here: 45 us
  waiting for transfers between devices  21.3 us (47%)
  starting transfers between devices  16.5 us (37%)
  Pallas kernels  6.25 us (14%)
  local copies, waits for them, and re-layouts  0.76 us (2%)
    all_to_all x1, waiting for transfers between devices, on_device(): lax.all_to_all(packed, 'tile', split_axis=0, concat_axis=0, tiled=True)  18 us
    all_to_all x1, starting transfers between devices, on_device(): lax.all_to_all(packed, 'tile', split_axis=0, concat_axis=0, tiled=True)  11.3 us
    ppermute x1, starting transfers between devices, outer(): before = lax.ppermute(last, 'band', up)  3.36 us
    ppermute x1, waiting for transfers between devices, outer(): before = lax.ppermute(last, 'band', up)  3.14 us
    pallas_call x1, Pallas kernels, pack(): pl.pallas_call(pack_kernel, out_shape=jax.ShapeDtypeStruct((TILES * LOCAL...  2.61 us
    ppermute x1, starting transfers between devices, outer(): after = lax.ppermute(first, 'band', down)  1.92 us
    pallas_call x1, Pallas kernels, outer(): pl.pallas_call(outer_kernel, out_shape=float_shape(8 * 2 * DIST * 2), in_...  1.31 us
    pallas_call x1, Pallas kernels, select(): pl.pallas_call(select_kernel, out_shape=(jax.ShapeDtypeStruct((DIST * COL...  1.22 us
  transfers between devices with their start and end apart: 3, of which 3 were waited for; matrix products, arithmetic and copies ran while one was open for 0% of the time, Pallas kernels for 4%

profile of v5, /device:TPU:263, one launch (start us, length us, event | category | flops | bytes accessed | tf_op | source)
XLA Modules:
  0.0 45.0 jit_solution(17657677419422554032)
XLA Ops:
  0.0 2.6 %shard_map.64 = bf16[512,640]{1,0:T(8,128)(2,1)} custom-call(bf16[8,32,512]{2,1,0:T(8,128)(2,1)} %frames_ref.1, s32[32,512]{1,0:T(8,128)} %mask_ref.3), custom_call_target="tpu_custom_call" | custom-call | tf_op jit(solution)/shard_map/pallas_call | solution.py:101
  2.6 0.0 copy-start.4
  2.6 0.0 copy-start.1
  2.6 0.0 copy-start
  2.7 11.3 %all-to-all-start = ((bf16[64,8,640]{2,1,0:T(8,128)(2,1)}), bf16[64,8,640]{2,1,0:T(8,128)(2,1)S(1)}, u32[]{:S(2)}, u32[]{:S(2)}) async-start(bf16[64,8,640]{2,1,0:T(8,128)(2,1)} %bitcast.8), calls=%async_computation | async-start | bytes 1310720 | tf_op jit(solution)/shard_map/all_to_all | solution.py:370
  13.9 0.0 copy-done.4
  14.0 0.1 add.20.offsets_ref
  14.0 0.0 copy-start.2
  14.0 0.0 copy-start.3
  14.0 0.0 copy-done.1
  14.1 0.6 %copy-done.2 = f32[128]{0:T(128)S(1)} copy-done((f32[128]{0:T(128)S(1)}, f32[128]{0:T(128)}, u32[]{:S(2)}) %copy-start.2) | copy-done | bytes 536
  14.7 0.0 copy-done.3
  14.7 1.2 %shard_map.65 = (bf16[512,512]{1,0:T(8,128)(2,1)S(1)}, f32[256,128]{1,0:T(8,128)S(1)}, f32[16,128]{1,0:T(8,128)S(1)}, f32[8,128]{1,0:T(8,128)S(1)}) custom-call(s32[64]{0:T(128)S(1)} %add.20.offsets_ref, s32[32,512]{1,0:T(8,128)S(1)} %copy-done.1, f32[1,128]{1,0:T(1,128)S(1)} %bitcast.6, f32[1,128]{1,0:T(1,128)S(1)} %bitcast.7), custom_call_target="tpu_custom_call" | custom-call | flops 4000000 | bytes 4000000 | tf_op jit(solution)/shard_map/pallas_call | solution.py:324
  15.9 18.0 %all-to-all-done = bf16[64,8,640]{2,1,0:T(8,128)(2,1)S(1)} async-done(((bf16[64,8,640]{2,1,0:T(8,128)(2,1)}), bf16[64,8,640]{2,1,0:T(8,128)(2,1)S(1)}, u32[]{:S(2)}, u32[]{:S(2)}) %all-to-all-start) | async-done | bytes 655392 | tf_op jit(solution)/shard_map/all_to_all | solution.py:370
  33.9 0.0 copy-done
  33.9 0.4 shard_map.66
  34.3 1.9 %collective-permute-start = (bf16[160,256]{1,0:T(8,128)(2,1)S(1)}, bf16[160,256]{1,0:T(8,128)(2,1)S(1)}, u32[]{:S(2)}, u32[]{:S(2)}) collective-permute-start(bf16[160,256]{1,0:T(8,128)(2,1)S(1)} %get-tuple-element.16.first_ref), channel_id=1, source_target_pairs={{64,0},{128,64},{192,128},{256,192},{320,256},{384,320},{448,384},... | collective-permute-start | bytes 245768 | tf_op jit(solution)/shard_map/ppermute | solution.py:353
  36.2 3.4 %collective-permute-start.1 = (bf16[160,256]{1,0:T(8,128)(2,1)S(1)}, bf16[160,256]{1,0:T(8,128)(2,1)S(1)}, u32[]{:S(2)}, u32[]{:S(2)}) collective-permute-start(bf16[160,256]{1,0:T(8,128)(2,1)S(1)} %get-tuple-element.17.last_ref), channel_id=1, source_target_pairs={{0,64},{64,128},{128,192},{192,256},{256,320},{320,384},{384,448},... | collective-permute-start | bytes 245768 | tf_op jit(solution)/shard_map/ppermute | solution.py:354
  39.6 0.7 %shard_map.67 = (f32[128,128]{1,0:T(8,128)S(1)}, f32[640,128]{1,0:T(8,128)S(1)}, f32[640,128]{1,0:T(8,128)S(1)}) custom-call(bf16[640,256]{1,0:T(8,128)(2,1)S(1)} %get-tuple-element.21.own_ref, bf16[512,512]{1,0:T(8,128)(2,1)S(1)} %get-tuple-element.18.pick_ref, f32[256,128]{1,0:T(8,128)S(1)} %get-tuple-element.19.weight_ref, ...), custom_call_target="tpu_custom_call" | custom-call | flops 6000000 | bytes 4000000 | tf_op jit(solution)/shard_map/pallas_call | solution.py:339
  40.3 0.2 collective-permute-done.after_ref
  40.5 3.1 %collective-permute-done.1.before_ref = bf16[160,256]{1,0:T(8,128)(2,1)S(1)} collective-permute-done((bf16[160,256]{1,0:T(8,128)(2,1)S(1)}, bf16[160,256]{1,0:T(8,128)(2,1)S(1)}, u32[]{:S(2)}, u32[]{:S(2)}) %collective-permute-start.1) | collective-permute-done | bytes 81952 | tf_op jit(solution)/shard_map/ppermute | solution.py:354
  43.7 1.3 %shard_map.68 = f32[256,128]{1,0:T(8,128)} custom-call(bf16[160,256]{1,0:T(8,128)(2,1)S(1)} %collective-permute-done.after_ref, bf16[160,256]{1,0:T(8,128)(2,1)S(1)} %collective-permute-done.1.before_ref, bf16[160,256]{1,0:T(8,128)(2,1)S(1)} %get-tuple-element.16.first_ref, bf16[160,256]{1,0:T(8,128)(2,1)S(1)} %get-tuple-element.17.last_ref, ...), custom_call_target="tpu_custom_call" | custom-call | tf_op jit(solution)/shard_map/pallas_call | solution.py:356
  (1 shorter events, 0.0 us)
Async XLA Ops:
  2.6 11.3 %copy-start.4 = (s32[8,8,2]{1,2,0:T(2,128)S(1)}, s32[8,8,2]{1,2,0:T(2,128)}, u32[]{:S(2)}) copy-start(s32[8,8,2]{1,2,0:T(2,128)} %param.8) | copy-start | bytes 1540
  2.6 11.4 %copy-start.1 = (s32[32,512]{1,0:T(8,128)S(1)}, s32[32,512]{1,0:T(8,128)}, u32[]{:S(2)}) copy-start(s32[32,512]{1,0:T(8,128)} %mask_ref.3) | copy-start | bytes 196612
  2.6 31.3 %copy-start = (bf16[512,256]{1,0:T(8,128)(2,1)S(1)}, bf16[512,256]{1,0:T(8,128)(2,1)}, u32[]{:S(2)}) copy-start(bf16[512,256]{1,0:T(8,128)(2,1)} %constant.8.table_ref) | copy-start | bytes 786436
  2.7 31.2 %all-to-all-start = ((bf16[64,8,640]{2,1,0:T(8,128)(2,1)}), bf16[64,8,640]{2,1,0:T(8,128)(2,1)S(1)}, u32[]{:S(2)}, u32[]{:S(2)}) async-start(bf16[64,8,640]{2,1,0:T(8,128)(2,1)} %bitcast.8), calls=%async_computation | async-start | bytes 1310720 | tf_op jit(solution)/shard_map/all_to_all | solution.py:370
  14.0 0.7 %copy-start.2 = (f32[128]{0:T(128)S(1)}, f32[128]{0:T(128)}, u32[]{:S(2)}) copy-start(f32[128]{0:T(128)} %param.9) | copy-start | bytes 1540
  14.0 0.7 %copy-start.3 = (f32[128]{0:T(128)S(1)}, f32[128]{0:T(128)}, u32[]{:S(2)}) copy-start(f32[128]{0:T(128)} %param.10) | copy-start | bytes 1540
  34.3 6.2 %collective-permute-start = (bf16[160,256]{1,0:T(8,128)(2,1)S(1)}, bf16[160,256]{1,0:T(8,128)(2,1)S(1)}, u32[]{:S(2)}, u32[]{:S(2)}) collective-permute-start(bf16[160,256]{1,0:T(8,128)(2,1)S(1)} %get-tuple-element.16.first_ref), channel_id=1, source_target_pairs={{64,0},{128,64},{192,128},{256,192},{320,256},{384,320},{448,384},... | collective-permute-start | bytes 245768 | tf_op jit(solution)/shard_map/ppermute | solution.py:353
  36.2 7.5 %collective-permute-start.1 = (bf16[160,256]{1,0:T(8,128)(2,1)S(1)}, bf16[160,256]{1,0:T(8,128)(2,1)S(1)}, u32[]{:S(2)}, u32[]{:S(2)}) collective-permute-start(bf16[160,256]{1,0:T(8,128)(2,1)S(1)} %get-tuple-element.17.last_ref), channel_id=1, source_target_pairs={{0,64},{64,128},{128,192},{192,256},{256,320},{320,384},{384,448},... | collective-permute-start | bytes 245768 | tf_op jit(solution)/shard_map/ppermute | solution.py:354

commit v6 on v5

--- a/solution.py
+++ b/solution.py
@@ -13,11 +13,12 @@
 DIST = 8
 OFFS = 8
 FLO = 48
-TILES = 64
+CHIPS = 32
 LOCAL = 8
 ROWS = 32
 COLS = 8
 WIDE = 20
+SPAN = 28
 LEAD = 6
 BLOCKS = 72
 TALL = 48
@@ -29,13 +30,25 @@
 
 
 def dft_table():
-    times = np.arange(FRAMES, dtype=np.int32)
+    times = np.arange(FRAMES, dtype=np.int32).reshape(CHIPS, 2, LOCAL)
+    times = times.transpose(1, 0, 2).reshape(FRAMES)
     freqs = FLO + np.arange(FREQ, dtype=np.int32)
     phases = times[:, None] * freqs[None, :] % FRAMES
     angles = phases.astype(np.float32) * np.float32(2.0 * math.pi / FRAMES)
     factor = np.float32(1.0 / math.sqrt(FRAMES))
     both = np.concatenate([np.cos(angles) * factor, -np.sin(angles) * factor], axis=1)
     return jnp.asarray(both.astype(np.float32)).astype(BF16)
+
+
+def exchanged(values, groups, distance):
+    upper = (groups // distance) % 2 == 1
+    result = list(values)
+    for n in range(4):
+        if (n // distance) % 2 == 0:
+            m = n + distance
+            result[n] = jnp.where(upper, pltpu.roll(values[m], 32 * distance, 1), values[n])
+            result[m] = jnp.where(upper, values[m], pltpu.roll(values[n], 128 - 32 * distance, 1))
+    return result
 
 
 def pack_kernel(
@@ -63,36 +76,32 @@
         (((1,), (1,)), ((), ())),
         preferred_element_type=F32,
     )
-    lane_group = lax.broadcasted_iota(jnp.int32, (BLOCKS, 128), 1) // 32
-    for half in range(2):
-        lanes = slice(half * 128, half * 128 + 128)
-        rolled = []
-        for c in range(COLS):
-            piece = turned[c * BLOCKS : (c + 1) * BLOCKS, lanes]
-            rolled.append([piece if n == 0 else pltpu.roll(piece, 32 * n, 1) for n in range(4)])
-        for f in range(4):
-            for part in range(2):
-                value = None
-                for g in range(4):
-                    piece = rolled[part * 4 + g][(g - f) % 4]
-                    value = piece if value is None else jnp.where(lane_group == g, piece, value)
-                at = half * 4 + f
-                (low_ref, high_ref)[part][pl.ds(at, BLOCKS, stride=LOCAL), :] = value
-    rows = TILES * LOCAL // 4
-    parts = []
-    for n in range(4):
-        here = slice(n * rows, (n + 1) * rows)
-        for at, source, start in (
-            (0, low_ref, 0),
-            (128, high_ref, 0),
-            (256, low_ref, 8),
-            (384, high_ref, 8),
-            (512, low_ref, 16),
-        ):
-            start = start + n * rows
-            laid_ref[here, at : at + 128] = source[start : start + rows, :].astype(BF16)
-        parts.append(pltpu.make_async_copy(laid_ref.at[here], out_ref.at[here], sems.at[2 + n]))
-        parts[n].start()
+    groups = lax.broadcasted_iota(jnp.int32, (BLOCKS, 128), 1) // 32
+    for part, ref in ((0, low_ref), (1, high_ref)):
+        for half in range(2):
+            lanes = slice(half * 128, half * 128 + 128)
+            values = [
+                turned[(part * 4 + g) * BLOCKS : (part * 4 + g + 1) * BLOCKS, lanes]
+                for g in range(4)
+            ]
+            values = exchanged(exchanged(values, groups, 2), groups, 1)
+            for f in range(4):
+                ref[pl.ds(half * 4 + f, BLOCKS, stride=LOCAL), :] = values[f]
+    for part, ref in ((0, low_ref), (1, high_ref)):
+        laid = ref[...].reshape(BLOCKS // 2, 2, LOCAL, 128).astype(BF16)
+        laid_ref[:, :, :, part * 128 : part * 128 + 128] = laid
+    parts = [
+        pltpu.make_async_copy(
+            laid_ref.at[start : start + CHIPS, parity, :, 0:size],
+            out_ref.at[:, :, at : at + size],
+            sems.at[n],
+        )
+        for n, (start, parity, at, size) in enumerate(
+            ((0, 0, 0, 256), (0, 1, 256, 256), (1, 0, 512, 256), (1, 1, 768, 128))
+        )
+    ]
+    for part in parts:
+        part.start()
     for part in parts:
         part.wait()
 
@@ -100,7 +109,7 @@
 def pack(frames, mask):
     return pl.pallas_call(
         pack_kernel,
-        out_shape=jax.ShapeDtypeStruct((TILES * LOCAL, WIDE * ROWS), BF16),
+        out_shape=jax.ShapeDtypeStruct((CHIPS, LOCAL, SPAN * ROWS), BF16),
         in_specs=[pl.BlockSpec(memory_space=pltpu.HBM)] * 2,
         out_specs=pl.BlockSpec(memory_space=pltpu.HBM),
         scratch_shapes=[
@@ -109,33 +118,39 @@
             pltpu.VMEM((COLS * BLOCKS, mask.shape[1]), F32),
             pltpu.VMEM((BLOCKS * LOCAL, 128), F32),
             pltpu.VMEM((BLOCKS * LOCAL, 128), F32),
-            pltpu.VMEM((TILES * LOCAL, WIDE * ROWS), BF16),
-            pltpu.SemaphoreType.DMA((6,)),
+            pltpu.VMEM((BLOCKS // 2, 2, LOCAL, 256), BF16),
+            pltpu.SemaphoreType.DMA((4,)),
         ],
         compiler_params=pltpu.CompilerParams(vmem_limit_bytes=60000000),
     )(frames, mask)
 
 
-def spectra_kernel(series_ref, table_ref, pair_ref, own_ref, first_ref, last_ref):
-    spectrum = lax.dot_general(
-        series_ref[...],
-        table_ref[...],
-        (((0,), (0,)), ((), ())),
-        preferred_element_type=F32,
-    )
+def spectra_kernel(mine_ref, other_ref, table_ref, own_ref, first_ref, last_ref):
+    core = lax.axis_index("tile") % 2
+    count = FRAMES // 2
+    lanes = pl.ds(pl.multiple_of(core * COLS * ROWS, 128), WIDE * ROWS)
+    spectrum = None
+    for ref, at in ((mine_ref, core), (other_ref, 1 - core)):
+        part = lax.dot_general(
+            ref[:, :, lanes].reshape(count, WIDE * ROWS),
+            table_ref[pl.ds(pl.multiple_of(at * count, count), count), :],
+            (((0,), (0,)), ((), ())),
+            preferred_element_type=F32,
+        )
+        spectrum = part if spectrum is None else spectrum + part
     own_ref[...] = spectrum.astype(BF16)
     by_column = spectrum.reshape(WIDE, ROWS, 2 * FREQ)
     first_ref[...] = by_column[:, :8].reshape(WIDE * 8, 2 * FREQ).astype(BF16)
     last_ref[...] = by_column[:, ROWS - 8 :].reshape(WIDE * 8, 2 * FREQ).astype(BF16)
 
 
-def spectra(series, table, pair):
+def spectra(mine, other, table):
     edge = jax.ShapeDtypeStruct((WIDE * 8, 2 * FREQ), BF16)
     return pl.pallas_call(
         spectra_kernel,
         out_shape=(jax.ShapeDtypeStruct((WIDE * ROWS, 2 * FREQ), BF16), edge, edge),
         compiler_params=pltpu.CompilerParams(vmem_limit_bytes=32 * 1024 * 1024),
-    )(series, table, pair)
+    )(mine, other, table)
 
 
 def select_kernel(offsets_ref, mask_ref, gain_ref, mix_ref, pick_ref, weight_ref, share_ref, pair_ref):
@@ -366,14 +381,22 @@
 
 
 def on_device(frames, disk_mask, offsets, filter_gain, filter_mix):
-    packed = pack(frames, disk_mask).reshape(TILES, LOCAL, WIDE * ROWS)
-    received = lax.all_to_all(packed, "tile", split_axis=0, concat_axis=0, tiled=True)
+    same_core = [[2 * chip + core for chip in range(CHIPS)] for core in range(2)]
+    mine = lax.all_to_all(
+        pack(frames, disk_mask),
+        "tile",
+        split_axis=0,
+        concat_axis=0,
+        axis_index_groups=same_core,
+        tiled=True,
+    )
     steps = ((offsets[..., 1] + 4) * 16 + offsets[..., 0] + 4).reshape(DIST * OFFS)
     gain = filter_gain.reshape(1, FREQ)
     mix = filter_mix.reshape(1, FREQ)
     chosen = select(steps, disk_mask, gain, mix)
-    series = received.reshape(FRAMES, WIDE * ROWS)
-    own, first, last = spectra(series, dft_table(), chosen[-1])
+    mine, chosen = lax.optimization_barrier((mine, chosen))
+    other = lax.ppermute(mine, "tile", [(i, i ^ 1) for i in range(2 * CHIPS)])
+    own, first, last = spectra(mine, other, dft_table())
     out = outer(first, last, chosen, middle(own, chosen))
     return out.reshape(8, 2, DIST, 2, FREQ)
 

time: 45.2 us -> 44.2 us (0.978)
  the two profiles are of different devices: /device:TPU:263 before, /device:TPU:200 now
where the time goes in v6:
time: 44.2 us; the launch traced here: 43.9 us
  starting transfers between devices  19.6 us (44%)
  waiting for transfers between devices  17.3 us (39%)
  Pallas kernels  6.11 us (14%)
  local copies, waits for them, and re-layouts  0.76 us (2%)
    all_to_all x1, waiting for transfers between devices, on_device(): lax.all_to_all(pack(frames, disk_mask), 'tile', split_axis=0, concat_axis...  14.2 us
    all_to_all x1, starting transfers between devices, on_device(): lax.all_to_all(pack(frames, disk_mask), 'tile', split_axis=0, concat_axis...  10.3 us
    ppermute x1, starting transfers between devices, outer(): before = lax.ppermute(last, 'band', up)  5.49 us
    pallas_call x1, Pallas kernels, pack(): pl.pallas_call(pack_kernel, out_shape=jax.ShapeDtypeStruct((CHIPS, LOCAL,...  2.45 us
    ppermute x1, starting transfers between devices, outer(): after = lax.ppermute(first, 'band', down)  1.92 us
    ppermute x1, starting transfers between devices, on_device(): other = lax.ppermute(mine, 'tile', [(i, i ^ 1) for i in range(2 * CHIPS)])  1.91 us
    ppermute x1, waiting for transfers between devices, on_device(): other = lax.ppermute(mine, 'tile', [(i, i ^ 1) for i in range(2 * CHIPS)])  1.78 us
    pallas_call x1, Pallas kernels, outer(): pl.pallas_call(outer_kernel, out_shape=float_shape(8 * 2 * DIST * 2), in_...  1.31 us
  transfers between devices with their start and end apart: 4, of which 4 were waited for; matrix products, arithmetic and copies ran while one was open for 0% of the time, Pallas kernels for 4%

profile of v6, /device:TPU:200, one launch (start us, length us, event | category | flops | bytes accessed | tf_op | source)
XLA Modules:
  0.0 43.9 jit_solution(12614251693208721190)
XLA Ops:
  0.0 2.4 %shard_map.64 = bf16[32,8,896]{2,1,0:T(8,128)(2,1)} custom-call(bf16[8,32,512]{2,1,0:T(8,128)(2,1)} %frames_ref.1, s32[32,512]{1,0:T(8,128)} %mask_ref.3), custom_call_target="tpu_custom_call" | custom-call | tf_op jit(solution)/shard_map/pallas_call | solution.py:110
  2.5 0.0 copy-start.4
  2.5 0.0 copy-start
  2.5 0.0 copy-start.1
  2.5 10.3 %all-to-all-start = ((bf16[32,8,896]{2,1,0:T(8,128)(2,1)}), bf16[32,8,896]{2,1,0:T(8,128)(2,1)S(1)}, u32[]{:S(2)}, u32[]{:S(2)}) async-start(bf16[32,8,896]{2,1,0:T(8,128)(2,1)} %shard_map.64), calls=%async_computation | async-start | bytes 917504 | tf_op jit(solution)/shard_map/all_to_all | solution.py:385
  12.8 0.0 copy-done.4
  12.8 0.1 add.20.offsets_ref
  12.9 0.0 copy-start.2
  12.9 0.0 copy-start.3
  12.9 0.0 copy-done
  12.9 0.6 %copy-done.2 = f32[128]{0:T(128)S(1)} copy-done((f32[128]{0:T(128)S(1)}, f32[128]{0:T(128)}, u32[]{:S(2)}) %copy-start.2) | copy-done | bytes 536
  13.6 0.0 copy-done.3
  13.6 1.2 %shard_map.65 = (bf16[512,512]{1,0:T(8,128)(2,1)S(1)}, f32[256,128]{1,0:T(8,128)S(1)}, f32[16,128]{1,0:T(8,128)S(1)}, f32[8,128]{1,0:T(8,128)S(1)}) custom-call(s32[64]{0:T(128)S(1)} %add.20.offsets_ref, s32[32,512]{1,0:T(8,128)S(1)} %copy-done, f32[1,128]{1,0:T(1,128)S(1)} %bitcast.3, f32[1,128]{1,0:T(1,128)S(1)} %bitcast.4), custom_call_target="tpu_custom_call" | custom-call | flops 4000000 | bytes 4000000 | tf_op jit(solution)/shard_map/pallas_call | solution.py:339
  14.8 14.2 %all-to-all-done.mine_ref = bf16[32,8,896]{2,1,0:T(8,128)(2,1)S(1)} async-done(((bf16[32,8,896]{2,1,0:T(8,128)(2,1)}), bf16[32,8,896]{2,1,0:T(8,128)(2,1)S(1)}, u32[]{:S(2)}, u32[]{:S(2)}) %all-to-all-start) | async-done | bytes 458784 | tf_op jit(solution)/shard_map/all_to_all | solution.py:385
  29.0 1.9 %collective-permute-start = (bf16[32,8,896]{2,1,0:T(8,128)(2,1)S(1)}, bf16[32,8,896]{2,1,0:T(8,128)(2,1)S(1)}, u32[]{:S(2)}, u32[]{:S(2)}) collective-permute-start(bf16[32,8,896]{2,1,0:T(8,128)(2,1)S(1)} %all-to-all-done.mine_ref), channel_id=1, source_target_pairs={{0,1},{1,0},{2,3},{3,2},{4,5},{5,4},{6,7},{7,6},{8,9},{9,8},{10,11... | collective-permute-start | bytes 1376264 | tf_op jit(solution)/shard_map/ppermute | solution.py:398
  30.9 1.8 %collective-permute-done.other_ref = bf16[32,8,896]{2,1,0:T(8,128)(2,1)S(1)} collective-permute-done((bf16[32,8,896]{2,1,0:T(8,128)(2,1)S(1)}, bf16[32,8,896]{2,1,0:T(8,128)(2,1)S(1)}, u32[]{:S(2)}, u32[]{:S(2)}) %collective-permute-start) | collective-permute-done | bytes 458784 | tf_op jit(solution)/shard_map/ppermute | solution.py:398
  32.7 0.0 copy-done.1
  32.7 0.4 shard_map.66
  33.1 1.9 %collective-permute-start.1 = (bf16[160,256]{1,0:T(8,128)(2,1)S(1)}, bf16[160,256]{1,0:T(8,128)(2,1)S(1)}, u32[]{:S(2)}, u32[]{:S(2)}) collective-permute-start(bf16[160,256]{1,0:T(8,128)(2,1)S(1)} %get-tuple-element.25.first_ref), channel_id=1, source_target_pairs={{64,0},{128,64},{192,128},{256,192},{320,256},{384,320},{448,384},... | collective-permute-start | bytes 245768 | tf_op jit(solution)/shard_map/ppermute | solution.py:368
  35.0 5.5 %collective-permute-start.2 = (bf16[160,256]{1,0:T(8,128)(2,1)S(1)}, bf16[160,256]{1,0:T(8,128)(2,1)S(1)}, u32[]{:S(2)}, u32[]{:S(2)}) collective-permute-start(bf16[160,256]{1,0:T(8,128)(2,1)S(1)} %get-tuple-element.26.last_ref), channel_id=1, source_target_pairs={{0,64},{64,128},{128,192},{192,256},{256,320},{320,384},{384,448},... | collective-permute-start | bytes 245768 | tf_op jit(solution)/shard_map/ppermute | solution.py:369
  40.5 0.7 %shard_map.67 = (f32[128,128]{1,0:T(8,128)S(1)}, f32[640,128]{1,0:T(8,128)S(1)}, f32[640,128]{1,0:T(8,128)S(1)}) custom-call(bf16[640,256]{1,0:T(8,128)(2,1)S(1)} %get-tuple-element.31.own_ref, bf16[512,512]{1,0:T(8,128)(2,1)S(1)} %get-tuple-element.27.pick_ref, f32[256,128]{1,0:T(8,128)S(1)} %get-tuple-element.28.weight_ref, ...), custom_call_target="tpu_custom_call" | custom-call | flops 6000000 | bytes 4000000 | tf_op jit(solution)/shard_map/pallas_call | solution.py:354
  41.3 0.1 collective-permute-done.1.after_ref
  41.3 1.2 %collective-permute-done.2.before_ref = bf16[160,256]{1,0:T(8,128)(2,1)S(1)} collective-permute-done((bf16[160,256]{1,0:T(8,128)(2,1)S(1)}, bf16[160,256]{1,0:T(8,128)(2,1)S(1)}, u32[]{:S(2)}, u32[]{:S(2)}) %collective-permute-start.2) | collective-permute-done | bytes 81952 | tf_op jit(solution)/shard_map/ppermute | solution.py:369
  42.6 1.3 %shard_map.68 = f32[256,128]{1,0:T(8,128)} custom-call(bf16[160,256]{1,0:T(8,128)(2,1)S(1)} %collective-permute-done.1.after_ref, bf16[160,256]{1,0:T(8,128)(2,1)S(1)} %collective-permute-done.2.before_ref, bf16[160,256]{1,0:T(8,128)(2,1)S(1)} %get-tuple-element.25.first_ref, bf16[160,256]{1,0:T(8,128)(2,1)S(1)} %get-tuple-element.26.last_ref, ...), custom_call_target="tpu_custom_call" | custom-call | tf_op jit(solution)/shard_map/pallas_call | solution.py:371
  (1 shorter events, 0.0 us)
Async XLA Ops:
  2.5 10.4 %copy-start.4 = (s32[8,8,2]{1,2,0:T(2,128)S(1)}, s32[8,8,2]{1,2,0:T(2,128)}, u32[]{:S(2)}) copy-start(s32[8,8,2]{1,2,0:T(2,128)} %param.8) | copy-start | bytes 1540
  2.5 10.5 %copy-start = (s32[32,512]{1,0:T(8,128)S(1)}, s32[32,512]{1,0:T(8,128)}, u32[]{:S(2)}) copy-start(s32[32,512]{1,0:T(8,128)} %mask_ref.3) | copy-start | bytes 196612
  2.5 30.2 %copy-start.1 = (bf16[512,256]{1,0:T(8,128)(2,1)S(1)}, bf16[512,256]{1,0:T(8,128)(2,1)}, u32[]{:S(2)}) copy-start(bf16[512,256]{1,0:T(8,128)(2,1)} %constant.8.table_ref) | copy-start | bytes 786436
  2.5 26.5 %all-to-all-start = ((bf16[32,8,896]{2,1,0:T(8,128)(2,1)}), bf16[32,8,896]{2,1,0:T(8,128)(2,1)S(1)}, u32[]{:S(2)}, u32[]{:S(2)}) async-start(bf16[32,8,896]{2,1,0:T(8,128)(2,1)} %shard_map.64), calls=%async_computation | async-start | bytes 917504 | tf_op jit(solution)/shard_map/all_to_all | solution.py:385
  12.9 0.7 %copy-start.2 = (f32[128]{0:T(128)S(1)}, f32[128]{0:T(128)}, u32[]{:S(2)}) copy-start(f32[128]{0:T(128)} %param.9) | copy-start | bytes 1540
  12.9 0.7 %copy-start.3 = (f32[128]{0:T(128)S(1)}, f32[128]{0:T(128)}, u32[]{:S(2)}) copy-start(f32[128]{0:T(128)} %param.10) | copy-start | bytes 1540
  29.0 3.7 %collective-permute-start = (bf16[32,8,896]{2,1,0:T(8,128)(2,1)S(1)}, bf16[32,8,896]{2,1,0:T(8,128)(2,1)S(1)}, u32[]{:S(2)}, u32[]{:S(2)}) collective-permute-start(bf16[32,8,896]{2,1,0:T(8,128)(2,1)S(1)} %all-to-all-done.mine_ref), channel_id=1, source_target_pairs={{0,1},{1,0},{2,3},{3,2},{4,5},{5,4},{6,7},{7,6},{8,9},{9,8},{10,11... | collective-permute-start | bytes 1376264 | tf_op jit(solution)/shard_map/ppermute | solution.py:398
  33.1 8.2 %collective-permute-start.1 = (bf16[160,256]{1,0:T(8,128)(2,1)S(1)}, bf16[160,256]{1,0:T(8,128)(2,1)S(1)}, u32[]{:S(2)}, u32[]{:S(2)}) collective-permute-start(bf16[160,256]{1,0:T(8,128)(2,1)S(1)} %get-tuple-element.25.first_ref), channel_id=1, source_target_pairs={{64,0},{128,64},{192,128},{256,192},{320,256},{384,320},{448,384},... | collective-permute-start | bytes 245768 | tf_op jit(solution)/shard_map/ppermute | solution.py:368
  35.0 7.5 %collective-permute-start.2 = (bf16[160,256]{1,0:T(8,128)(2,1)S(1)}, bf16[160,256]{1,0:T(8,128)(2,1)S(1)}, u32[]{:S(2)}, u32[]{:S(2)}) collective-permute-start(bf16[160,256]{1,0:T(8,128)(2,1)S(1)} %get-tuple-element.26.last_ref), channel_id=1, source_target_pairs={{0,64},{64,128},{128,192},{192,256},{256,320},{320,384},{384,448},... | collective-permute-start | bytes 245768 | tf_op jit(solution)/shard_map/ppermute | solution.py:369

commit v7 on v6

--- a/solution.py
+++ b/solution.py
@@ -20,6 +20,7 @@
 WIDE = 20
 SPAN = 28
 LEAD = 6
+QUADS = (0, 16, 8, 24, 32, 48, 40)
 BLOCKS = 72
 TALL = 48
 REACH = 40
@@ -52,7 +53,7 @@
 
 
 def pack_kernel(
-    frames_ref, mask_ref, out_ref, frames_vmem, mask_vmem, pick_ref, low_ref, high_ref, laid_ref, sems
+    frames_ref, mask_ref, out_ref, frames_vmem, mask_vmem, pick_ref, low_ref, high_ref, sems
 ):
     copies = [
         pltpu.make_async_copy(mask_ref, mask_vmem, sems.at[0]),
@@ -87,39 +88,26 @@
             values = exchanged(exchanged(values, groups, 2), groups, 1)
             for f in range(4):
                 ref[pl.ds(half * 4 + f, BLOCKS, stride=LOCAL), :] = values[f]
-    for part, ref in ((0, low_ref), (1, high_ref)):
-        laid = ref[...].reshape(BLOCKS // 2, 2, LOCAL, 128).astype(BF16)
-        laid_ref[:, :, :, part * 128 : part * 128 + 128] = laid
-    parts = [
-        pltpu.make_async_copy(
-            laid_ref.at[start : start + CHIPS, parity, :, 0:size],
-            out_ref.at[:, :, at : at + size],
-            sems.at[n],
-        )
-        for n, (start, parity, at, size) in enumerate(
-            ((0, 0, 0, 256), (0, 1, 256, 256), (1, 0, 512, 256), (1, 1, 768, 128))
-        )
-    ]
-    for part in parts:
-        part.start()
-    for part in parts:
-        part.wait()
+    count = CHIPS * 16
+    for at, ref, start in ((0, low_ref, 0), (16, high_ref, 0), (32, low_ref, 16)):
+        laid = ref[start : start + count, :].reshape(CHIPS, 16, 128)
+        out_ref[:, at : at + 16, :] = laid.astype(BF16)
+    laid = high_ref[16 : 16 + count, :].reshape(CHIPS, 16, 128)
+    out_ref[:, 48:56, :] = laid[:, 0:8, :].astype(BF16)
 
 
 def pack(frames, mask):
     return pl.pallas_call(
         pack_kernel,
-        out_shape=jax.ShapeDtypeStruct((CHIPS, LOCAL, SPAN * ROWS), BF16),
+        out_shape=pltpu.VMEM((CHIPS, 2 * SPAN, 128), BF16),
         in_specs=[pl.BlockSpec(memory_space=pltpu.HBM)] * 2,
-        out_specs=pl.BlockSpec(memory_space=pltpu.HBM),
         scratch_shapes=[
             pltpu.VMEM(frames.shape, BF16),
             pltpu.VMEM(mask.shape, jnp.int32),
             pltpu.VMEM((COLS * BLOCKS, mask.shape[1]), F32),
             pltpu.VMEM((BLOCKS * LOCAL, 128), F32),
             pltpu.VMEM((BLOCKS * LOCAL, 128), F32),
-            pltpu.VMEM((BLOCKS // 2, 2, LOCAL, 256), BF16),
-            pltpu.SemaphoreType.DMA((4,)),
+            pltpu.SemaphoreType.DMA((2,)),
         ],
         compiler_params=pltpu.CompilerParams(vmem_limit_bytes=60000000),
     )(frames, mask)
@@ -128,11 +116,12 @@
 def spectra_kernel(mine_ref, other_ref, table_ref, own_ref, first_ref, last_ref):
     core = lax.axis_index("tile") % 2
     count = FRAMES // 2
-    lanes = pl.ds(pl.multiple_of(core * COLS * ROWS, 128), WIDE * ROWS)
     spectrum = None
     for ref, at in ((mine_ref, core), (other_ref, 1 - core)):
+        quads = [ref[:, row : row + 8, :].reshape(count, 128) for row in QUADS]
+        series = [jnp.where(core == 0, quads[n], quads[n + 2]) for n in range(5)]
         part = lax.dot_general(
-            ref[:, :, lanes].reshape(count, WIDE * ROWS),
+            jnp.concatenate(series, axis=1),
             table_ref[pl.ds(pl.multiple_of(at * count, count), count), :],
             (((0,), (0,)), ((), ())),
             preferred_element_type=F32,
@@ -153,7 +142,7 @@
     )(mine, other, table)
 
 
-def select_kernel(offsets_ref, mask_ref, gain_ref, mix_ref, pick_ref, weight_ref, share_ref, pair_ref):
+def select_kernel(offsets_ref, mask_ref, pick_ref, weight_ref, share_ref):
     shape = (COLS * 8, SIDE * 16)
     pixel = lax.broadcasted_iota(jnp.int32, shape, 0)
     lane = lax.broadcasted_iota(jnp.int32, shape, 1)
@@ -187,8 +176,6 @@
             for k in range(1, 4):
                 count = count + total[block * 4 + k : block * 4 + k + 1]
             share_ref[block * 2 + part : block * 2 + part + 1, :] = 1.0 / jnp.maximum(count, 1.0)
-    pair_ref[0:1, :] = gain_ref[...]
-    pair_ref[1:2, :] = mix_ref[...]
 
 
 def filtered(tall, rim, at, rows, gain, mix):
@@ -248,12 +235,26 @@
 
 
 def middle_kernel(
-    own_ref, pick_ref, weight_ref, share_ref, pair_ref, out_ref, filt_re, filt_im, own_re, own_im, *scratch
+    own_ref,
+    gain_ref,
+    mix_ref,
+    pick_ref,
+    weight_ref,
+    share_ref,
+    out_ref,
+    filt_re,
+    filt_im,
+    pair_ref,
+    own_re,
+    own_im,
+    *scratch,
 ):
     own_re[...] = own_ref[:, :FREQ].astype(F32)
     own_im[...] = own_ref[:, FREQ:].astype(F32)
-    gain = pair_ref[0:1, :]
-    mix = pair_ref[1:2, :]
+    gain = gain_ref[...]
+    mix = mix_ref[...]
+    pair_ref[0:1, :] = gain
+    pair_ref[1:2, :] = mix
     for source, filt in ((own_re, filt_re), (own_im, filt_im)):
         for q in range(SIDE):
             value = filtered(source, ROWS, (q + 2) * ROWS + 1, ROWS - 2, gain, mix)
@@ -264,56 +265,82 @@
         )
 
 
-def outer_kernel(
-    after_ref,
+def edge_blocks(
+    group, upper_ref, lower_ref, pick_ref, weight_ref, share_ref, own_re, own_im, pair_ref, out_ref, scratch
+):
+    tall_re, tall_im, filt_re, filt_im, *scratch = scratch
+    for ref, at in ((upper_ref, 0), (lower_ref, 8)):
+        value = ref[...].astype(F32).reshape(WIDE, 8, 2 * FREQ)
+        for q in range(WIDE):
+            tall_re[at + q * 16 : at + q * 16 + 8, :] = value[q, :, :FREQ]
+            tall_im[at + q * 16 : at + q * 16 + 8, :] = value[q, :, FREQ:]
+    gain = pair_ref[0:1, :]
+    mix = pair_ref[1:2, :]
+    edge, kept = (0, 8) if group == 0 else (32, 24)
+    for tall, inside, filt in ((tall_re, own_re, filt_re), (tall_im, own_im, filt_im)):
+        for q in range(SIDE):
+            at = q * REACH
+            value = filtered(tall, 16, (q + 2) * 16 + 4, 8, gain, mix)
+            filt[at + edge : at + edge + 8, :] = value
+            filt[at + kept : at + kept + 8, :] = inside[at + kept : at + kept + 8, :]
+    group_blocks(group, pick_ref, filt_re, filt_im, weight_ref, share_ref, out_ref, 0, scratch)
+
+
+def bottom_kernel(
+    last_ref, after_ref, pick_ref, weight_ref, share_ref, own_re, own_im, pair_ref, out_ref, *scratch
+):
+    edge_blocks(
+        3,
+        last_ref,
+        after_ref,
+        pick_ref,
+        weight_ref,
+        share_ref,
+        own_re,
+        own_im,
+        pair_ref,
+        out_ref,
+        scratch,
+    )
+
+
+def top_kernel(
     before_ref,
     first_ref,
-    last_ref,
     pick_ref,
     weight_ref,
     share_ref,
+    own_re,
+    own_im,
     pair_ref,
     mid_ref,
-    own_filt_re,
-    own_filt_im,
+    bottom_ref,
     out_ref,
-    tall_re,
-    tall_im,
-    filt_re,
-    filt_im,
     result,
     sems,
     *scratch,
 ):
     copies = [
         pltpu.make_async_copy(mid_ref, out_ref.at[64:192], sems.at[0]),
-        pltpu.make_async_copy(result.at[0:64], out_ref.at[0:64], sems.at[1]),
-        pltpu.make_async_copy(result.at[64:128], out_ref.at[192:256], sems.at[2]),
+        pltpu.make_async_copy(bottom_ref, out_ref.at[192:256], sems.at[1]),
+        pltpu.make_async_copy(result, out_ref.at[0:64], sems.at[2]),
     ]
     copies[0].start()
-    half = WIDE * 16
-    for ref, at in ((before_ref, 0), (first_ref, 8), (last_ref, half), (after_ref, half + 8)):
-        value = ref[...].astype(F32).reshape(WIDE, 8, 2 * FREQ)
-        for q in range(WIDE):
-            tall_re[at + q * 16 : at + q * 16 + 8, :] = value[q, :, :FREQ]
-            tall_im[at + q * 16 : at + q * 16 + 8, :] = value[q, :, FREQ:]
-    gain = pair_ref[0:1, :]
-    mix = pair_ref[1:2, :]
-    for n, group in enumerate((0, 3)):
-        edge, kept = ((0, 8), (32, 24))[n]
-        for tall, inside, filt in (
-            (tall_re, own_filt_re, filt_re),
-            (tall_im, own_filt_im, filt_im),
-        ):
-            for q in range(SIDE):
-                at = q * REACH
-                value = filtered(tall, 16, n * half + (q + 2) * 16 + 4, 8, gain, mix)
-                filt[at + edge : at + edge + 8, :] = value
-                filt[at + kept : at + kept + 8, :] = inside[at + kept : at + kept + 8, :]
-        group_blocks(
-            group, pick_ref, filt_re, filt_im, weight_ref, share_ref, result, n * 64, scratch
-        )
-        copies[1 + n].start()
+    copies[1].start()
+    edge_blocks(
+        0,
+        before_ref,
+        first_ref,
+        pick_ref,
+        weight_ref,
+        share_ref,
+        own_re,
+        own_im,
+        pair_ref,
+        result,
+        scratch,
+    )
+    copies[2].start()
     for copy in copies:
         copy.wait()
 
@@ -335,30 +362,29 @@
     return pltpu.CompilerParams(vmem_limit_bytes=32 * 1024 * 1024)
 
 
-def select(steps, mask, gain, mix):
+def select(steps, mask):
     return pl.pallas_call(
         select_kernel,
         out_shape=(
             jax.ShapeDtypeStruct((DIST * COLS * 8, 2 * SIDE * 16), BF16),
             float_shape(COLS * ROWS),
             float_shape(16),
-            float_shape(8),
         ),
-        in_specs=[SMEM] + [VMEM] * 3,
+        in_specs=[SMEM, VMEM],
         compiler_params=params(),
         cost_estimate=pl.CostEstimate(flops=4_000_000, bytes_accessed=4_000_000, transcendentals=0),
-    )(steps, mask, gain, mix)
-
-
-def middle(own, chosen):
+    )(steps, mask)
+
+
+def middle(own, gain, mix, chosen):
     return pl.pallas_call(
         middle_kernel,
-        out_shape=(float_shape(128), float_shape(SIDE * REACH), float_shape(SIDE * REACH)),
-        in_specs=[VMEM] * 5,
+        out_shape=tuple(float_shape(n) for n in (128, SIDE * REACH, SIDE * REACH, 8)),
+        in_specs=[VMEM] * 6,
         scratch_shapes=[pltpu.VMEM((WIDE * ROWS, FREQ), F32)] * 2 + GROUP_SCRATCH,
         compiler_params=params(),
         cost_estimate=pl.CostEstimate(flops=6_000_000, bytes_accessed=4_000_000, transcendentals=0),
-    )(own, *chosen)
+    )(own, gain, mix, *chosen)
 
 
 def outer(first, last, chosen, kept):
@@ -367,17 +393,27 @@
     down = [(j, i) for i, j in up]
     after = lax.ppermute(first, "band", down)
     before = lax.ppermute(last, "band", up)
-    rows = [WIDE * 32] * 2 + [SIDE * REACH] * 2 + [128]
+    mid, *shared = kept
+    rows = [WIDE * 16] * 2 + [SIDE * REACH] * 2
+    scratch = [pltpu.VMEM((n, FREQ), F32) for n in rows] + GROUP_SCRATCH
+    cost = pl.CostEstimate(flops=3_000_000, bytes_accessed=3_000_000, transcendentals=0)
+    bottom = pl.pallas_call(
+        bottom_kernel,
+        out_shape=float_shape(64),
+        in_specs=[VMEM] * 8,
+        scratch_shapes=scratch,
+        compiler_params=params(),
+        cost_estimate=cost,
+    )(last, after, *chosen, *shared)
     return pl.pallas_call(
-        outer_kernel,
+        top_kernel,
         out_shape=float_shape(8 * 2 * DIST * 2),
-        in_specs=[VMEM] * 11,
+        in_specs=[VMEM] * 10,
         out_specs=pl.BlockSpec(memory_space=pltpu.HBM),
-        scratch_shapes=[pltpu.VMEM((n, FREQ), F32) for n in rows]
-        + [pltpu.SemaphoreType.DMA((3,))]
-        + GROUP_SCRATCH,
+        scratch_shapes=[pltpu.VMEM((64, FREQ), F32), pltpu.SemaphoreType.DMA((3,))] + scratch,
         compiler_params=params(),
-    )(after, before, first, last, *chosen, *kept)
+        cost_estimate=cost,
+    )(before, first, *chosen, *shared, mid, bottom)
 
 
 def on_device(frames, disk_mask, offsets, filter_gain, filter_mix):
@@ -393,11 +429,11 @@
     steps = ((offsets[..., 1] + 4) * 16 + offsets[..., 0] + 4).reshape(DIST * OFFS)
     gain = filter_gain.reshape(1, FREQ)
     mix = filter_mix.reshape(1, FREQ)
-    chosen = select(steps, disk_mask, gain, mix)
-    mine, chosen = lax.optimization_barrier((mine, chosen))
+    chosen = select(steps, disk_mask)
     other = lax.ppermute(mine, "tile", [(i, i ^ 1) for i in range(2 * CHIPS)])
+    other, chosen = lax.optimization_barrier((other, chosen))
     own, first, last = spectra(mine, other, dft_table())
-    out = outer(first, last, chosen, middle(own, chosen))
+    out = outer(first, last, chosen, middle(own, gain, mix, chosen))
     return out.reshape(8, 2, DIST, 2, FREQ)
 
 

time: 44.2 us -> 42.9 us (0.971)
  the two profiles are of different devices: /device:TPU:200 before, /device:TPU:264 now
where the time goes in v7:
time: 42.9 us; the launch traced here: 42.7 us
  blocking collectives  26.3 us (61%)
  starting transfers between devices  7.75 us (18%)
  Pallas kernels  5.48 us (13%)
  waiting for transfers between devices  2.23 us (5%)
  local copies, waits for them, and re-layouts  0.76 us (2%)
    all_to_all x1, blocking collectives, on_device(): lax.all_to_all(pack(frames, disk_mask), 'tile', split_axis=0, concat_axis...  26.3 us
    ppermute x1, starting transfers between devices, outer(): before = lax.ppermute(last, 'band', up)  3.92 us
    ppermute x1, starting transfers between devices, outer(): after = lax.ppermute(first, 'band', down)  1.92 us
    ppermute x1, starting transfers between devices, on_device(): other = lax.ppermute(mine, 'tile', [(i, i ^ 1) for i in range(2 * CHIPS)])  1.91 us
    ppermute x1, waiting for transfers between devices, outer(): before = lax.ppermute(last, 'band', up)  1.8 us
    pallas_call x1, Pallas kernels, pack(): pl.pallas_call(pack_kernel, out_shape=pltpu.VMEM((CHIPS, 2 * SPAN, 128),...  1.63 us
    pallas_call x1, Pallas kernels, select(): pl.pallas_call(select_kernel, out_shape=(jax.ShapeDtypeStruct((DIST * COL...  1.22 us
    pallas_call x1, Pallas kernels, outer(): pl.pallas_call(top_kernel, out_shape=float_shape(8 * 2 * DIST * 2), in_sp...  1.06 us
  transfers between devices with their start and end apart: 3, of which 2 were waited for; matrix products, arithmetic and copies ran while one was open for 0% of the time, Pallas kernels for 6%

profile of v7, /device:TPU:264, one launch (start us, length us, event | category | flops | bytes accessed | tf_op | source)
XLA Modules:
  0.0 42.7 jit_solution(3988462449503442183)
XLA Ops:
  0.0 1.6 %shard_map.64 = bf16[32,56,128]{2,1,0:T(8,128)(2,1)S(1)} custom-call(bf16[8,32,512]{2,1,0:T(8,128)(2,1)} %frames_ref.1, s32[32,512]{1,0:T(8,128)} %mask_ref.3), custom_call_target="tpu_custom_call" | custom-call | tf_op jit(solution)/shard_map/pallas_call | solution.py:100
  1.6 0.0 copy-start.4
  1.6 0.0 copy-start
  1.7 0.0 copy-start.1
  1.7 26.3 %all_to_all.5.mine_ref = bf16[32,56,128]{2,1,0:T(8,128)(2,1)S(1)} all-to-all(bf16[32,56,128]{2,1,0:T(8,128)(2,1)S(1)} %shard_map.64), channel_id=1, replica_groups={{0,2,4,6,8,10,12,14,16,18,20,22,24,26,28,30,32,34,36,38,40,42,44,46,48,..., dimensions={0} | all-to-all | bytes 917504 | tf_op jit(solution)/shard_map/all_to_all | solution.py:421
  28.0 1.9 %collective-permute-start = (bf16[32,56,128]{2,1,0:T(8,128)(2,1)S(1)}, bf16[32,56,128]{2,1,0:T(8,128)(2,1)S(1)}, u32[]{:S(2)}, u32[]{:S(2)}) collective-permute-start(bf16[32,56,128]{2,1,0:T(8,128)(2,1)S(1)} %all_to_all.5.mine_ref), channel_id=1, source_target_pairs={{0,1},{1,0},{2,3},{3,2},{4,5},{5,4},{6,7},{7,6},{8,9},{9,8},{10,11... | collective-permute-start | bytes 1376264 | tf_op jit(solution)/shard_map/ppermute | solution.py:433
  29.9 0.0 copy-done.4
  29.9 0.1 add.20.offsets_ref
  30.0 0.0 copy-done
  30.0 1.2 %shard_map.65 = (bf16[512,512]{1,0:T(8,128)(2,1)S(1)}, f32[256,128]{1,0:T(8,128)S(1)}, f32[16,128]{1,0:T(8,128)S(1)}) custom-call(s32[64]{0:T(128)S(1)} %add.20.offsets_ref, s32[32,512]{1,0:T(8,128)S(1)} %copy-done), custom_call_target="tpu_custom_call" | custom-call | flops 4000000 | bytes 4000000 | tf_op jit(solution)/shard_map/pallas_call | solution.py:366
  31.2 0.4 %collective-permute-done.other_ref = bf16[32,56,128]{2,1,0:T(8,128)(2,1)S(1)} collective-permute-done((bf16[32,56,128]{2,1,0:T(8,128)(2,1)S(1)}, bf16[32,56,128]{2,1,0:T(8,128)(2,1)S(1)}, u32[]{:S(2)}, u32[]{:S(2)}) %collective-permute-start) | collective-permute-done | bytes 458784 | tf_op jit(solution)/shard_map/ppermute | solution.py:433
  31.7 0.0 copy-done.1
  31.7 0.4 shard_map.66
  32.1 1.9 %collective-permute-start.2 = (bf16[160,256]{1,0:T(8,128)(2,1)S(1)}, bf16[160,256]{1,0:T(8,128)(2,1)S(1)}, u32[]{:S(2)}, u32[]{:S(2)}) collective-permute-start(bf16[160,256]{1,0:T(8,128)(2,1)S(1)} %get-tuple-element.24.first_ref), channel_id=1, source_target_pairs={{64,0},{128,64},{192,128},{256,192},{320,256},{384,320},{448,384},... | collective-permute-start | bytes 245768 | tf_op jit(solution)/shard_map/ppermute | solution.py:394
  34.0 3.9 %collective-permute-start.1 = (bf16[160,256]{1,0:T(8,128)(2,1)S(1)}, bf16[160,256]{1,0:T(8,128)(2,1)S(1)}, u32[]{:S(2)}, u32[]{:S(2)}) collective-permute-start(bf16[160,256]{1,0:T(8,128)(2,1)S(1)} %get-tuple-element.23.last_ref), channel_id=1, source_target_pairs={{0,64},{64,128},{128,192},{192,256},{256,320},{320,384},{384,448},... | collective-permute-start | bytes 245768 | tf_op jit(solution)/shard_map/ppermute | solution.py:395
  37.9 0.0 copy-start.2
  37.9 0.0 copy-start.3
  38.0 0.6 %copy-done.2 = f32[128]{0:T(128)S(1)} copy-done((f32[128]{0:T(128)S(1)}, f32[128]{0:T(128)}, u32[]{:S(2)}) %copy-start.2) | copy-done | bytes 536
  38.6 0.0 copy-done.3
  38.6 0.7 %shard_map.67 = (f32[128,128]{1,0:T(8,128)S(1)}, f32[640,128]{1,0:T(8,128)S(1)}, f32[640,128]{1,0:T(8,128)S(1)}, f32[8,128]{1,0:T(8,128)S(1)}) custom-call(bf16[640,256]{1,0:T(8,128)(2,1)S(1)} %get-tuple-element.28.own_ref, f32[1,128]{1,0:T(1,128)S(1)} %bitcast.3, f32[1,128]{1,0:T(1,128)S(1)} %bitcast.4, bf16[512,512]{1,0:T(8,128)(2,1)S(1)} %get-tuple-element.25.pick_ref, ...), custom_call_target="tpu_custom_call" | custom-call | flops 6000000 | bytes 4000000 | tf_op jit(solution)/shard_map/pallas_call | solution.py:380
  39.4 0.0 collective-permute-done.2.after_ref
  39.4 0.4 shard_map.68.bottom_ref
  39.8 1.8 %collective-permute-done.1.before_ref = bf16[160,256]{1,0:T(8,128)(2,1)S(1)} collective-permute-done((bf16[160,256]{1,0:T(8,128)(2,1)S(1)}, bf16[160,256]{1,0:T(8,128)(2,1)S(1)}, u32[]{:S(2)}, u32[]{:S(2)}) %collective-permute-start.1) | collective-permute-done | bytes 81952 | tf_op jit(solution)/shard_map/ppermute | solution.py:395
  41.6 1.1 %shard_map.69 = f32[256,128]{1,0:T(8,128)} custom-call(bf16[160,256]{1,0:T(8,128)(2,1)S(1)} %collective-permute-done.1.before_ref, bf16[160,256]{1,0:T(8,128)(2,1)S(1)} %get-tuple-element.24.first_ref, bf16[512,512]{1,0:T(8,128)(2,1)S(1)} %get-tuple-element.25.pick_ref, f32[256,128]{1,0:T(8,128)S(1)} %get-tuple-element.26.weight_ref, ...), custom_call_target="tpu_custom_call" | custom-call | flops 3000000 | bytes 3000000 | tf_op jit(solution)/shard_map/pallas_call | solution.py:408
  (1 shorter events, 0.0 us)
Async XLA Ops:
  1.6 28.3 %copy-start.4 = (s32[8,8,2]{1,2,0:T(2,128)S(1)}, s32[8,8,2]{1,2,0:T(2,128)}, u32[]{:S(2)}) copy-start(s32[8,8,2]{1,2,0:T(2,128)} %param.8) | copy-start | bytes 1540
  1.6 28.4 %copy-start = (s32[32,512]{1,0:T(8,128)S(1)}, s32[32,512]{1,0:T(8,128)}, u32[]{:S(2)}) copy-start(s32[32,512]{1,0:T(8,128)} %mask_ref.3) | copy-start | bytes 196612
  1.7 30.0 %copy-start.1 = (bf16[512,256]{1,0:T(8,128)(2,1)S(1)}, bf16[512,256]{1,0:T(8,128)(2,1)}, u32[]{:S(2)}) copy-start(bf16[512,256]{1,0:T(8,128)(2,1)} %constant.8.table_ref) | copy-start | bytes 786436
  28.0 3.7 %collective-permute-start = (bf16[32,56,128]{2,1,0:T(8,128)(2,1)S(1)}, bf16[32,56,128]{2,1,0:T(8,128)(2,1)S(1)}, u32[]{:S(2)}, u32[]{:S(2)}) collective-permute-start(bf16[32,56,128]{2,1,0:T(8,128)(2,1)S(1)} %all_to_all.5.mine_ref), channel_id=1, source_target_pairs={{0,1},{1,0},{2,3},{3,2},{4,5},{5,4},{6,7},{7,6},{8,9},{9,8},{10,11... | collective-permute-start | bytes 1376264 | tf_op jit(solution)/shard_map/ppermute | solution.py:433
  32.1 7.3 %collective-permute-start.2 = (bf16[160,256]{1,0:T(8,128)(2,1)S(1)}, bf16[160,256]{1,0:T(8,128)(2,1)S(1)}, u32[]{:S(2)}, u32[]{:S(2)}) collective-permute-start(bf16[160,256]{1,0:T(8,128)(2,1)S(1)} %get-tuple-element.24.first_ref), channel_id=1, source_target_pairs={{64,0},{128,64},{192,128},{256,192},{320,256},{384,320},{448,384},... | collective-permute-start | bytes 245768 | tf_op jit(solution)/shard_map/ppermute | solution.py:394
  34.0 7.6 %collective-permute-start.1 = (bf16[160,256]{1,0:T(8,128)(2,1)S(1)}, bf16[160,256]{1,0:T(8,128)(2,1)S(1)}, u32[]{:S(2)}, u32[]{:S(2)}) collective-permute-start(bf16[160,256]{1,0:T(8,128)(2,1)S(1)} %get-tuple-element.23.last_ref), channel_id=1, source_target_pairs={{0,64},{64,128},{128,192},{192,256},{256,320},{320,384},{384,448},... | collective-permute-start | bytes 245768 | tf_op jit(solution)/shard_map/ppermute | solution.py:395
  37.9 0.7 %copy-start.2 = (f32[128]{0:T(128)S(1)}, f32[128]{0:T(128)}, u32[]{:S(2)}) copy-start(f32[128]{0:T(128)} %param.9) | copy-start | bytes 1540
  37.9 0.7 %copy-start.3 = (f32[128]{0:T(128)S(1)}, f32[128]{0:T(128)}, u32[]{:S(2)}) copy-start(f32[128]{0:T(128)} %param.10) | copy-start | bytes 1540

commit v8 on v7

--- a/solution.py
+++ b/solution.py
@@ -21,6 +21,9 @@
 SPAN = 28
 LEAD = 6
 QUADS = (0, 16, 8, 24, 32, 48, 40)
+MARGIN = 5
+NARROW = 18
+SENT = 96
 BLOCKS = 72
 TALL = 48
 REACH = 40
@@ -53,11 +56,26 @@
 
 
 def pack_kernel(
-    frames_ref, mask_ref, out_ref, frames_vmem, mask_vmem, pick_ref, low_ref, high_ref, sems
+    frames_ref,
+    mask_ref,
+    gain_ref,
+    mix_ref,
+    out_ref,
+    pair_ref,
+    frames_vmem,
+    mask_vmem,
+    gain_vmem,
+    mix_vmem,
+    pick_ref,
+    low_ref,
+    high_ref,
+    sems,
 ):
     copies = [
         pltpu.make_async_copy(mask_ref, mask_vmem, sems.at[0]),
         pltpu.make_async_copy(frames_ref, frames_vmem, sems.at[1]),
+        pltpu.make_async_copy(gain_ref, gain_vmem, sems.at[2]),
+        pltpu.make_async_copy(mix_ref, mix_vmem, sems.at[3]),
     ]
     for copy in copies:
         copy.start()
@@ -69,6 +87,8 @@
         pick_ref[c * BLOCKS : (c + 1) * BLOCKS, :] = jnp.where(place == c, 1.0, 0.0)
     for copy in copies:
         copy.wait()
+    pair_ref[0:1, :] = gain_vmem[...]
+    pair_ref[1:2, :] = mix_vmem[...]
     mask = mask_vmem[...].astype(F32)
     masked = (frames_vmem[...].astype(F32) * mask[None]).astype(BF16)
     turned = lax.dot_general(
@@ -96,24 +116,37 @@
     out_ref[:, 48:56, :] = laid[:, 0:8, :].astype(BF16)
 
 
-def pack(frames, mask):
+def pack(frames, mask, gain, mix):
     return pl.pallas_call(
         pack_kernel,
-        out_shape=pltpu.VMEM((CHIPS, 2 * SPAN, 128), BF16),
-        in_specs=[pl.BlockSpec(memory_space=pltpu.HBM)] * 2,
+        out_shape=(pltpu.VMEM((CHIPS, 2 * SPAN, 128), BF16), pltpu.VMEM((8, FREQ), F32)),
+        in_specs=[pl.BlockSpec(memory_space=pltpu.HBM)] * 4,
         scratch_shapes=[
             pltpu.VMEM(frames.shape, BF16),
             pltpu.VMEM(mask.shape, jnp.int32),
+            pltpu.VMEM((1, FREQ), F32),
+            pltpu.VMEM((1, FREQ), F32),
             pltpu.VMEM((COLS * BLOCKS, mask.shape[1]), F32),
             pltpu.VMEM((BLOCKS * LOCAL, 128), F32),
             pltpu.VMEM((BLOCKS * LOCAL, 128), F32),
-            pltpu.SemaphoreType.DMA((2,)),
+            pltpu.SemaphoreType.DMA((4,)),
         ],
         compiler_params=pltpu.CompilerParams(vmem_limit_bytes=60000000),
-    )(frames, mask)
-
-
-def spectra_kernel(mine_ref, other_ref, table_ref, own_ref, first_ref, last_ref):
+    )(frames, mask, gain, mix)
+
+
+def spectra_kernel(
+    mine_ref,
+    other_ref,
+    table_ref,
+    own_ref,
+    first_ref,
+    last_ref,
+    first_re,
+    first_im,
+    last_re,
+    last_im,
+):
     core = lax.axis_index("tile") % 2
     count = FRAMES // 2
     spectrum = None
@@ -129,16 +162,27 @@
         spectrum = part if spectrum is None else spectrum + part
     own_ref[...] = spectrum.astype(BF16)
     by_column = spectrum.reshape(WIDE, ROWS, 2 * FREQ)
-    first_ref[...] = by_column[:, :8].reshape(WIDE * 8, 2 * FREQ).astype(BF16)
-    last_ref[...] = by_column[:, ROWS - 8 :].reshape(WIDE * 8, 2 * FREQ).astype(BF16)
+    for q in range(NARROW):
+        first_re[q * MARGIN : q * MARGIN + 8, :] = by_column[q + 1, :8, :FREQ]
+        first_im[q * MARGIN : q * MARGIN + 8, :] = by_column[q + 1, :8, FREQ:]
+    for q in reversed(range(NARROW)):
+        at = q * MARGIN + 5
+        last_re[at : at + 8, :] = by_column[q + 1, ROWS - 8 :, :FREQ]
+        last_im[at : at + 8, :] = by_column[q + 1, ROWS - 8 :, FREQ:]
+    first_ref[:, :FREQ] = first_re[0:SENT, :].astype(BF16)
+    first_ref[:, FREQ:] = first_im[0:SENT, :].astype(BF16)
+    last_ref[:, :FREQ] = last_re[8 : 8 + SENT, :].astype(BF16)
+    last_ref[:, FREQ:] = last_im[8 : 8 + SENT, :].astype(BF16)
 
 
 def spectra(mine, other, table):
-    edge = jax.ShapeDtypeStruct((WIDE * 8, 2 * FREQ), BF16)
+    edge = jax.ShapeDtypeStruct((SENT, 2 * FREQ), BF16)
+    own = jax.ShapeDtypeStruct((WIDE * ROWS, 2 * FREQ), BF16)
     return pl.pallas_call(
         spectra_kernel,
-        out_shape=(jax.ShapeDtypeStruct((WIDE * ROWS, 2 * FREQ), BF16), edge, edge),
-        compiler_params=pltpu.CompilerParams(vmem_limit_bytes=32 * 1024 * 1024),
+        out_shape=(own, edge, edge),
+        scratch_shapes=[pltpu.VMEM((SENT + 16, FREQ), F32)] * 4,
+        compiler_params=params(),
     )(mine, other, table)
 
 
@@ -218,9 +262,10 @@
                 two = real_c * imag_a - imag_c * real_a
                 first_sum = one if first_sum is None else first_sum + one
                 second_sum = two if c == 0 else second_sum + two
-            at = (part * 16 + 2 * d) * 8
-            sums[at : at + 8, :] = first_sum
-            sums[at + 8 : at + 16, :] = second_sum
+            for n, value in enumerate((first_sum, second_sum)):
+                at = (part * 16 + 2 * d + n) * 8
+                value = value + pltpu.roll(value, 7, 0)
+                sums[at : at + 8, :] = value + pltpu.roll(value, 6, 0)
     for half in range(2):
         for part in range(2):
             block = (group * 2 + half) * 2 + part
@@ -228,33 +273,27 @@
             for piece in range(2):
                 base = (part * 16 + piece * 8) * 8 + half * 4
                 total = sums[pl.ds(base, 8, stride=8), :]
-                for k in range(1, 4):
-                    total = total + sums[pl.ds(base + k, 8, stride=8), :]
                 to = first + (half * 2 + part) * 16 + piece * 8
                 out_ref[to : to + 8, :] = total * share
 
 
 def middle_kernel(
     own_ref,
-    gain_ref,
-    mix_ref,
+    pair_ref,
     pick_ref,
     weight_ref,
     share_ref,
     out_ref,
     filt_re,
     filt_im,
-    pair_ref,
     own_re,
     own_im,
     *scratch,
 ):
     own_re[...] = own_ref[:, :FREQ].astype(F32)
     own_im[...] = own_ref[:, FREQ:].astype(F32)
-    gain = gain_ref[...]
-    mix = mix_ref[...]
-    pair_ref[0:1, :] = gain
-    pair_ref[1:2, :] = mix
+    gain = pair_ref[0:1, :]
+    mix = pair_ref[1:2, :]
     for source, filt in ((own_re, filt_re), (own_im, filt_im)):
         for q in range(SIDE):
             value = filtered(source, ROWS, (q + 2) * ROWS + 1, ROWS - 2, gain, mix)
@@ -266,33 +305,40 @@
 
 
 def edge_blocks(
-    group, upper_ref, lower_ref, pick_ref, weight_ref, share_ref, own_re, own_im, pair_ref, out_ref, scratch
-):
-    tall_re, tall_im, filt_re, filt_im, *scratch = scratch
-    for ref, at in ((upper_ref, 0), (lower_ref, 8)):
-        value = ref[...].astype(F32).reshape(WIDE, 8, 2 * FREQ)
-        for q in range(WIDE):
-            tall_re[at + q * 16 : at + q * 16 + 8, :] = value[q, :, :FREQ]
-            tall_im[at + q * 16 : at + q * 16 + 8, :] = value[q, :, FREQ:]
+    group, came_ref, own_ref, pick_ref, weight_ref, share_ref, own_re, own_im, pair_ref, out_ref, scratch
+):
+    came_re, came_im, tall_re, tall_im, filt_re, filt_im, *scratch = scratch
+    came_re[8 : 8 + SENT, :] = came_ref[:, :FREQ].astype(F32)
+    came_im[8 : 8 + SENT, :] = came_ref[:, FREQ:].astype(F32)
+    at, before, inside = (0, 3, 8) if group == 0 else (8, 0, 0)
+    row = 0 if group == 0 else ROWS - 8
+    for q in range(NARROW):
+        to = (q + 1) * 16
+        own = own_ref[(q + 1) * ROWS : (q + 2) * ROWS, :].astype(F32)[row : row + 8]
+        start = 8 + q * MARGIN - before
+        tall_re[to + at : to + at + 8, :] = came_re[start : start + 8, :]
+        tall_im[to + at : to + at + 8, :] = came_im[start : start + 8, :]
+        tall_re[to + inside : to + inside + 8, :] = own[:, :FREQ]
+        tall_im[to + inside : to + inside + 8, :] = own[:, FREQ:]
     gain = pair_ref[0:1, :]
     mix = pair_ref[1:2, :]
     edge, kept = (0, 8) if group == 0 else (32, 24)
-    for tall, inside, filt in ((tall_re, own_re, filt_re), (tall_im, own_im, filt_im)):
+    for tall, source, filt in ((tall_re, own_re, filt_re), (tall_im, own_im, filt_im)):
         for q in range(SIDE):
             at = q * REACH
             value = filtered(tall, 16, (q + 2) * 16 + 4, 8, gain, mix)
             filt[at + edge : at + edge + 8, :] = value
-            filt[at + kept : at + kept + 8, :] = inside[at + kept : at + kept + 8, :]
+            filt[at + kept : at + kept + 8, :] = source[at + kept : at + kept + 8, :]
     group_blocks(group, pick_ref, filt_re, filt_im, weight_ref, share_ref, out_ref, 0, scratch)
 
 
 def bottom_kernel(
-    last_ref, after_ref, pick_ref, weight_ref, share_ref, own_re, own_im, pair_ref, out_ref, *scratch
+    after_ref, own_ref, pick_ref, weight_ref, share_ref, own_re, own_im, pair_ref, out_ref, *scratch
 ):
     edge_blocks(
         3,
-        last_ref,
         after_ref,
+        own_ref,
         pick_ref,
         weight_ref,
         share_ref,
@@ -306,7 +352,7 @@
 
 def top_kernel(
     before_ref,
-    first_ref,
+    own_ref,
     pick_ref,
     weight_ref,
     share_ref,
@@ -330,7 +376,7 @@
     edge_blocks(
         0,
         before_ref,
-        first_ref,
+        own_ref,
         pick_ref,
         weight_ref,
         share_ref,
@@ -376,25 +422,25 @@
     )(steps, mask)
 
 
-def middle(own, gain, mix, chosen):
+def middle(own, pair, chosen):
     return pl.pallas_call(
         middle_kernel,
-        out_shape=tuple(float_shape(n) for n in (128, SIDE * REACH, SIDE * REACH, 8)),
-        in_specs=[VMEM] * 6,
+        out_shape=tuple(float_shape(n) for n in (128, SIDE * REACH, SIDE * REACH)),
+        in_specs=[VMEM] * 5,
         scratch_shapes=[pltpu.VMEM((WIDE * ROWS, FREQ), F32)] * 2 + GROUP_SCRATCH,
         compiler_params=params(),
         cost_estimate=pl.CostEstimate(flops=6_000_000, bytes_accessed=4_000_000, transcendentals=0),
-    )(own, gain, mix, *chosen)
-
-
-def outer(first, last, chosen, kept):
+    )(own, pair, *chosen)
+
+
+def outer(own, first, last, pair, chosen, kept):
     bands = lax.axis_size("band")
     up = [(i, i + 1) for i in range(bands - 1)]
     down = [(j, i) for i, j in up]
     after = lax.ppermute(first, "band", down)
     before = lax.ppermute(last, "band", up)
-    mid, *shared = kept
-    rows = [WIDE * 16] * 2 + [SIDE * REACH] * 2
+    mid, *shared = (*kept, pair)
+    rows = [SENT + 16] * 2 + [WIDE * 16] * 2 + [SIDE * REACH] * 2
     scratch = [pltpu.VMEM((n, FREQ), F32) for n in rows] + GROUP_SCRATCH
     cost = pl.CostEstimate(flops=3_000_000, bytes_accessed=3_000_000, transcendentals=0)
     bottom = pl.pallas_call(
@@ -404,7 +450,7 @@
         scratch_shapes=scratch,
         compiler_params=params(),
         cost_estimate=cost,
-    )(last, after, *chosen, *shared)
+    )(after, own, *chosen, *shared)
     return pl.pallas_call(
         top_kernel,
         out_shape=float_shape(8 * 2 * DIST * 2),
@@ -413,27 +459,23 @@
         scratch_shapes=[pltpu.VMEM((64, FREQ), F32), pltpu.SemaphoreType.DMA((3,))] + scratch,
         compiler_params=params(),
         cost_estimate=cost,
-    )(before, first, *chosen, *shared, mid, bottom)
+    )(before, own, *chosen, *shared, mid, bottom)
 
 
 def on_device(frames, disk_mask, offsets, filter_gain, filter_mix):
     same_core = [[2 * chip + core for chip in range(CHIPS)] for core in range(2)]
-    mine = lax.all_to_all(
-        pack(frames, disk_mask),
-        "tile",
-        split_axis=0,
-        concat_axis=0,
-        axis_index_groups=same_core,
-        tiled=True,
-    )
-    steps = ((offsets[..., 1] + 4) * 16 + offsets[..., 0] + 4).reshape(DIST * OFFS)
     gain = filter_gain.reshape(1, FREQ)
     mix = filter_mix.reshape(1, FREQ)
+    packed, pair = pack(frames, disk_mask, gain, mix)
+    mine = lax.all_to_all(
+        packed, "tile", split_axis=0, concat_axis=0, axis_index_groups=same_core, tiled=True
+    )
+    other = lax.ppermute(mine, "tile", [(i, i ^ 1) for i in range(2 * CHIPS)])
+    steps = ((offsets[..., 1] + 4) * 16 + offsets[..., 0] + 4).reshape(DIST * OFFS)
     chosen = select(steps, disk_mask)
-    other = lax.ppermute(mine, "tile", [(i, i ^ 1) for i in range(2 * CHIPS)])
     other, chosen = lax.optimization_barrier((other, chosen))
     own, first, last = spectra(mine, other, dft_table())
-    out = outer(first, last, chosen, middle(own, gain, mix, chosen))
+    out = outer(own, first, last, pair, chosen, middle(own, pair, chosen))
     return out.reshape(8, 2, DIST, 2, FREQ)
 
 

time: 42.9 us -> 42.6 us (level)
  the two profiles are of different devices: /device:TPU:264 before, /device:TPU:200 now
where the time goes in v8:
time: 42.6 us; the launch traced here: 42.4 us
  blocking collectives  26.3 us (62%)
  starting transfers between devices  9.33 us (22%)
  Pallas kernels  5.57 us (13%)
  waiting for transfers between devices  0.96 us (2%)
    all_to_all x1, blocking collectives, on_device(): lax.all_to_all(packed, 'tile', split_axis=0, concat_axis=0, axis_index_gr...  26.3 us
    ppermute x1, starting transfers between devices, outer(): before = lax.ppermute(last, 'band', up)  5.5 us
    ppermute x1, starting transfers between devices, outer(): after = lax.ppermute(first, 'band', down)  1.92 us
    ppermute x1, starting transfers between devices, on_device(): other = lax.ppermute(mine, 'tile', [(i, i ^ 1) for i in range(2 * CHIPS)])  1.91 us
    pallas_call x1, Pallas kernels, pack(): pl.pallas_call(pack_kernel, out_shape=(pltpu.VMEM((CHIPS, 2 * SPAN, 128),...  1.65 us
    pallas_call x1, Pallas kernels, select(): pl.pallas_call(select_kernel, out_shape=(jax.ShapeDtypeStruct((DIST * COL...  1.22 us
    pallas_call x1, Pallas kernels, outer(): pl.pallas_call(top_kernel, out_shape=float_shape(8 * 2 * DIST * 2), in_sp...  1.08 us
  transfers between devices with their start and end apart: 3, of which 2 were waited for; matrix products, arithmetic and copies ran while one was open for 0% of the time, Pallas kernels for 6%

profile of v8, /device:TPU:200, one launch (start us, length us, event | category | flops | bytes accessed | tf_op | source)
XLA Modules:
  0.0 42.4 jit_solution(3422323575920520941)
XLA Ops:
  0.0 1.6 %shard_map.64 = (bf16[32,56,128]{2,1,0:T(8,128)(2,1)S(1)}, f32[8,128]{1,0:T(8,128)S(1)}) custom-call(bf16[8,32,512]{2,1,0:T(8,128)(2,1)} %frames_ref.1, s32[32,512]{1,0:T(8,128)} %mask_ref.3, f32[1,128]{1,0:T(1,128)} %bitcast.3, f32[1,128]{1,0:T(1,128)} %bitcast.4), custom_call_target="tpu_custom_call" | custom-call | tf_op jit(solution)/shard_map/pallas_call | solution.py:120
  1.7 0.0 copy-start.2
  1.7 0.0 copy-start
  1.7 0.0 copy-start.1
  1.7 26.3 %all_to_all.5.mine_ref = bf16[32,56,128]{2,1,0:T(8,128)(2,1)S(1)} all-to-all(bf16[32,56,128]{2,1,0:T(8,128)(2,1)S(1)} %get-tuple-element.20), channel_id=1, replica_groups={{0,2,4,6,8,10,12,14,16,18,20,22,24,26,28,30,32,34,36,38,40,42,44,46,48,..., dimensions={0} | all-to-all | bytes 917504 | tf_op jit(solution)/shard_map/all_to_all | solution.py:470
  28.0 1.9 %collective-permute-start = (bf16[32,56,128]{2,1,0:T(8,128)(2,1)S(1)}, bf16[32,56,128]{2,1,0:T(8,128)(2,1)S(1)}, u32[]{:S(2)}, u32[]{:S(2)}) collective-permute-start(bf16[32,56,128]{2,1,0:T(8,128)(2,1)S(1)} %all_to_all.5.mine_ref), channel_id=1, source_target_pairs={{0,1},{1,0},{2,3},{3,2},{4,5},{5,4},{6,7},{7,6},{8,9},{9,8},{10,11... | collective-permute-start | bytes 1376264 | tf_op jit(solution)/shard_map/ppermute | solution.py:473
  29.9 0.0 copy-done.2
  29.9 0.1 add.20.offsets_ref
  30.0 0.0 copy-done
  30.0 1.2 %shard_map.65 = (bf16[512,512]{1,0:T(8,128)(2,1)S(1)}, f32[256,128]{1,0:T(8,128)S(1)}, f32[16,128]{1,0:T(8,128)S(1)}) custom-call(s32[64]{0:T(128)S(1)} %add.20.offsets_ref, s32[32,512]{1,0:T(8,128)S(1)} %copy-done), custom_call_target="tpu_custom_call" | custom-call | flops 4000000 | bytes 4000000 | tf_op jit(solution)/shard_map/pallas_call | solution.py:412
  31.3 0.4 %collective-permute-done.other_ref = bf16[32,56,128]{2,1,0:T(8,128)(2,1)S(1)} collective-permute-done((bf16[32,56,128]{2,1,0:T(8,128)(2,1)S(1)}, bf16[32,56,128]{2,1,0:T(8,128)(2,1)S(1)}, u32[]{:S(2)}, u32[]{:S(2)}) %collective-permute-start) | collective-permute-done | bytes 458784 | tf_op jit(solution)/shard_map/ppermute | solution.py:473
  31.7 0.0 copy-done.1
  31.7 0.4 %shard_map.66 = (bf16[640,256]{1,0:T(8,128)(2,1)S(1)}, bf16[96,256]{1,0:T(8,128)(2,1)S(1)}, bf16[96,256]{1,0:T(8,128)(2,1)S(1)}) custom-call(bf16[32,56,128]{2,1,0:T(8,128)(2,1)S(1)} %all_to_all.5.mine_ref, bf16[32,56,128]{2,1,0:T(8,128)(2,1)S(1)} %collective-permute-done.other_ref, bf16[512,256]{1,0:T(8,128)(2,1)S(1)} %copy-done.1), custom_call_target="tpu_custom_call" | custom-call | tf_op jit(solution)/shard_map/pallas_call | solution.py:181
  32.1 1.9 %collective-permute-start.2 = (bf16[96,256]{1,0:T(8,128)(2,1)S(1)}, bf16[96,256]{1,0:T(8,128)(2,1)S(1)}, u32[]{:S(2)}, u32[]{:S(2)}) collective-permute-start(bf16[96,256]{1,0:T(8,128)(2,1)S(1)} %get-tuple-element.34), channel_id=1, source_target_pairs={{64,0},{128,64},{192,128},{256,192},{320,256},{384,320},{448,384},... | collective-permute-start | bytes 147464 | tf_op jit(solution)/shard_map/ppermute | solution.py:440
  34.1 5.5 %collective-permute-start.1 = (bf16[96,256]{1,0:T(8,128)(2,1)S(1)}, bf16[96,256]{1,0:T(8,128)(2,1)S(1)}, u32[]{:S(2)}, u32[]{:S(2)}) collective-permute-start(bf16[96,256]{1,0:T(8,128)(2,1)S(1)} %get-tuple-element.25), channel_id=1, source_target_pairs={{0,64},{64,128},{128,192},{192,256},{256,320},{320,384},{384,448},... | collective-permute-start | bytes 147464 | tf_op jit(solution)/shard_map/ppermute | solution.py:441
  39.6 0.8 %shard_map.67 = (f32[128,128]{1,0:T(8,128)S(1)}, f32[640,128]{1,0:T(8,128)S(1)}, f32[640,128]{1,0:T(8,128)S(1)}) custom-call(bf16[640,256]{1,0:T(8,128)(2,1)S(1)} %get-tuple-element.26.own_ref, f32[8,128]{1,0:T(8,128)S(1)} %get-tuple-element.30.pair_ref, bf16[512,512]{1,0:T(8,128)(2,1)S(1)} %get-tuple-element.27.pick_ref, ...), custom_call_target="tpu_custom_call" | custom-call | flops 6000000 | bytes 4000000 | tf_op jit(solution)/shard_map/pallas_call | solution.py:426
  40.3 0.0 collective-permute-done.2.after_ref
  40.3 0.4 %shard_map.68.bottom_ref = f32[64,128]{1,0:T(8,128)S(1)} custom-call(bf16[96,256]{1,0:T(8,128)(2,1)S(1)} %collective-permute-done.2.after_ref, bf16[640,256]{1,0:T(8,128)(2,1)S(1)} %get-tuple-element.26.own_ref, bf16[512,512]{1,0:T(8,128)(2,1)S(1)} %get-tuple-element.27.pick_ref, f32[256,128]{1,0:T(8,128)S(1)} %get-tuple-element.28.weight_ref, ...), custom_call_target="tpu_custom_call" | custom-call | flops 3000000 | bytes 3000000 | tf_op jit(solution)/shard_map/pallas_call | solution.py:446
  40.8 0.5 %collective-permute-done.1.before_ref = bf16[96,256]{1,0:T(8,128)(2,1)S(1)} collective-permute-done((bf16[96,256]{1,0:T(8,128)(2,1)S(1)}, bf16[96,256]{1,0:T(8,128)(2,1)S(1)}, u32[]{:S(2)}, u32[]{:S(2)}) %collective-permute-start.1) | collective-permute-done | bytes 49184 | tf_op jit(solution)/shard_map/ppermute | solution.py:441
  41.3 1.1 %shard_map.69 = f32[256,128]{1,0:T(8,128)} custom-call(bf16[96,256]{1,0:T(8,128)(2,1)S(1)} %collective-permute-done.1.before_ref, bf16[640,256]{1,0:T(8,128)(2,1)S(1)} %get-tuple-element.26.own_ref, bf16[512,512]{1,0:T(8,128)(2,1)S(1)} %get-tuple-element.27.pick_ref, f32[256,128]{1,0:T(8,128)S(1)} %get-tuple-element.28.weight_ref, ...), custom_call_target="tpu_custom_call" | custom-call | flops 3000000 | bytes 3000000 | tf_op jit(solution)/shard_map/pallas_call | solution.py:454
  (1 shorter events, 0.0 us)
Async XLA Ops:
  1.7 28.3 %copy-start.2 = (s32[8,8,2]{1,2,0:T(2,128)S(1)}, s32[8,8,2]{1,2,0:T(2,128)}, u32[]{:S(2)}) copy-start(s32[8,8,2]{1,2,0:T(2,128)} %param.8) | copy-start | bytes 1540
  1.7 28.4 %copy-start = (s32[32,512]{1,0:T(8,128)S(1)}, s32[32,512]{1,0:T(8,128)}, u32[]{:S(2)}) copy-start(s32[32,512]{1,0:T(8,128)} %mask_ref.3) | copy-start | bytes 196612
  1.7 30.0 %copy-start.1 = (bf16[512,256]{1,0:T(8,128)(2,1)S(1)}, bf16[512,256]{1,0:T(8,128)(2,1)}, u32[]{:S(2)}) copy-start(bf16[512,256]{1,0:T(8,128)(2,1)} %constant.8.table_ref) | copy-start | bytes 786436
  28.0 3.7 %collective-permute-start = (bf16[32,56,128]{2,1,0:T(8,128)(2,1)S(1)}, bf16[32,56,128]{2,1,0:T(8,128)(2,1)S(1)}, u32[]{:S(2)}, u32[]{:S(2)}) collective-permute-start(bf16[32,56,128]{2,1,0:T(8,128)(2,1)S(1)} %all_to_all.5.mine_ref), channel_id=1, source_target_pairs={{0,1},{1,0},{2,3},{3,2},{4,5},{5,4},{6,7},{7,6},{8,9},{9,8},{10,11... | collective-permute-start | bytes 1376264 | tf_op jit(solution)/shard_map/ppermute | solution.py:473
  32.1 8.2 %collective-permute-start.2 = (bf16[96,256]{1,0:T(8,128)(2,1)S(1)}, bf16[96,256]{1,0:T(8,128)(2,1)S(1)}, u32[]{:S(2)}, u32[]{:S(2)}) collective-permute-start(bf16[96,256]{1,0:T(8,128)(2,1)S(1)} %get-tuple-element.34), channel_id=1, source_target_pairs={{64,0},{128,64},{192,128},{256,192},{320,256},{384,320},{448,384},... | collective-permute-start | bytes 147464 | tf_op jit(solution)/shard_map/ppermute | solution.py:440
  34.1 7.2 %collective-permute-start.1 = (bf16[96,256]{1,0:T(8,128)(2,1)S(1)}, bf16[96,256]{1,0:T(8,128)(2,1)S(1)}, u32[]{:S(2)}, u32[]{:S(2)}) collective-permute-start(bf16[96,256]{1,0:T(8,128)(2,1)S(1)} %get-tuple-element.25), channel_id=1, source_target_pairs={{0,64},{64,128},{128,192},{192,256},{256,320},{320,384},{384,448},... | collective-permute-start | bytes 147464 | tf_op jit(solution)/shard_map/ppermute | solution.py:441

commit v9 on v8

--- a/solution.py
+++ b/solution.py
@@ -73,18 +73,19 @@
 ):
     copies = [
         pltpu.make_async_copy(mask_ref, mask_vmem, sems.at[0]),
-        pltpu.make_async_copy(frames_ref, frames_vmem, sems.at[1]),
-        pltpu.make_async_copy(gain_ref, gain_vmem, sems.at[2]),
-        pltpu.make_async_copy(mix_ref, mix_vmem, sems.at[3]),
+        pltpu.make_async_copy(gain_ref, gain_vmem, sems.at[1]),
+        pltpu.make_async_copy(mix_ref, mix_vmem, sems.at[2]),
+    ] + [
+        pltpu.make_async_copy(frames_ref.at[f], frames_vmem.at[f], sems.at[3 + f])
+        for f in range(LOCAL)
     ]
     for copy in copies:
         copy.start()
     width = mask_vmem.shape[1]
-    cols = lax.broadcasted_iota(jnp.int32, (BLOCKS, width), 1)
-    block = lax.broadcasted_iota(jnp.int32, (BLOCKS, width), 0)
-    place = cols - 8 * block + LEAD
-    for c in range(COLS):
-        pick_ref[c * BLOCKS : (c + 1) * BLOCKS, :] = jnp.where(place == c, 1.0, 0.0)
+    cols = lax.broadcasted_iota(jnp.int32, (COLS * BLOCKS, width), 1)
+    line = lax.broadcasted_iota(jnp.int32, (COLS * BLOCKS, width), 0)
+    wanted = 8 * (line % BLOCKS) + line // BLOCKS - LEAD
+    pick_ref[...] = jnp.where(cols == wanted, 1.0, 0.0).astype(BF16)
     for copy in copies:
         copy.wait()
     pair_ref[0:1, :] = gain_vmem[...]
@@ -92,7 +93,7 @@
     mask = mask_vmem[...].astype(F32)
     masked = (frames_vmem[...].astype(F32) * mask[None]).astype(BF16)
     turned = lax.dot_general(
-        pick_ref[...].astype(BF16),
+        pick_ref[...],
         masked.reshape(LOCAL * ROWS, width),
         (((1,), (1,)), ((), ())),
         preferred_element_type=F32,
@@ -126,10 +127,10 @@
             pltpu.VMEM(mask.shape, jnp.int32),
             pltpu.VMEM((1, FREQ), F32),
             pltpu.VMEM((1, FREQ), F32),
-            pltpu.VMEM((COLS * BLOCKS, mask.shape[1]), F32),
+            pltpu.VMEM((COLS * BLOCKS, mask.shape[1]), BF16),
             pltpu.VMEM((BLOCKS * LOCAL, 128), F32),
             pltpu.VMEM((BLOCKS * LOCAL, 128), F32),
-            pltpu.SemaphoreType.DMA((4,)),
+            pltpu.SemaphoreType.DMA((3 + LOCAL,)),
         ],
         compiler_params=pltpu.CompilerParams(vmem_limit_bytes=60000000),
     )(frames, mask, gain, mix)

time: 42.6 us -> 42.6 us (level)
  no operation moved by 1% of the time
where the time goes in v9:
time: 42.6 us; the launch traced here: 42.4 us
  blocking collectives  26.3 us (62%)
  starting transfers between devices  9.32 us (22%)
  Pallas kernels  5.57 us (13%)
  waiting for transfers between devices  0.95 us (2%)
    all_to_all x1, blocking collectives, on_device(): lax.all_to_all(packed, 'tile', split_axis=0, concat_axis=0, axis_index_gr...  26.3 us
    ppermute x1, starting transfers between devices, outer(): before = lax.ppermute(last, 'band', up)  5.49 us
    ppermute x1, starting transfers between devices, outer(): after = lax.ppermute(first, 'band', down)  1.92 us
    ppermute x1, starting transfers between devices, on_device(): other = lax.ppermute(mine, 'tile', [(i, i ^ 1) for i in range(2 * CHIPS)])  1.91 us
    pallas_call x1, Pallas kernels, pack(): pl.pallas_call(pack_kernel, out_shape=(pltpu.VMEM((CHIPS, 2 * SPAN, 128),...  1.65 us
    pallas_call x1, Pallas kernels, select(): pl.pallas_call(select_kernel, out_shape=(jax.ShapeDtypeStruct((DIST * COL...  1.22 us
    pallas_call x1, Pallas kernels, outer(): pl.pallas_call(top_kernel, out_shape=float_shape(8 * 2 * DIST * 2), in_sp...  1.08 us
  transfers between devices with their start and end apart: 3, of which 2 were waited for; matrix products, arithmetic and copies ran while one was open for 0% of the time, Pallas kernels for 6%

profile of v9, /device:TPU:200, one launch (start us, length us, event | category | flops | bytes accessed | tf_op | source)
XLA Modules:
  0.0 42.4 jit_solution(12989515445477907437)
XLA Ops:
  0.0 1.6 %shard_map.64 = (bf16[32,56,128]{2,1,0:T(8,128)(2,1)S(1)}, f32[8,128]{1,0:T(8,128)S(1)}) custom-call(bf16[8,32,512]{2,1,0:T(8,128)(2,1)} %frames_ref.1, s32[32,512]{1,0:T(8,128)} %mask_ref.3, f32[1,128]{1,0:T(1,128)} %bitcast.3, f32[1,128]{1,0:T(1,128)} %bitcast.4), custom_call_target="tpu_custom_call" | custom-call | tf_op jit(solution)/shard_map/pallas_call | solution.py:121
  1.7 0.0 copy-start.2
  1.7 0.0 copy-start
  1.7 0.0 copy-start.1
  1.7 26.3 %all_to_all.5.mine_ref = bf16[32,56,128]{2,1,0:T(8,128)(2,1)S(1)} all-to-all(bf16[32,56,128]{2,1,0:T(8,128)(2,1)S(1)} %get-tuple-element.20), channel_id=1, replica_groups={{0,2,4,6,8,10,12,14,16,18,20,22,24,26,28,30,32,34,36,38,40,42,44,46,48,..., dimensions={0} | all-to-all | bytes 917504 | tf_op jit(solution)/shard_map/all_to_all | solution.py:471
  28.0 1.9 %collective-permute-start = (bf16[32,56,128]{2,1,0:T(8,128)(2,1)S(1)}, bf16[32,56,128]{2,1,0:T(8,128)(2,1)S(1)}, u32[]{:S(2)}, u32[]{:S(2)}) collective-permute-start(bf16[32,56,128]{2,1,0:T(8,128)(2,1)S(1)} %all_to_all.5.mine_ref), channel_id=1, source_target_pairs={{0,1},{1,0},{2,3},{3,2},{4,5},{5,4},{6,7},{7,6},{8,9},{9,8},{10,11... | collective-permute-start | bytes 1376264 | tf_op jit(solution)/shard_map/ppermute | solution.py:474
  29.9 0.0 copy-done.2
  29.9 0.1 add.20.offsets_ref
  30.0 0.0 copy-done
  30.0 1.2 %shard_map.65 = (bf16[512,512]{1,0:T(8,128)(2,1)S(1)}, f32[256,128]{1,0:T(8,128)S(1)}, f32[16,128]{1,0:T(8,128)S(1)}) custom-call(s32[64]{0:T(128)S(1)} %add.20.offsets_ref, s32[32,512]{1,0:T(8,128)S(1)} %copy-done), custom_call_target="tpu_custom_call" | custom-call | flops 4000000 | bytes 4000000 | tf_op jit(solution)/shard_map/pallas_call | solution.py:413
  31.3 0.4 %collective-permute-done.other_ref = bf16[32,56,128]{2,1,0:T(8,128)(2,1)S(1)} collective-permute-done((bf16[32,56,128]{2,1,0:T(8,128)(2,1)S(1)}, bf16[32,56,128]{2,1,0:T(8,128)(2,1)S(1)}, u32[]{:S(2)}, u32[]{:S(2)}) %collective-permute-start) | collective-permute-done | bytes 458784 | tf_op jit(solution)/shard_map/ppermute | solution.py:474
  31.7 0.0 copy-done.1
  31.7 0.4 %shard_map.66 = (bf16[640,256]{1,0:T(8,128)(2,1)S(1)}, bf16[96,256]{1,0:T(8,128)(2,1)S(1)}, bf16[96,256]{1,0:T(8,128)(2,1)S(1)}) custom-call(bf16[32,56,128]{2,1,0:T(8,128)(2,1)S(1)} %all_to_all.5.mine_ref, bf16[32,56,128]{2,1,0:T(8,128)(2,1)S(1)} %collective-permute-done.other_ref, bf16[512,256]{1,0:T(8,128)(2,1)S(1)} %copy-done.1), custom_call_target="tpu_custom_call" | custom-call | tf_op jit(solution)/shard_map/pallas_call | solution.py:182
  32.1 1.9 %collective-permute-start.2 = (bf16[96,256]{1,0:T(8,128)(2,1)S(1)}, bf16[96,256]{1,0:T(8,128)(2,1)S(1)}, u32[]{:S(2)}, u32[]{:S(2)}) collective-permute-start(bf16[96,256]{1,0:T(8,128)(2,1)S(1)} %get-tuple-element.34), channel_id=1, source_target_pairs={{64,0},{128,64},{192,128},{256,192},{320,256},{384,320},{448,384},... | collective-permute-start | bytes 147464 | tf_op jit(solution)/shard_map/ppermute | solution.py:441
  34.1 5.5 %collective-permute-start.1 = (bf16[96,256]{1,0:T(8,128)(2,1)S(1)}, bf16[96,256]{1,0:T(8,128)(2,1)S(1)}, u32[]{:S(2)}, u32[]{:S(2)}) collective-permute-start(bf16[96,256]{1,0:T(8,128)(2,1)S(1)} %get-tuple-element.25), channel_id=1, source_target_pairs={{0,64},{64,128},{128,192},{192,256},{256,320},{320,384},{384,448},... | collective-permute-start | bytes 147464 | tf_op jit(solution)/shard_map/ppermute | solution.py:442
  39.6 0.8 %shard_map.67 = (f32[128,128]{1,0:T(8,128)S(1)}, f32[640,128]{1,0:T(8,128)S(1)}, f32[640,128]{1,0:T(8,128)S(1)}) custom-call(bf16[640,256]{1,0:T(8,128)(2,1)S(1)} %get-tuple-element.26.own_ref, f32[8,128]{1,0:T(8,128)S(1)} %get-tuple-element.30.pair_ref, bf16[512,512]{1,0:T(8,128)(2,1)S(1)} %get-tuple-element.27.pick_ref, ...), custom_call_target="tpu_custom_call" | custom-call | flops 6000000 | bytes 4000000 | tf_op jit(solution)/shard_map/pallas_call | solution.py:427
  40.3 0.0 collective-permute-done.2.after_ref
  40.3 0.4 %shard_map.68.bottom_ref = f32[64,128]{1,0:T(8,128)S(1)} custom-call(bf16[96,256]{1,0:T(8,128)(2,1)S(1)} %collective-permute-done.2.after_ref, bf16[640,256]{1,0:T(8,128)(2,1)S(1)} %get-tuple-element.26.own_ref, bf16[512,512]{1,0:T(8,128)(2,1)S(1)} %get-tuple-element.27.pick_ref, f32[256,128]{1,0:T(8,128)S(1)} %get-tuple-element.28.weight_ref, ...), custom_call_target="tpu_custom_call" | custom-call | flops 3000000 | bytes 3000000 | tf_op jit(solution)/shard_map/pallas_call | solution.py:447
  40.8 0.5 %collective-permute-done.1.before_ref = bf16[96,256]{1,0:T(8,128)(2,1)S(1)} collective-permute-done((bf16[96,256]{1,0:T(8,128)(2,1)S(1)}, bf16[96,256]{1,0:T(8,128)(2,1)S(1)}, u32[]{:S(2)}, u32[]{:S(2)}) %collective-permute-start.1) | collective-permute-done | bytes 49184 | tf_op jit(solution)/shard_map/ppermute | solution.py:442
  41.3 1.1 %shard_map.69 = f32[256,128]{1,0:T(8,128)} custom-call(bf16[96,256]{1,0:T(8,128)(2,1)S(1)} %collective-permute-done.1.before_ref, bf16[640,256]{1,0:T(8,128)(2,1)S(1)} %get-tuple-element.26.own_ref, bf16[512,512]{1,0:T(8,128)(2,1)S(1)} %get-tuple-element.27.pick_ref, f32[256,128]{1,0:T(8,128)S(1)} %get-tuple-element.28.weight_ref, ...), custom_call_target="tpu_custom_call" | custom-call | flops 3000000 | bytes 3000000 | tf_op jit(solution)/shard_map/pallas_call | solution.py:455
  (1 shorter events, 0.0 us)
Async XLA Ops:
  1.7 28.3 %copy-start.2 = (s32[8,8,2]{1,2,0:T(2,128)S(1)}, s32[8,8,2]{1,2,0:T(2,128)}, u32[]{:S(2)}) copy-start(s32[8,8,2]{1,2,0:T(2,128)} %param.8) | copy-start | bytes 1540
  1.7 28.4 %copy-start = (s32[32,512]{1,0:T(8,128)S(1)}, s32[32,512]{1,0:T(8,128)}, u32[]{:S(2)}) copy-start(s32[32,512]{1,0:T(8,128)} %mask_ref.3) | copy-start | bytes 196612
  1.7 30.0 %copy-start.1 = (bf16[512,256]{1,0:T(8,128)(2,1)S(1)}, bf16[512,256]{1,0:T(8,128)(2,1)}, u32[]{:S(2)}) copy-start(bf16[512,256]{1,0:T(8,128)(2,1)} %constant.8.table_ref) | copy-start | bytes 786436
  28.0 3.7 %collective-permute-start = (bf16[32,56,128]{2,1,0:T(8,128)(2,1)S(1)}, bf16[32,56,128]{2,1,0:T(8,128)(2,1)S(1)}, u32[]{:S(2)}, u32[]{:S(2)}) collective-permute-start(bf16[32,56,128]{2,1,0:T(8,128)(2,1)S(1)} %all_to_all.5.mine_ref), channel_id=1, source_target_pairs={{0,1},{1,0},{2,3},{3,2},{4,5},{5,4},{6,7},{7,6},{8,9},{9,8},{10,11... | collective-permute-start | bytes 1376264 | tf_op jit(solution)/shard_map/ppermute | solution.py:474
  32.1 8.2 %collective-permute-start.2 = (bf16[96,256]{1,0:T(8,128)(2,1)S(1)}, bf16[96,256]{1,0:T(8,128)(2,1)S(1)}, u32[]{:S(2)}, u32[]{:S(2)}) collective-permute-start(bf16[96,256]{1,0:T(8,128)(2,1)S(1)} %get-tuple-element.34), channel_id=1, source_target_pairs={{64,0},{128,64},{192,128},{256,192},{320,256},{384,320},{448,384},... | collective-permute-start | bytes 147464 | tf_op jit(solution)/shard_map/ppermute | solution.py:441
  34.1 7.2 %collective-permute-start.1 = (bf16[96,256]{1,0:T(8,128)(2,1)S(1)}, bf16[96,256]{1,0:T(8,128)(2,1)S(1)}, u32[]{:S(2)}, u32[]{:S(2)}) collective-permute-start(bf16[96,256]{1,0:T(8,128)(2,1)S(1)} %get-tuple-element.25), channel_id=1, source_target_pairs={{0,64},{64,128},{128,192},{192,256},{256,320},{320,384},{384,448},... | collective-permute-start | bytes 147464 | tf_op jit(solution)/shard_map/ppermute | solution.py:442

commit v10 on v9

--- a/solution.py
+++ b/solution.py
@@ -333,12 +333,12 @@
     group_blocks(group, pick_ref, filt_re, filt_im, weight_ref, share_ref, out_ref, 0, scratch)
 
 
-def bottom_kernel(
-    after_ref, own_ref, pick_ref, weight_ref, share_ref, own_re, own_im, pair_ref, out_ref, *scratch
+def first_edge_kernel(
+    came_ref, own_ref, pick_ref, weight_ref, share_ref, own_re, own_im, pair_ref, out_ref, *scratch
 ):
     edge_blocks(
-        3,
-        after_ref,
+        0,
+        came_ref,
         own_ref,
         pick_ref,
         weight_ref,
@@ -351,8 +351,8 @@
     )
 
 
-def top_kernel(
-    before_ref,
+def last_edge_kernel(
+    came_ref,
     own_ref,
     pick_ref,
     weight_ref,
@@ -361,7 +361,7 @@
     own_im,
     pair_ref,
     mid_ref,
-    bottom_ref,
+    edge_ref,
     out_ref,
     result,
     sems,
@@ -369,14 +369,14 @@
 ):
     copies = [
         pltpu.make_async_copy(mid_ref, out_ref.at[64:192], sems.at[0]),
-        pltpu.make_async_copy(bottom_ref, out_ref.at[192:256], sems.at[1]),
-        pltpu.make_async_copy(result, out_ref.at[0:64], sems.at[2]),
+        pltpu.make_async_copy(edge_ref, out_ref.at[0:64], sems.at[1]),
+        pltpu.make_async_copy(result, out_ref.at[192:256], sems.at[2]),
     ]
     copies[0].start()
     copies[1].start()
     edge_blocks(
-        0,
-        before_ref,
+        3,
+        came_ref,
         own_ref,
         pick_ref,
         weight_ref,
@@ -444,23 +444,23 @@
     rows = [SENT + 16] * 2 + [WIDE * 16] * 2 + [SIDE * REACH] * 2
     scratch = [pltpu.VMEM((n, FREQ), F32) for n in rows] + GROUP_SCRATCH
     cost = pl.CostEstimate(flops=3_000_000, bytes_accessed=3_000_000, transcendentals=0)
-    bottom = pl.pallas_call(
-        bottom_kernel,
+    top = pl.pallas_call(
+        first_edge_kernel,
         out_shape=float_shape(64),
         in_specs=[VMEM] * 8,
         scratch_shapes=scratch,
         compiler_params=params(),
         cost_estimate=cost,
-    )(after, own, *chosen, *shared)
+    )(before, own, *chosen, *shared)
     return pl.pallas_call(
-        top_kernel,
+        last_edge_kernel,
         out_shape=float_shape(8 * 2 * DIST * 2),
         in_specs=[VMEM] * 10,
         out_specs=pl.BlockSpec(memory_space=pltpu.HBM),
         scratch_shapes=[pltpu.VMEM((64, FREQ), F32), pltpu.SemaphoreType.DMA((3,))] + scratch,
         compiler_params=params(),
         cost_estimate=cost,
-    )(before, own, *chosen, *shared, mid, bottom)
+    )(after, own, *chosen, *shared, mid, top)
 
 
 def on_device(frames, disk_mask, offsets, filter_gain, filter_mix):

time: 42.6 us -> 46.1 us (1.082)
  waiting for transfers between devices: 0.95 us -> 4.49 us
    ppermute x1, waiting for transfers between devices: 0.01 us -> 4.06 us  [outer(): after = lax.ppermute(first, 'band', down)]
    ppermute x1, waiting for transfers between devices: 0.52 us -> 0.01 us  [outer(): before = lax.ppermute(last, 'band', up)]
  transfers between devices with their start and end apart: 3 -> 3, of which waited for: 2 -> 2; matrix products, arithmetic and copies ran while one was open for 0% -> 0% of each run, Pallas kernels for 6% -> 5%
where the time goes in v10:
time: 46.1 us; the launch traced here: 45.9 us
  blocking collectives  26.3 us (57%)
  starting transfers between devices  9.32 us (20%)
  Pallas kernels  5.57 us (12%)
  waiting for transfers between devices  4.49 us (10%)
    all_to_all x1, blocking collectives, on_device(): lax.all_to_all(packed, 'tile', split_axis=0, concat_axis=0, axis_index_gr...  26.3 us
    ppermute x1, starting transfers between devices, outer(): before = lax.ppermute(last, 'band', up)  5.49 us
    ppermute x1, waiting for transfers between devices, outer(): after = lax.ppermute(first, 'band', down)  4.06 us
    ppermute x1, starting transfers between devices, outer(): after = lax.ppermute(first, 'band', down)  1.92 us
    ppermute x1, starting transfers between devices, on_device(): other = lax.ppermute(mine, 'tile', [(i, i ^ 1) for i in range(2 * CHIPS)])  1.91 us
    pallas_call x1, Pallas kernels, pack(): pl.pallas_call(pack_kernel, out_shape=(pltpu.VMEM((CHIPS, 2 * SPAN, 128),...  1.65 us
    pallas_call x1, Pallas kernels, select(): pl.pallas_call(select_kernel, out_shape=(jax.ShapeDtypeStruct((DIST * COL...  1.22 us
    pallas_call x1, Pallas kernels, outer(): pl.pallas_call(last_edge_kernel, out_shape=float_shape(8 * 2 * DIST * 2),...  1.07 us
  transfers between devices with their start and end apart: 3, of which 2 were waited for; matrix products, arithmetic and copies ran while one was open for 0% of the time, Pallas kernels for 5%

profile of v10, /device:TPU:200, one launch (start us, length us, event | category | flops | bytes accessed | tf_op | source)
XLA Modules:
  0.0 45.9 jit_solution(6106266266513580396)
XLA Ops:
  0.0 1.6 %shard_map.64 = (bf16[32,56,128]{2,1,0:T(8,128)(2,1)S(1)}, f32[8,128]{1,0:T(8,128)S(1)}) custom-call(bf16[8,32,512]{2,1,0:T(8,128)(2,1)} %frames_ref.1, s32[32,512]{1,0:T(8,128)} %mask_ref.3, f32[1,128]{1,0:T(1,128)} %bitcast.3, f32[1,128]{1,0:T(1,128)} %bitcast.4), custom_call_target="tpu_custom_call" | custom-call | tf_op jit(solution)/shard_map/pallas_call | solution.py:121
  1.7 0.0 copy-start.2
  1.7 0.0 copy-start
  1.7 0.0 copy-start.1
  1.7 26.3 %all_to_all.5.mine_ref = bf16[32,56,128]{2,1,0:T(8,128)(2,1)S(1)} all-to-all(bf16[32,56,128]{2,1,0:T(8,128)(2,1)S(1)} %get-tuple-element.20), channel_id=1, replica_groups={{0,2,4,6,8,10,12,14,16,18,20,22,24,26,28,30,32,34,36,38,40,42,44,46,48,..., dimensions={0} | all-to-all | bytes 917504 | tf_op jit(solution)/shard_map/all_to_all | solution.py:471
  28.0 1.9 %collective-permute-start = (bf16[32,56,128]{2,1,0:T(8,128)(2,1)S(1)}, bf16[32,56,128]{2,1,0:T(8,128)(2,1)S(1)}, u32[]{:S(2)}, u32[]{:S(2)}) collective-permute-start(bf16[32,56,128]{2,1,0:T(8,128)(2,1)S(1)} %all_to_all.5.mine_ref), channel_id=1, source_target_pairs={{0,1},{1,0},{2,3},{3,2},{4,5},{5,4},{6,7},{7,6},{8,9},{9,8},{10,11... | collective-permute-start | bytes 1376264 | tf_op jit(solution)/shard_map/ppermute | solution.py:474
  29.9 0.0 copy-done.2
  29.9 0.1 add.20.offsets_ref
  30.0 0.0 copy-done
  30.0 1.2 %shard_map.65 = (bf16[512,512]{1,0:T(8,128)(2,1)S(1)}, f32[256,128]{1,0:T(8,128)S(1)}, f32[16,128]{1,0:T(8,128)S(1)}) custom-call(s32[64]{0:T(128)S(1)} %add.20.offsets_ref, s32[32,512]{1,0:T(8,128)S(1)} %copy-done), custom_call_target="tpu_custom_call" | custom-call | flops 4000000 | bytes 4000000 | tf_op jit(solution)/shard_map/pallas_call | solution.py:413
  31.3 0.4 collective-permute-done.other_ref
  31.7 0.0 copy-done.1
  31.7 0.4 shard_map.66
  32.1 5.5 %collective-permute-start.2 = (bf16[96,256]{1,0:T(8,128)(2,1)S(1)}, bf16[96,256]{1,0:T(8,128)(2,1)S(1)}, u32[]{:S(2)}, u32[]{:S(2)}) collective-permute-start(bf16[96,256]{1,0:T(8,128)(2,1)S(1)} %get-tuple-element.34), channel_id=1, source_target_pairs={{0,64},{64,128},{128,192},{192,256},{256,320},{320,384},{384,448},... | collective-permute-start | bytes 147464 | tf_op jit(solution)/shard_map/ppermute | solution.py:442
  37.6 1.9 %collective-permute-start.1 = (bf16[96,256]{1,0:T(8,128)(2,1)S(1)}, bf16[96,256]{1,0:T(8,128)(2,1)S(1)}, u32[]{:S(2)}, u32[]{:S(2)}) collective-permute-start(bf16[96,256]{1,0:T(8,128)(2,1)S(1)} %get-tuple-element.25), channel_id=1, source_target_pairs={{64,0},{128,64},{192,128},{256,192},{320,256},{384,320},{448,384},... | collective-permute-start | bytes 147464 | tf_op jit(solution)/shard_map/ppermute | solution.py:441
  39.6 0.8 %shard_map.67 = (f32[128,128]{1,0:T(8,128)S(1)}, f32[640,128]{1,0:T(8,128)S(1)}, f32[640,128]{1,0:T(8,128)S(1)}) custom-call(bf16[640,256]{1,0:T(8,128)(2,1)S(1)} %get-tuple-element.26.own_ref, f32[8,128]{1,0:T(8,128)S(1)} %get-tuple-element.30.pair_ref, bf16[512,512]{1,0:T(8,128)(2,1)S(1)} %get-tuple-element.27.pick_ref, ...), custom_call_target="tpu_custom_call" | custom-call | flops 6000000 | bytes 4000000 | tf_op jit(solution)/shard_map/pallas_call | solution.py:427
  40.3 0.0 collective-permute-done.2.came_ref
  40.3 0.4 shard_map.68.edge_ref
  40.8 4.1 %collective-permute-done.1.came_ref = bf16[96,256]{1,0:T(8,128)(2,1)S(1)} collective-permute-done((bf16[96,256]{1,0:T(8,128)(2,1)S(1)}, bf16[96,256]{1,0:T(8,128)(2,1)S(1)}, u32[]{:S(2)}, u32[]{:S(2)}) %collective-permute-start.1) | collective-permute-done | bytes 49184 | tf_op jit(solution)/shard_map/ppermute | solution.py:441
  44.8 1.1 %shard_map.69 = f32[256,128]{1,0:T(8,128)} custom-call(bf16[96,256]{1,0:T(8,128)(2,1)S(1)} %collective-permute-done.1.came_ref, bf16[640,256]{1,0:T(8,128)(2,1)S(1)} %get-tuple-element.26.own_ref, bf16[512,512]{1,0:T(8,128)(2,1)S(1)} %get-tuple-element.27.pick_ref, f32[256,128]{1,0:T(8,128)S(1)} %get-tuple-element.28.weight_ref, ...), custom_call_target="tpu_custom_call" | custom-call | flops 3000000 | bytes 3000000 | tf_op jit(solution)/shard_map/pallas_call | solution.py:455
  (1 shorter events, 0.0 us)
Async XLA Ops:
  1.7 28.3 %copy-start.2 = (s32[8,8,2]{1,2,0:T(2,128)S(1)}, s32[8,8,2]{1,2,0:T(2,128)}, u32[]{:S(2)}) copy-start(s32[8,8,2]{1,2,0:T(2,128)} %param.8) | copy-start | bytes 1540
  1.7 28.4 %copy-start = (s32[32,512]{1,0:T(8,128)S(1)}, s32[32,512]{1,0:T(8,128)}, u32[]{:S(2)}) copy-start(s32[32,512]{1,0:T(8,128)} %mask_ref.3) | copy-start | bytes 196612
  1.7 30.0 %copy-start.1 = (bf16[512,256]{1,0:T(8,128)(2,1)S(1)}, bf16[512,256]{1,0:T(8,128)(2,1)}, u32[]{:S(2)}) copy-start(bf16[512,256]{1,0:T(8,128)(2,1)} %constant.8.table_ref) | copy-start | bytes 786436
  28.0 3.7 %collective-permute-start = (bf16[32,56,128]{2,1,0:T(8,128)(2,1)S(1)}, bf16[32,56,128]{2,1,0:T(8,128)(2,1)S(1)}, u32[]{:S(2)}, u32[]{:S(2)}) collective-permute-start(bf16[32,56,128]{2,1,0:T(8,128)(2,1)S(1)} %all_to_all.5.mine_ref), channel_id=1, source_target_pairs={{0,1},{1,0},{2,3},{3,2},{4,5},{5,4},{6,7},{7,6},{8,9},{9,8},{10,11... | collective-permute-start | bytes 1376264 | tf_op jit(solution)/shard_map/ppermute | solution.py:474
  32.1 8.2 %collective-permute-start.2 = (bf16[96,256]{1,0:T(8,128)(2,1)S(1)}, bf16[96,256]{1,0:T(8,128)(2,1)S(1)}, u32[]{:S(2)}, u32[]{:S(2)}) collective-permute-start(bf16[96,256]{1,0:T(8,128)(2,1)S(1)} %get-tuple-element.34), channel_id=1, source_target_pairs={{0,64},{64,128},{128,192},{192,256},{256,320},{320,384},{384,448},... | collective-permute-start | bytes 147464 | tf_op jit(solution)/shard_map/ppermute | solution.py:442
  37.6 7.2 %collective-permute-start.1 = (bf16[96,256]{1,0:T(8,128)(2,1)S(1)}, bf16[96,256]{1,0:T(8,128)(2,1)S(1)}, u32[]{:S(2)}, u32[]{:S(2)}) collective-permute-start(bf16[96,256]{1,0:T(8,128)(2,1)S(1)} %get-tuple-element.25), channel_id=1, source_target_pairs={{64,0},{128,64},{192,128},{256,192},{320,256},{384,320},{448,384},... | collective-permute-start | bytes 147464 | tf_op jit(solution)/shard_map/ppermute | solution.py:441

commit v11 on v9

--- a/solution.py
+++ b/solution.py
@@ -474,7 +474,6 @@
     other = lax.ppermute(mine, "tile", [(i, i ^ 1) for i in range(2 * CHIPS)])
     steps = ((offsets[..., 1] + 4) * 16 + offsets[..., 0] + 4).reshape(DIST * OFFS)
     chosen = select(steps, disk_mask)
-    other, chosen = lax.optimization_barrier((other, chosen))
     own, first, last = spectra(mine, other, dft_table())
     out = outer(own, first, last, pair, chosen, middle(own, pair, chosen))
     return out.reshape(8, 2, DIST, 2, FREQ)

time: 42.6 us -> 46.6 us (1.094)
  waiting for transfers between devices: 0.95 us -> 4.94 us
    ppermute x1, waiting for transfers between devices: 0.01 us -> 3.15 us  [outer(): after = lax.ppermute(first, 'band', down)]
    ppermute x1, waiting for transfers between devices: 0.43 us -> 1.78 us  [on_device(): other = lax.ppermute(mine, 'tile', [(i, i ^ 1) for i in range(2 * CHIPS)])]
    ppermute x1, waiting for transfers between devices: 0.52 us -> 0.01 us  [outer(): before = lax.ppermute(last, 'band', up)]
  transfers between devices with their start and end apart: 3 -> 3, of which waited for: 2 -> 2; matrix products, arithmetic and copies ran while one was open for 0% -> 0% of each run, Pallas kernels for 6% -> 5%
where the time goes in v11:
time: 46.6 us; the launch traced here: 46.3 us
  blocking collectives  26.3 us (56%)
  starting transfers between devices  9.32 us (20%)
  Pallas kernels  5.57 us (12%)
  waiting for transfers between devices  4.94 us (11%)
    all_to_all x1, blocking collectives, on_device(): lax.all_to_all(packed, 'tile', split_axis=0, concat_axis=0, axis_index_gr...  26.3 us
    ppermute x1, starting transfers between devices, outer(): before = lax.ppermute(last, 'band', up)  5.49 us
    ppermute x1, waiting for transfers between devices, outer(): after = lax.ppermute(first, 'band', down)  3.15 us
    ppermute x1, starting transfers between devices, outer(): after = lax.ppermute(first, 'band', down)  1.92 us
    ppermute x1, starting transfers between devices, on_device(): other = lax.ppermute(mine, 'tile', [(i, i ^ 1) for i in range(2 * CHIPS)])  1.91 us
    ppermute x1, waiting for transfers between devices, on_device(): other = lax.ppermute(mine, 'tile', [(i, i ^ 1) for i in range(2 * CHIPS)])  1.78 us
    pallas_call x1, Pallas kernels, pack(): pl.pallas_call(pack_kernel, out_shape=(pltpu.VMEM((CHIPS, 2 * SPAN, 128),...  1.65 us
    pallas_call x1, Pallas kernels, select(): pl.pallas_call(select_kernel, out_shape=(jax.ShapeDtypeStruct((DIST * COL...  1.22 us
  transfers between devices with their start and end apart: 3, of which 2 were waited for; matrix products, arithmetic and copies ran while one was open for 0% of the time, Pallas kernels for 5%

profile of v11, /device:TPU:200, one launch (start us, length us, event | category | flops | bytes accessed | tf_op | source)
XLA Modules:
  0.0 46.3 jit_solution(3494761153270355386)
XLA Ops:
  0.0 1.6 %shard_map.64 = (bf16[32,56,128]{2,1,0:T(8,128)(2,1)S(1)}, f32[8,128]{1,0:T(8,128)S(1)}) custom-call(bf16[8,32,512]{2,1,0:T(8,128)(2,1)} %frames_ref.1, s32[32,512]{1,0:T(8,128)} %mask_ref.3, f32[1,128]{1,0:T(1,128)} %bitcast.3, f32[1,128]{1,0:T(1,128)} %bitcast.4), custom_call_target="tpu_custom_call" | custom-call | tf_op jit(solution)/shard_map/pallas_call | solution.py:121
  1.7 0.0 copy-start.1
  1.7 26.3 %all_to_all.5.mine_ref = bf16[32,56,128]{2,1,0:T(8,128)(2,1)S(1)} all-to-all(bf16[32,56,128]{2,1,0:T(8,128)(2,1)S(1)} %get-tuple-element.16), channel_id=1, replica_groups={{0,2,4,6,8,10,12,14,16,18,20,22,24,26,28,30,32,34,36,38,40,42,44,46,48,..., dimensions={0} | all-to-all | bytes 917504 | tf_op jit(solution)/shard_map/all_to_all | solution.py:471
  28.0 1.9 %collective-permute-start = (bf16[32,56,128]{2,1,0:T(8,128)(2,1)S(1)}, bf16[32,56,128]{2,1,0:T(8,128)(2,1)S(1)}, u32[]{:S(2)}, u32[]{:S(2)}) collective-permute-start(bf16[32,56,128]{2,1,0:T(8,128)(2,1)S(1)} %all_to_all.5.mine_ref), channel_id=1, source_target_pairs={{0,1},{1,0},{2,3},{3,2},{4,5},{5,4},{6,7},{7,6},{8,9},{9,8},{10,11... | collective-permute-start | bytes 1376264 | tf_op jit(solution)/shard_map/ppermute | solution.py:474
  29.9 1.8 %collective-permute-done.other_ref = bf16[32,56,128]{2,1,0:T(8,128)(2,1)S(1)} collective-permute-done((bf16[32,56,128]{2,1,0:T(8,128)(2,1)S(1)}, bf16[32,56,128]{2,1,0:T(8,128)(2,1)S(1)}, u32[]{:S(2)}, u32[]{:S(2)}) %collective-permute-start) | collective-permute-done | bytes 458784 | tf_op jit(solution)/shard_map/ppermute | solution.py:474
  31.7 0.0 copy-done.1
  31.7 0.0 copy-start.2
  31.7 0.0 copy-start
  31.7 0.4 shard_map.65
  32.1 5.5 %collective-permute-start.1 = (bf16[96,256]{1,0:T(8,128)(2,1)S(1)}, bf16[96,256]{1,0:T(8,128)(2,1)S(1)}, u32[]{:S(2)}, u32[]{:S(2)}) collective-permute-start(bf16[96,256]{1,0:T(8,128)(2,1)S(1)} %get-tuple-element.17), channel_id=1, source_target_pairs={{0,64},{64,128},{128,192},{192,256},{256,320},{320,384},{384,448},... | collective-permute-start | bytes 147464 | tf_op jit(solution)/shard_map/ppermute | solution.py:442
  37.6 1.9 %collective-permute-start.2 = (bf16[96,256]{1,0:T(8,128)(2,1)S(1)}, bf16[96,256]{1,0:T(8,128)(2,1)S(1)}, u32[]{:S(2)}, u32[]{:S(2)}) collective-permute-start(bf16[96,256]{1,0:T(8,128)(2,1)S(1)} %get-tuple-element.26), channel_id=1, source_target_pairs={{64,0},{128,64},{192,128},{256,192},{320,256},{384,320},{448,384},... | collective-permute-start | bytes 147464 | tf_op jit(solution)/shard_map/ppermute | solution.py:441
  39.5 0.0 copy-done.2
  39.6 0.1 add.20.offsets_ref
  39.7 0.0 copy-done
  39.7 1.2 %shard_map.66 = (bf16[512,512]{1,0:T(8,128)(2,1)S(1)}, f32[256,128]{1,0:T(8,128)S(1)}, f32[16,128]{1,0:T(8,128)S(1)}) custom-call(s32[64]{0:T(128)S(1)} %add.20.offsets_ref, s32[32,512]{1,0:T(8,128)S(1)} %copy-done), custom_call_target="tpu_custom_call" | custom-call | flops 4000000 | bytes 4000000 | tf_op jit(solution)/shard_map/pallas_call | solution.py:413
  40.9 0.8 %shard_map.67 = (f32[128,128]{1,0:T(8,128)S(1)}, f32[640,128]{1,0:T(8,128)S(1)}, f32[640,128]{1,0:T(8,128)S(1)}) custom-call(bf16[640,256]{1,0:T(8,128)(2,1)S(1)} %get-tuple-element.18.own_ref, f32[8,128]{1,0:T(8,128)S(1)} %get-tuple-element.22.pair_ref, bf16[512,512]{1,0:T(8,128)(2,1)S(1)} %get-tuple-element.19.pick_ref, ...), custom_call_target="tpu_custom_call" | custom-call | flops 6000000 | bytes 4000000 | tf_op jit(solution)/shard_map/pallas_call | solution.py:427
  41.6 3.2 %collective-permute-done.2.after_ref = bf16[96,256]{1,0:T(8,128)(2,1)S(1)} collective-permute-done((bf16[96,256]{1,0:T(8,128)(2,1)S(1)}, bf16[96,256]{1,0:T(8,128)(2,1)S(1)}, u32[]{:S(2)}, u32[]{:S(2)}) %collective-permute-start.2) | collective-permute-done | bytes 49184 | tf_op jit(solution)/shard_map/ppermute | solution.py:441
  44.8 0.4 shard_map.68.bottom_ref
  45.2 0.0 collective-permute-done.1.before_ref
  45.2 1.1 %shard_map.69 = f32[256,128]{1,0:T(8,128)} custom-call(bf16[96,256]{1,0:T(8,128)(2,1)S(1)} %collective-permute-done.1.before_ref, bf16[640,256]{1,0:T(8,128)(2,1)S(1)} %get-tuple-element.18.own_ref, bf16[512,512]{1,0:T(8,128)(2,1)S(1)} %get-tuple-element.19.pick_ref, f32[256,128]{1,0:T(8,128)S(1)} %get-tuple-element.20.weight_ref, ...), custom_call_target="tpu_custom_call" | custom-call | flops 3000000 | bytes 3000000 | tf_op jit(solution)/shard_map/pallas_call | solution.py:455
  (1 shorter events, 0.0 us)
Async XLA Ops:
  1.7 30.0 %copy-start.1 = (bf16[512,256]{1,0:T(8,128)(2,1)S(1)}, bf16[512,256]{1,0:T(8,128)(2,1)}, u32[]{:S(2)}) copy-start(bf16[512,256]{1,0:T(8,128)(2,1)} %constant.8.table_ref) | copy-start | bytes 786436
  28.0 3.7 %collective-permute-start = (bf16[32,56,128]{2,1,0:T(8,128)(2,1)S(1)}, bf16[32,56,128]{2,1,0:T(8,128)(2,1)S(1)}, u32[]{:S(2)}, u32[]{:S(2)}) collective-permute-start(bf16[32,56,128]{2,1,0:T(8,128)(2,1)S(1)} %all_to_all.5.mine_ref), channel_id=1, source_target_pairs={{0,1},{1,0},{2,3},{3,2},{4,5},{5,4},{6,7},{7,6},{8,9},{9,8},{10,11... | collective-permute-start | bytes 1376264 | tf_op jit(solution)/shard_map/ppermute | solution.py:474
  31.7 7.9 %copy-start.2 = (s32[8,8,2]{1,2,0:T(2,128)S(1)}, s32[8,8,2]{1,2,0:T(2,128)}, u32[]{:S(2)}) copy-start(s32[8,8,2]{1,2,0:T(2,128)} %param.8) | copy-start | bytes 1540
  31.7 8.0 %copy-start = (s32[32,512]{1,0:T(8,128)S(1)}, s32[32,512]{1,0:T(8,128)}, u32[]{:S(2)}) copy-start(s32[32,512]{1,0:T(8,128)} %mask_ref.3) | copy-start | bytes 196612
  32.1 13.1 %collective-permute-start.1 = (bf16[96,256]{1,0:T(8,128)(2,1)S(1)}, bf16[96,256]{1,0:T(8,128)(2,1)S(1)}, u32[]{:S(2)}, u32[]{:S(2)}) collective-permute-start(bf16[96,256]{1,0:T(8,128)(2,1)S(1)} %get-tuple-element.17), channel_id=1, source_target_pairs={{0,64},{64,128},{128,192},{192,256},{256,320},{320,384},{384,448},... | collective-permute-start | bytes 147464 | tf_op jit(solution)/shard_map/ppermute | solution.py:442
  37.6 7.2 %collective-permute-start.2 = (bf16[96,256]{1,0:T(8,128)(2,1)S(1)}, bf16[96,256]{1,0:T(8,128)(2,1)S(1)}, u32[]{:S(2)}, u32[]{:S(2)}) collective-permute-start(bf16[96,256]{1,0:T(8,128)(2,1)S(1)} %get-tuple-element.26), channel_id=1, source_target_pairs={{64,0},{128,64},{192,128},{256,192},{320,256},{384,320},{448,384},... | collective-permute-start | bytes 147464 | tf_op jit(solution)/shard_map/ppermute | solution.py:441
